TPU v7x, 32 devices: a whole 2x2x4 slice. The times are simulated.
32 devices in a mesh: row: 4 (over y, core), col: 8 (over z, x).
Axes of the slice: x: 2, y: 2, z: 4, core: 2. Of those that a mesh axis runs over, the one named last changes fastest.
Arguments:
- left_blocks: bfloat16 [4, 8, 2, 8, 64, 64], P('row', 'col'), may hold values from -0.375 to 0.375
- left_cols: int32 [4, 8, 2, 8], P('row', 'col'), may hold values from 0 to 15, all different within a row
- right_blocks: bfloat16 [4, 8, 16, 6, 64, 64], P('row', 'col'), may hold values from -6 to 6
- right_cols: int32 [4, 8, 16, 6], P('row', 'col'), may hold values from 0 to 15, all different within a row
- out_cols: int32 [4, 8, 2, 8], P('row', 'col'), may hold values from 0 to 15, all different within a row
Outputs:
- product: float32 [4, 8, 2, 8, 64, 64], P('row', 'col')
Inputs may be any that keep to these rules, and one draw needn't show every extreme that they name: `left_cols`: the entries of one block row are distinct. `right_cols`: the entries of one block row are distinct. `out_cols`: the entries of one block row are distinct.
All inputs are finite; a program needn't handle non-finite values.
Results may differ from a plain program's by a relative error of at most 0.0003.
Values may be sent and summed in bfloat16 or wider, within the bound.
No kernel may reach another device: no remote copies, remote signals or barrier semaphores. Data moves between devices by JAX's collectives and lax.ppermute only.
A program may use at most 64 MiB of HBM per device.

v0:
```python
import jax
import jax.numpy as jnp
from jax import lax
from jax.sharding import PartitionSpec as P

TICKS = 8


def shifted(value, axis, steps):
    count = lax.axis_size(axis)
    pairs = [(source, (source + steps) % count) for source in range(count)]
    return lax.ppermute(value, axis, pairs)


def one_tick(left, left_cols, right, right_cols, pattern):
    inner = right.shape[0]
    pick_row = (left_cols[:, :, None] == jnp.arange(inner, dtype=jnp.int32)[None, None, :]).astype(
        jnp.float32
    )
    match = (right_cols[None, None, :, :] == pattern[:, :, None, None]).astype(jnp.float32)
    select = jnp.einsum("iak,iokb->iaokb", pick_row, match).astype(jnp.bfloat16)
    chosen = jnp.einsum(
        "iaokb,kbyz->iaoyz", select, right, preferred_element_type=jnp.float32
    ).astype(jnp.bfloat16)
    return jnp.einsum("iaxy,iaoyz->ioxz", left, chosen, preferred_element_type=jnp.float32)


def on_device(left_blocks, left_cols, right_blocks, right_cols, out_cols):
    left = left_blocks[0, 0]
    left_index = left_cols[0, 0]
    right = right_blocks[0, 0]
    right_index = right_cols[0, 0]
    pattern = out_cols[0, 0]
    total = jnp.zeros((left.shape[0], pattern.shape[1], left.shape[2], left.shape[3]), jnp.float32)
    carried = shifted(pattern, "col", 1 - TICKS)
    for step in range(TICKS):
        total = total + one_tick(left, left_index, right, right_index, carried)
        if step + 1 < TICKS:
            total, carried = shifted((total, carried), "col", 1)
            left, left_index = shifted((left, left_index), "row", 1)
    return total[None, None]


def solution(mesh):
    in_specs = (
        P("row", "col", None, None, None, None),
        P("row", "col", None, None),
        P("row", "col", None, None, None, None),
        P("row", "col", None, None),
        P("row", "col", None, None),
    )
    out_specs = P("row", "col", None, None, None, None)
    return jax.shard_map(
        on_device, mesh=mesh, in_specs=in_specs, out_specs=out_specs, check_vma=False
    )
```

profile of v0, /device:TPU:0, one launch (start us, length us, event | category | flops | bytes accessed | tf_op | source)
XLA Modules:
  0.0 181.0 jit_solution(5090130229811249899)
XLA Ops:
  0.0 2.9 %collective-permute-start = (s32[2,8]{1,0:T(2,128)}, s32[2,8]{1,0:T(2,128)S(1)}, u32[]{:S(2)}, u32[]{:S(2)}) collective-permute-start(s32[2,8]{1,0:T(2,128)} %bitcast.246), channel_id=1, source_target_pairs={{0,1},{1,2},{2,3},{3,4},{4,5},{5,6},{6,7},{7,0},{8,9},{9,10},{10,1... | collective-permute-start | bytes 200 | tf_op jit(solution)/shard_map/ppermute | solution.py:12
  2.9 1.6 collective-permute-start.4
  6.0 1.7 collective-permute-done
  8.4 5.6 %collective-permute-done.2 = s32[2,8]{1,0:T(2,128)S(1)} collective-permute-done((s32[2,8]{1,0:T(2,128)S(1)}, s32[2,8]{1,0:T(2,128)S(1)}, u32[]{:S(2)}, u32[]{:S(2)}) %collective-permute-start.2) | collective-permute-done | bytes 96 | tf_op jit(solution)/shard_map/ppermute | solution.py:12
  14.6 5.6 %collective-permute-done.6 = s32[2,8]{1,0:T(2,128)S(1)} collective-permute-done((s32[2,8]{1,0:T(2,128)S(1)}, s32[2,8]{1,0:T(2,128)S(1)}, u32[]{:S(2)}, u32[]{:S(2)}) %collective-permute-start.6) | collective-permute-done | bytes 96 | tf_op jit(solution)/shard_map/ppermute | solution.py:12
  20.9 5.7 %collective-permute-done.10 = s32[2,8]{1,0:T(2,128)S(1)} collective-permute-done((s32[2,8]{1,0:T(2,128)S(1)}, s32[2,8]{1,0:T(2,128)S(1)}, u32[]{:S(2)}, u32[]{:S(2)}) %collective-permute-start.10) | collective-permute-done | bytes 96 | tf_op jit(solution)/shard_map/ppermute | solution.py:12
  27.1 5.7 %collective-permute-done.14 = s32[2,8]{1,0:T(2,128)S(1)} collective-permute-done((s32[2,8]{1,0:T(2,128)S(1)}, s32[2,8]{1,0:T(2,128)S(1)}, u32[]{:S(2)}, u32[]{:S(2)}) %collective-permute-start.14) | collective-permute-done | bytes 96 | tf_op jit(solution)/shard_map/ppermute | solution.py:12
  33.4 5.7 %collective-permute-done.18 = s32[2,8]{1,0:T(2,128)S(1)} collective-permute-done((s32[2,8]{1,0:T(2,128)S(1)}, s32[2,8]{1,0:T(2,128)S(1)}, u32[]{:S(2)}, u32[]{:S(2)}) %collective-permute-start.18) | collective-permute-done | bytes 96 | tf_op jit(solution)/shard_map/ppermute | solution.py:12
  39.7 5.6 %collective-permute-done.22 = s32[2,8]{1,0:T(2,128)S(1)} collective-permute-done((s32[2,8]{1,0:T(2,128)S(1)}, s32[2,8]{1,0:T(2,128)S(1)}, u32[]{:S(2)}, u32[]{:S(2)}) %collective-permute-start.22) | collective-permute-done | bytes 96 | tf_op jit(solution)/shard_map/ppermute | solution.py:12
  45.3 6.3 %collective-permute-done.26 = s32[2,8]{1,0:T(2,128)S(1)} collective-permute-done((s32[2,8]{1,0:T(2,128)S(1)}, s32[2,8]{1,0:T(2,128)S(1)}, u32[]{:S(2)}, u32[]{:S(2)}) %collective-permute-start.26) | collective-permute-done | bytes 96 | tf_op jit(solution)/shard_map/ppermute | solution.py:12
  53.5 2.7 %fusion.46 = bf16[2,8,8,64,64,1]{4,2,5,3,1,0:T(8,128)(2,1)} fusion(bf16[2,8,8,16,6,1]{3,2,4,5,1,0:T(8,128)(2,1)S(1)} %copy.16, bf16[16,6,64,64,1,1]{3,2,1,0,4,5:T(8,128)(2,1)S(1)} %bitcast.234), kind=kOutput, calls=%fused_computation.62 | convolution fusion | flops 100663296 | bytes 1859584 | tf_op jit(solution)/shard_map/iaokb,kbyz->iaoyz/dot_general | solution.py:22
  56.3 4.2 %copy.18 = bf16[2,8,8,64,64,1]{3,4,1,2,0,5:T(8,128)(2,1)} copy(bf16[2,8,8,64,64,1]{4,2,5,3,1,0:T(8,128)(2,1)} %fusion.46) | data formatting | bytes 2097152 | tf_op jit(solution)/shard_map/iaokb,kbyz->iaoyz/dot_general | solution.py:22
  60.5 2.3 %fusion.15 = f32[2,8,64,64]{2,3,1,0:T(8,128)S(1)} fusion(bf16[2,8,8,64,64,1]{3,4,1,2,0,5:T(8,128)(2,1)} %copy.18, bf16[1,1,2,8,64,64]{5,4,3,2,1,0:T(8,128)(2,1)S(1)} %copy-done.5), kind=kOutput, calls=%fused_computation.23 | convolution fusion | flops 67108864 | bytes 1441792 | tf_op jit(solution)/shard_map/iaxy,iaoyz->ioxz/dot_general | solution.py:25
  63.3 1.3 copy.21
  64.5 3.6 %fusion.44 = bf16[2,8,8,64,64,1]{4,2,5,3,1,0:T(8,128)(2,1)} fusion(bf16[2,8,8,16,6,1]{3,2,4,5,1,0:T(8,128)(2,1)} %copy.21, bf16[16,6,64,64,1,1]{3,2,1,0,4,5:T(8,128)(2,1)S(1)} %bitcast.241), kind=kOutput, calls=%fused_computation.60 | convolution fusion | flops 100663296 | bytes 1859584 | tf_op jit(solution)/shard_map/iaokb,kbyz->iaoyz/dot_general | solution.py:22
  68.2 4.2 %copy.22 = bf16[2,8,8,64,64,1]{3,4,1,2,0,5:T(8,128)(2,1)} copy(bf16[2,8,8,64,64,1]{4,2,5,3,1,0:T(8,128)(2,1)} %fusion.44) | data formatting | bytes 2097152 | tf_op jit(solution)/shard_map/iaokb,kbyz->iaoyz/dot_general | solution.py:22
  73.4 1.3 copy.25
  74.7 2.3 %fusion.16 = f32[2,8,64,64]{2,3,1,0:T(8,128)S(1)} fusion(f32[2,8,64,64]{2,3,1,0:T(8,128)S(1)} %collective-permute-done.1, bf16[2,8,8,64,64,1]{3,4,1,2,0,5:T(8,128)(2,1)} %copy.22, bf16[2,8,64,64]{3,2,1,0:T(8,128)(2,1)} %collective-permute-done.4), kind=kOutput, calls=%fused_computation.24 | convolution fusion | flops 67174400 | bytes 1703936 | tf_op jit(solution)/shard_map/iaxy,iaoyz->ioxz/dot_general | solution.py:25
  77.1 2.7 %fusion.42 = bf16[2,8,8,64,64,1]{4,2,5,3,1,0:T(8,128)(2,1)} fusion(bf16[2,8,8,16,6,1]{3,2,4,5,1,0:T(8,128)(2,1)S(1)} %copy-done.11, bf16[16,6,64,64,1,1]{3,2,1,0,4,5:T(8,128)(2,1)S(1)} %bitcast.240), kind=kOutput, calls=%fused_computation.58 | convolution fusion | flops 100663296 | bytes 1859584 | tf_op jit(solution)/shard_map/iaokb,kbyz->iaoyz/dot_general | solution.py:22
  79.8 4.2 %copy.26 = bf16[2,8,8,64,64,1]{3,4,1,2,0,5:T(8,128)(2,1)} copy(bf16[2,8,8,64,64,1]{4,2,5,3,1,0:T(8,128)(2,1)} %fusion.42) | data formatting | bytes 2097152 | tf_op jit(solution)/shard_map/iaokb,kbyz->iaoyz/dot_general | solution.py:22
  85.3 1.3 copy.29
  86.6 3.8 %collective-permute-done.8 = bf16[2,8,64,64]{3,2,1,0:T(8,128)(2,1)} collective-permute-done((bf16[2,8,64,64]{3,2,1,0:T(8,128)(2,1)}, bf16[2,8,64,64]{3,2,1,0:T(8,128)(2,1)}, u32[]{:S(2)}, u32[]{:S(2)}) %collective-permute-start.8) | collective-permute-done | bytes 131104 | tf_op jit(solution)/shard_map/ppermute | solution.py:12
  90.4 2.3 %fusion.17 = f32[2,8,64,64]{2,3,1,0:T(8,128)S(1)} fusion(f32[2,8,64,64]{2,3,1,0:T(8,128)S(1)} %collective-permute-done.5, bf16[2,8,8,64,64,1]{3,4,1,2,0,5:T(8,128)(2,1)} %copy.26, bf16[2,8,64,64]{3,2,1,0:T(8,128)(2,1)} %collective-permute-done.8), kind=kOutput, calls=%fused_computation.25 | convolution fusion | flops 67174400 | bytes 1703936 | tf_op jit(solution)/shard_map/iaxy,iaoyz->ioxz/dot_general | solution.py:25
  92.7 2.7 %fusion.40 = bf16[2,8,8,64,64,1]{4,2,5,3,1,0:T(8,128)(2,1)} fusion(bf16[2,8,8,16,6,1]{3,2,4,5,1,0:T(8,128)(2,1)S(1)} %copy-done.7, bf16[16,6,64,64,1,1]{3,2,1,0,4,5:T(8,128)(2,1)S(1)} %bitcast.239), kind=kOutput, calls=%fused_computation.56 | convolution fusion | flops 100663296 | bytes 1859584 | tf_op jit(solution)/shard_map/iaokb,kbyz->iaoyz/dot_general | solution.py:22
  95.5 4.2 %copy.30 = bf16[2,8,8,64,64,1]{3,4,1,2,0,5:T(8,128)(2,1)} copy(bf16[2,8,8,64,64,1]{4,2,5,3,1,0:T(8,128)(2,1)} %fusion.40) | data formatting | bytes 2097152 | tf_op jit(solution)/shard_map/iaokb,kbyz->iaoyz/dot_general | solution.py:22
  100.8 1.3 copy.33
  102.1 3.8 %collective-permute-done.12 = bf16[2,8,64,64]{3,2,1,0:T(8,128)(2,1)} collective-permute-done((bf16[2,8,64,64]{3,2,1,0:T(8,128)(2,1)}, bf16[2,8,64,64]{3,2,1,0:T(8,128)(2,1)}, u32[]{:S(2)}, u32[]{:S(2)}) %collective-permute-start.12) | collective-permute-done | bytes 131104 | tf_op jit(solution)/shard_map/ppermute | solution.py:12
  105.8 3.0 %collective-permute-done.9 = f32[2,8,64,64]{2,3,1,0:T(8,128)S(1)} collective-permute-done((f32[2,8,64,64]{2,3,1,0:T(8,128)S(1)}, f32[2,8,64,64]{2,3,1,0:T(8,128)S(1)}, u32[]{:S(2)}, u32[]{:S(2)}) %collective-permute-start.9) | collective-permute-done | bytes 262176 | tf_op jit(solution)/shard_map/ppermute | solution.py:12
  108.9 2.3 %fusion.18 = f32[2,8,64,64]{2,3,1,0:T(8,128)S(1)} fusion(f32[2,8,64,64]{2,3,1,0:T(8,128)S(1)} %collective-permute-done.9, bf16[2,8,8,64,64,1]{3,4,1,2,0,5:T(8,128)(2,1)} %copy.30, bf16[2,8,64,64]{3,2,1,0:T(8,128)(2,1)} %collective-permute-done.12), kind=kOutput, calls=%fused_computation.26 | convolution fusion | flops 67174400 | bytes 1703936 | tf_op jit(solution)/shard_map/iaxy,iaoyz->ioxz/dot_general | solution.py:25
  111.2 2.7 %fusion.38 = bf16[2,8,8,64,64,1]{4,2,5,3,1,0:T(8,128)(2,1)} fusion(bf16[2,8,8,16,6,1]{3,2,4,5,1,0:T(8,128)(2,1)S(1)} %copy-done.8, bf16[16,6,64,64,1,1]{3,2,1,0,4,5:T(8,128)(2,1)S(1)} %bitcast.238), kind=kOutput, calls=%fused_computation.54 | convolution fusion | flops 100663296 | bytes 1859584 | tf_op jit(solution)/shard_map/iaokb,kbyz->iaoyz/dot_general | solution.py:22
  113.9 4.1 %copy.34 = bf16[2,8,8,64,64,1]{3,4,1,2,0,5:T(8,128)(2,1)} copy(bf16[2,8,8,64,64,1]{4,2,5,3,1,0:T(8,128)(2,1)} %fusion.38) | data formatting | bytes 2097152 | tf_op jit(solution)/shard_map/iaokb,kbyz->iaoyz/dot_general | solution.py:22
  119.2 1.3 copy.37
  120.5 3.8 %collective-permute-done.16 = bf16[2,8,64,64]{3,2,1,0:T(8,128)(2,1)} collective-permute-done((bf16[2,8,64,64]{3,2,1,0:T(8,128)(2,1)}, bf16[2,8,64,64]{3,2,1,0:T(8,128)(2,1)}, u32[]{:S(2)}, u32[]{:S(2)}) %collective-permute-start.16) | collective-permute-done | bytes 131104 | tf_op jit(solution)/shard_map/ppermute | solution.py:12
  124.3 2.2 %collective-permute-done.13 = f32[2,8,64,64]{2,3,1,0:T(8,128)S(1)} collective-permute-done((f32[2,8,64,64]{2,3,1,0:T(8,128)S(1)}, f32[2,8,64,64]{2,3,1,0:T(8,128)S(1)}, u32[]{:S(2)}, u32[]{:S(2)}) %collective-permute-start.13) | collective-permute-done | bytes 262176 | tf_op jit(solution)/shard_map/ppermute | solution.py:12
  126.4 2.3 %fusion.19 = f32[2,8,64,64]{2,3,1,0:T(8,128)S(1)} fusion(f32[2,8,64,64]{2,3,1,0:T(8,128)S(1)} %collective-permute-done.13, bf16[2,8,8,64,64,1]{3,4,1,2,0,5:T(8,128)(2,1)} %copy.34, bf16[2,8,64,64]{3,2,1,0:T(8,128)(2,1)} %collective-permute-done.16), kind=kOutput, calls=%fused_computation.27 | convolution fusion | flops 67174400 | bytes 1703936 | tf_op jit(solution)/shard_map/iaxy,iaoyz->ioxz/dot_general | solution.py:25
  128.8 2.7 %fusion.36 = bf16[2,8,8,64,64,1]{4,2,5,3,1,0:T(8,128)(2,1)} fusion(bf16[2,8,8,16,6,1]{3,2,4,5,1,0:T(8,128)(2,1)S(1)} %copy-done.9, bf16[16,6,64,64,1,1]{3,2,1,0,4,5:T(8,128)(2,1)S(1)} %bitcast.237), kind=kOutput, calls=%fused_computation.52 | convolution fusion | flops 100663296 | bytes 1859584 | tf_op jit(solution)/shard_map/iaokb,kbyz->iaoyz/dot_general | solution.py:22
  131.5 4.1 %copy.38 = bf16[2,8,8,64,64,1]{3,4,1,2,0,5:T(8,128)(2,1)} copy(bf16[2,8,8,64,64,1]{4,2,5,3,1,0:T(8,128)(2,1)} %fusion.36) | data formatting | bytes 2097152 | tf_op jit(solution)/shard_map/iaokb,kbyz->iaoyz/dot_general | solution.py:22
  138.1 3.7 %collective-permute-done.20 = bf16[2,8,64,64]{3,2,1,0:T(8,128)(2,1)S(1)} collective-permute-done((bf16[2,8,64,64]{3,2,1,0:T(8,128)(2,1)}, bf16[2,8,64,64]{3,2,1,0:T(8,128)(2,1)S(1)}, u32[]{:S(2)}, u32[]{:S(2)}) %collective-permute-start.20) | collective-permute-done | bytes 131104 | tf_op jit(solution)/shard_map/ppermute | solution.py:12
  141.7 1.3 collective-permute-done.17
  143.1 2.3 %fusion.20 = f32[2,8,64,64]{2,3,1,0:T(8,128)S(1)} fusion(f32[2,8,64,64]{2,3,1,0:T(8,128)S(1)} %collective-permute-done.17, bf16[2,8,8,64,64,1]{3,4,1,2,0,5:T(8,128)(2,1)} %copy.38, bf16[2,8,64,64]{3,2,1,0:T(8,128)(2,1)S(1)} %collective-permute-done.20), kind=kOutput, calls=%fused_computation.28 | convolution fusion | flops 67174400 | bytes 1703936 | tf_op jit(solution)/shard_map/iaxy,iaoyz->ioxz/dot_general | solution.py:25
  145.7 2.7 %fusion.34 = bf16[2,8,8,64,64,1]{4,2,5,3,1,0:T(8,128)(2,1)} fusion(bf16[2,8,8,16,6,1]{3,2,4,5,1,0:T(8,128)(2,1)S(1)} %copy-done.10, bf16[16,6,64,64,1,1]{3,2,1,0,4,5:T(8,128)(2,1)S(1)} %bitcast.236), kind=kOutput, calls=%fused_computation.50 | convolution fusion | flops 100663296 | bytes 1859584 | tf_op jit(solution)/shard_map/iaokb,kbyz->iaoyz/dot_general | solution.py:22
  148.4 4.1 %copy.42 = bf16[2,8,8,64,64,1]{3,4,1,2,0,5:T(8,128)(2,1)} copy(bf16[2,8,8,64,64,1]{4,2,5,3,1,0:T(8,128)(2,1)} %fusion.34) | data formatting | bytes 2097152 | tf_op jit(solution)/shard_map/iaokb,kbyz->iaoyz/dot_general | solution.py:22
  154.2 4.3 %collective-permute-done.24 = bf16[2,8,64,64]{3,2,1,0:T(8,128)(2,1)} collective-permute-done((bf16[2,8,64,64]{3,2,1,0:T(8,128)(2,1)S(1)}, bf16[2,8,64,64]{3,2,1,0:T(8,128)(2,1)}, u32[]{:S(2)}, u32[]{:S(2)}) %collective-permute-start.24) | collective-permute-done | bytes 131104 | tf_op jit(solution)/shard_map/ppermute | solution.py:12
  159.0 2.3 %fusion.21 = f32[2,8,64,64]{2,3,1,0:T(8,128)S(1)} fusion(f32[2,8,64,64]{2,3,1,0:T(8,128)S(1)} %collective-permute-done.21, bf16[2,8,8,64,64,1]{3,4,1,2,0,5:T(8,128)(2,1)} %copy.42, bf16[2,8,64,64]{3,2,1,0:T(8,128)(2,1)} %collective-permute-done.24), kind=kOutput, calls=%fused_computation.29 | convolution fusion | flops 67174400 | bytes 1703936 | tf_op jit(solution)/shard_map/iaxy,iaoyz->ioxz/dot_general | solution.py:25
  161.4 2.7 %fusion.32 = bf16[2,8,8,64,64,1]{4,2,5,3,1,0:T(8,128)(2,1)} fusion(bf16[2,8,8,16,6,1]{3,2,4,5,1,0:T(8,128)(2,1)S(1)} %copy-done.6, bf16[16,6,64,64,1,1]{3,2,1,0,4,5:T(8,128)(2,1)S(1)} %bitcast.235), kind=kOutput, calls=%fused_computation.48 | convolution fusion | flops 100663296 | bytes 1859584 | tf_op jit(solution)/shard_map/iaokb,kbyz->iaoyz/dot_general | solution.py:22
  164.1 4.1 %copy.46 = bf16[2,8,8,64,64,1]{3,4,1,2,0,5:T(8,128)(2,1)} copy(bf16[2,8,8,64,64,1]{4,2,5,3,1,0:T(8,128)(2,1)} %fusion.32) | data formatting | bytes 2097152 | tf_op jit(solution)/shard_map/iaokb,kbyz->iaoyz/dot_general | solution.py:22
  168.2 9.5 %collective-permute-done.25 = f32[2,8,64,64]{2,3,1,0:T(8,128)S(1)} collective-permute-done((f32[2,8,64,64]{2,3,1,0:T(8,128)S(1)}, f32[2,8,64,64]{2,3,1,0:T(8,128)S(1)}, u32[]{:S(2)}, u32[]{:S(2)}) %collective-permute-start.25) | collective-permute-done | bytes 262176 | tf_op jit(solution)/shard_map/ppermute | solution.py:12
  177.7 2.3 %fusion.23 = f32[1,1,2,8,64,64]{4,5,3,2,1,0:T(8,128)S(1)} fusion(f32[2,8,64,64]{2,3,1,0:T(8,128)S(1)} %collective-permute-done.25, bf16[2,8,8,64,64,1]{3,4,1,2,0,5:T(8,128)(2,1)} %copy.46, bf16[2,8,64,64]{3,2,1,0:T(8,128)(2,1)S(1)} %collective-permute-done.28), kind=kOutput, calls=%fused_computation.31 | convolution fusion | flops 67174400 | bytes 1703936 | tf_op jit(solution)/shard_map/iaxy,iaoyz->ioxz/dot_general | solution.py:25
  (95 shorter events, 18.5 us)
Async XLA Ops:
  0.0 53.5 %copy-start = (bf16[1,1,16,6,64,64]{5,4,3,2,1,0:T(8,128)(2,1)S(1)}, bf16[1,1,16,6,64,64]{5,4,3,2,1,0:T(8,128)(2,1)}, u32[]{:S(2)}) copy-start(bf16[1,1,16,6,64,64]{5,4,3,2,1,0:T(8,128)(2,1)} %param.7) | copy-start | bytes 2359300
  0.0 7.7 %collective-permute-start = (s32[2,8]{1,0:T(2,128)}, s32[2,8]{1,0:T(2,128)S(1)}, u32[]{:S(2)}, u32[]{:S(2)}) collective-permute-start(s32[2,8]{1,0:T(2,128)} %bitcast.246), channel_id=1, source_target_pairs={{0,1},{1,2},{2,3},{3,4},{4,5},{5,6},{6,7},{7,0},{8,9},{9,10},{10,1... | collective-permute-start | bytes 200 | tf_op jit(solution)/shard_map/ppermute | solution.py:12
  2.9 4.8 %collective-permute-start.3 = (s32[2,8]{1,0:T(2,128)}, s32[2,8]{1,0:T(2,128)S(1)}, u32[]{:S(2)}, u32[]{:S(2)}) collective-permute-start(s32[2,8]{1,0:T(2,128)} %bitcast.244), channel_id=1, source_target_pairs={{0,8},{8,16},{16,24},{24,0},{1,9},{9,17},{17,25},{25,1},{2,10},{10... | collective-permute-start | bytes 200 | tf_op jit(solution)/shard_map/ppermute | solution.py:12
  2.9 71.7 %collective-permute-start.4 = (bf16[2,8,64,64]{3,2,1,0:T(8,128)(2,1)}, bf16[2,8,64,64]{3,2,1,0:T(8,128)(2,1)}, u32[]{:S(2)}, u32[]{:S(2)}) collective-permute-start(bf16[2,8,64,64]{3,2,1,0:T(8,128)(2,1)} %bitcast.242), channel_id=1, source_target_pairs={{0,8},{8,16},{16,24},{24,0},{1,9},{9,17},{17,25},{25,1},{2,10},{10... | collective-permute-start | bytes 393224 | tf_op jit(solution)/shard_map/ppermute | solution.py:12
  7.7 6.3 %collective-permute-start.2 = (s32[2,8]{1,0:T(2,128)S(1)}, s32[2,8]{1,0:T(2,128)S(1)}, u32[]{:S(2)}, u32[]{:S(2)}) collective-permute-start(s32[2,8]{1,0:T(2,128)S(1)} %collective-permute-done), channel_id=1, source_target_pairs={{0,1},{1,2},{2,3},{3,4},{4,5},{5,6},{6,7},{7,0},{8,9},{9,10},{10,1... | collective-permute-start | bytes 200 | tf_op jit(solution)/shard_map/ppermute | solution.py:12
  8.4 5.7 %collective-permute-start.7 = (s32[2,8]{1,0:T(2,128)S(1)}, s32[2,8]{1,0:T(2,128)S(1)}, u32[]{:S(2)}, u32[]{:S(2)}) collective-permute-start(s32[2,8]{1,0:T(2,128)S(1)} %collective-permute-done.3), channel_id=1, source_target_pairs={{0,8},{8,16},{16,24},{24,0},{1,9},{9,17},{17,25},{25,1},{2,10},{10... | collective-permute-start | bytes 200 | tf_op jit(solution)/shard_map/ppermute | solution.py:12
  14.0 6.3 %collective-permute-start.6 = (s32[2,8]{1,0:T(2,128)S(1)}, s32[2,8]{1,0:T(2,128)S(1)}, u32[]{:S(2)}, u32[]{:S(2)}) collective-permute-start(s32[2,8]{1,0:T(2,128)S(1)} %collective-permute-done.2), channel_id=1, source_target_pairs={{0,1},{1,2},{2,3},{3,4},{4,5},{5,6},{6,7},{7,0},{8,9},{9,10},{10,1... | collective-permute-start | bytes 200 | tf_op jit(solution)/shard_map/ppermute | solution.py:12
  14.6 5.7 %collective-permute-start.11 = (s32[2,8]{1,0:T(2,128)S(1)}, s32[2,8]{1,0:T(2,128)S(1)}, u32[]{:S(2)}, u32[]{:S(2)}) collective-permute-start(s32[2,8]{1,0:T(2,128)S(1)} %collective-permute-done.7), channel_id=1, source_target_pairs={{0,8},{8,16},{16,24},{24,0},{1,9},{9,17},{17,25},{25,1},{2,10},{10... | collective-permute-start | bytes 200 | tf_op jit(solution)/shard_map/ppermute | solution.py:12
  20.3 6.3 %collective-permute-start.10 = (s32[2,8]{1,0:T(2,128)S(1)}, s32[2,8]{1,0:T(2,128)S(1)}, u32[]{:S(2)}, u32[]{:S(2)}) collective-permute-start(s32[2,8]{1,0:T(2,128)S(1)} %collective-permute-done.6), channel_id=1, source_target_pairs={{0,1},{1,2},{2,3},{3,4},{4,5},{5,6},{6,7},{7,0},{8,9},{9,10},{10,1... | collective-permute-start | bytes 200 | tf_op jit(solution)/shard_map/ppermute | solution.py:12
  20.9 5.7 %collective-permute-start.15 = (s32[2,8]{1,0:T(2,128)S(1)}, s32[2,8]{1,0:T(2,128)S(1)}, u32[]{:S(2)}, u32[]{:S(2)}) collective-permute-start(s32[2,8]{1,0:T(2,128)S(1)} %collective-permute-done.11), channel_id=1, source_target_pairs={{0,8},{8,16},{16,24},{24,0},{1,9},{9,17},{17,25},{25,1},{2,10},{10... | collective-permute-start | bytes 200 | tf_op jit(solution)/shard_map/ppermute | solution.py:12
  26.5 6.3 %collective-permute-start.14 = (s32[2,8]{1,0:T(2,128)S(1)}, s32[2,8]{1,0:T(2,128)S(1)}, u32[]{:S(2)}, u32[]{:S(2)}) collective-permute-start(s32[2,8]{1,0:T(2,128)S(1)} %collective-permute-done.10), channel_id=1, source_target_pairs={{0,1},{1,2},{2,3},{3,4},{4,5},{5,6},{6,7},{7,0},{8,9},{9,10},{10,1... | collective-permute-start | bytes 200 | tf_op jit(solution)/shard_map/ppermute | solution.py:12
  27.1 5.7 %collective-permute-start.19 = (s32[2,8]{1,0:T(2,128)S(1)}, s32[2,8]{1,0:T(2,128)S(1)}, u32[]{:S(2)}, u32[]{:S(2)}) collective-permute-start(s32[2,8]{1,0:T(2,128)S(1)} %collective-permute-done.15), channel_id=1, source_target_pairs={{0,8},{8,16},{16,24},{24,0},{1,9},{9,17},{17,25},{25,1},{2,10},{10... | collective-permute-start | bytes 200 | tf_op jit(solution)/shard_map/ppermute | solution.py:12
  32.8 6.3 %collective-permute-start.18 = (s32[2,8]{1,0:T(2,128)S(1)}, s32[2,8]{1,0:T(2,128)S(1)}, u32[]{:S(2)}, u32[]{:S(2)}) collective-permute-start(s32[2,8]{1,0:T(2,128)S(1)} %collective-permute-done.14), channel_id=1, source_target_pairs={{0,1},{1,2},{2,3},{3,4},{4,5},{5,6},{6,7},{7,0},{8,9},{9,10},{10,1... | collective-permute-start | bytes 200 | tf_op jit(solution)/shard_map/ppermute | solution.py:12
  33.4 5.7 %collective-permute-start.23 = (s32[2,8]{1,0:T(2,128)S(1)}, s32[2,8]{1,0:T(2,128)S(1)}, u32[]{:S(2)}, u32[]{:S(2)}) collective-permute-start(s32[2,8]{1,0:T(2,128)S(1)} %collective-permute-done.19), channel_id=1, source_target_pairs={{0,8},{8,16},{16,24},{24,0},{1,9},{9,17},{17,25},{25,1},{2,10},{10... | collective-permute-start | bytes 200 | tf_op jit(solution)/shard_map/ppermute | solution.py:12
  39.1 6.3 %collective-permute-start.22 = (s32[2,8]{1,0:T(2,128)S(1)}, s32[2,8]{1,0:T(2,128)S(1)}, u32[]{:S(2)}, u32[]{:S(2)}) collective-permute-start(s32[2,8]{1,0:T(2,128)S(1)} %collective-permute-done.18), channel_id=1, source_target_pairs={{0,1},{1,2},{2,3},{3,4},{4,5},{5,6},{6,7},{7,0},{8,9},{9,10},{10,1... | collective-permute-start | bytes 200 | tf_op jit(solution)/shard_map/ppermute | solution.py:12
  39.7 5.6 %collective-permute-start.27 = (s32[2,8]{1,0:T(2,128)S(1)}, s32[2,8]{1,0:T(2,128)S(1)}, u32[]{:S(2)}, u32[]{:S(2)}) collective-permute-start(s32[2,8]{1,0:T(2,128)S(1)} %collective-permute-done.23), channel_id=1, source_target_pairs={{0,8},{8,16},{16,24},{24,0},{1,9},{9,17},{17,25},{25,1},{2,10},{10... | collective-permute-start | bytes 200 | tf_op jit(solution)/shard_map/ppermute | solution.py:12
  45.3 6.3 %collective-permute-start.26 = (s32[2,8]{1,0:T(2,128)S(1)}, s32[2,8]{1,0:T(2,128)S(1)}, u32[]{:S(2)}, u32[]{:S(2)}) collective-permute-start(s32[2,8]{1,0:T(2,128)S(1)} %collective-permute-done.22), channel_id=1, source_target_pairs={{0,1},{1,2},{2,3},{3,4},{4,5},{5,6},{6,7},{7,0},{8,9},{9,10},{10,1... | collective-permute-start | bytes 200 | tf_op jit(solution)/shard_map/ppermute | solution.py:12
  56.3 4.2 %copy-start.5 = (bf16[1,1,2,8,64,64]{5,4,3,2,1,0:T(8,128)(2,1)S(1)}, bf16[1,1,2,8,64,64]{5,4,3,2,1,0:T(8,128)(2,1)}, u32[]{:S(2)}) copy-start(bf16[1,1,2,8,64,64]{5,4,3,2,1,0:T(8,128)(2,1)} %param.5) | copy-start | bytes 393220
  60.5 2.4 %copy-start.4 = (f32[2,16,8,6]{3,1,2,0:T(8,128)S(1)}, f32[2,16,8,6]{3,1,2,0:T(8,128)}, u32[]{:S(2)}) copy-start(f32[2,16,8,6]{3,1,2,0:T(8,128)} %get-tuple-element.6) | copy-start | bytes 18436
  60.5 2.4 %copy-start.12 = (f32[2,16,8]{2,1,0:T(8,128)S(1)}, f32[2,16,8]{2,1,0:T(8,128)}, u32[]{:S(2)}) copy-start(f32[2,16,8]{2,1,0:T(8,128)} %convert_bitcast_fusion.14) | copy-start | bytes 3076
  62.8 11.9 %collective-permute-start.1 = (f32[2,8,64,64]{2,3,1,0:T(8,128)S(1)}, f32[2,8,64,64]{2,3,1,0:T(8,128)S(1)}, u32[]{:S(2)}, u32[]{:S(2)}) collective-permute-start(f32[2,8,64,64]{2,3,1,0:T(8,128)S(1)} %fusion.15), channel_id=1, source_target_pairs={{0,1},{1,2},{2,3},{3,4},{4,5},{5,6},{6,7},{7,0},{8,9},{9,10},{10,1... | collective-permute-start | bytes 786440 | tf_op jit(solution)/shard_map/ppermute | solution.py:12
  68.2 4.2 %copy-start.3 = (f32[2,16,8,6]{3,1,2,0:T(8,128)S(1)}, f32[2,16,8,6]{3,1,2,0:T(8,128)}, u32[]{:S(2)}) copy-start(f32[2,16,8,6]{3,1,2,0:T(8,128)} %get-tuple-element.7) | copy-start | bytes 18436
  74.7 2.4 %copy-start.11 = (bf16[2,8,8,16,6,1]{3,2,4,5,1,0:T(8,128)(2,1)S(1)}, bf16[2,8,8,16,6,1]{3,2,4,5,1,0:T(8,128)(2,1)}, u32[]{:S(2)}) copy-start(bf16[2,8,8,16,6,1]{3,2,4,5,1,0:T(8,128)(2,1)} %copy.25) | copy-start | bytes 73732
  77.0 13.3 %collective-permute-start.5 = (f32[2,8,64,64]{2,3,1,0:T(8,128)S(1)}, f32[2,8,64,64]{2,3,1,0:T(8,128)S(1)}, u32[]{:S(2)}, u32[]{:S(2)}) collective-permute-start(f32[2,8,64,64]{2,3,1,0:T(8,128)S(1)} %fusion.16), channel_id=1, source_target_pairs={{0,1},{1,2},{2,3},{3,4},{4,5},{5,6},{6,7},{7,0},{8,9},{9,10},{10,1... | collective-permute-start | bytes 786440 | tf_op jit(solution)/shard_map/ppermute | solution.py:12
  79.8 4.2 %copy-start.2 = (f32[2,16,8,6]{3,1,2,0:T(8,128)S(1)}, f32[2,16,8,6]{3,1,2,0:T(8,128)}, u32[]{:S(2)}) copy-start(f32[2,16,8,6]{3,1,2,0:T(8,128)} %get-tuple-element.8) | copy-start | bytes 18436
  84.0 6.3 %collective-permute-start.8 = (bf16[2,8,64,64]{3,2,1,0:T(8,128)(2,1)}, bf16[2,8,64,64]{3,2,1,0:T(8,128)(2,1)}, u32[]{:S(2)}, u32[]{:S(2)}) collective-permute-start(bf16[2,8,64,64]{3,2,1,0:T(8,128)(2,1)} %collective-permute-done.4), channel_id=1, source_target_pairs={{0,8},{8,16},{16,24},{24,0},{1,9},{9,17},{17,25},{25,1},{2,10},{10... | collective-permute-start | bytes 393224 | tf_op jit(solution)/shard_map/ppermute | solution.py:12
  86.6 6.1 %copy-start.7 = (bf16[2,8,8,16,6,1]{3,2,4,5,1,0:T(8,128)(2,1)S(1)}, bf16[2,8,8,16,6,1]{3,2,4,5,1,0:T(8,128)(2,1)}, u32[]{:S(2)}) copy-start(bf16[2,8,8,16,6,1]{3,2,4,5,1,0:T(8,128)(2,1)} %copy.29) | copy-start | bytes 73732
  92.7 16.2 %collective-permute-start.9 = (f32[2,8,64,64]{2,3,1,0:T(8,128)S(1)}, f32[2,8,64,64]{2,3,1,0:T(8,128)S(1)}, u32[]{:S(2)}, u32[]{:S(2)}) collective-permute-start(f32[2,8,64,64]{2,3,1,0:T(8,128)S(1)} %fusion.17), channel_id=1, source_target_pairs={{0,1},{1,2},{2,3},{3,4},{4,5},{5,6},{6,7},{7,0},{8,9},{9,10},{10,1... | collective-permute-start | bytes 786440 | tf_op jit(solution)/shard_map/ppermute | solution.py:12
  95.5 4.2 %copy-start.1 = (f32[2,16,8,6]{3,1,2,0:T(8,128)S(1)}, f32[2,16,8,6]{3,1,2,0:T(8,128)}, u32[]{:S(2)}) copy-start(f32[2,16,8,6]{3,1,2,0:T(8,128)} %get-tuple-element.9) | copy-start | bytes 18436
  99.7 6.2 %collective-permute-start.12 = (bf16[2,8,64,64]{3,2,1,0:T(8,128)(2,1)}, bf16[2,8,64,64]{3,2,1,0:T(8,128)(2,1)}, u32[]{:S(2)}, u32[]{:S(2)}) collective-permute-start(bf16[2,8,64,64]{3,2,1,0:T(8,128)(2,1)} %collective-permute-done.8), channel_id=1, source_target_pairs={{0,8},{8,16},{16,24},{24,0},{1,9},{9,17},{17,25},{25,1},{2,10},{10... | collective-permute-start | bytes 393224 | tf_op jit(solution)/shard_map/ppermute | solution.py:12
  102.1 9.2 %copy-start.8 = (bf16[2,8,8,16,6,1]{3,2,4,5,1,0:T(8,128)(2,1)S(1)}, bf16[2,8,8,16,6,1]{3,2,4,5,1,0:T(8,128)(2,1)}, u32[]{:S(2)}) copy-start(bf16[2,8,8,16,6,1]{3,2,4,5,1,0:T(8,128)(2,1)} %copy.33) | copy-start | bytes 73732
  111.1 15.3 %collective-permute-start.13 = (f32[2,8,64,64]{2,3,1,0:T(8,128)S(1)}, f32[2,8,64,64]{2,3,1,0:T(8,128)S(1)}, u32[]{:S(2)}, u32[]{:S(2)}) collective-permute-start(f32[2,8,64,64]{2,3,1,0:T(8,128)S(1)} %fusion.18), channel_id=1, source_target_pairs={{0,1},{1,2},{2,3},{3,4},{4,5},{5,6},{6,7},{7,0},{8,9},{9,10},{10,1... | collective-permute-start | bytes 786440 | tf_op jit(solution)/shard_map/ppermute | solution.py:12
  118.1 6.2 %collective-permute-start.16 = (bf16[2,8,64,64]{3,2,1,0:T(8,128)(2,1)}, bf16[2,8,64,64]{3,2,1,0:T(8,128)(2,1)}, u32[]{:S(2)}, u32[]{:S(2)}) collective-permute-start(bf16[2,8,64,64]{3,2,1,0:T(8,128)(2,1)} %collective-permute-done.12), channel_id=1, source_target_pairs={{0,8},{8,16},{16,24},{24,0},{1,9},{9,17},{17,25},{25,1},{2,10},{10... | collective-permute-start | bytes 393224 | tf_op jit(solution)/shard_map/ppermute | solution.py:12
  120.5 8.3 %copy-start.9 = (bf16[2,8,8,16,6,1]{3,2,4,5,1,0:T(8,128)(2,1)S(1)}, bf16[2,8,8,16,6,1]{3,2,4,5,1,0:T(8,128)(2,1)}, u32[]{:S(2)}) copy-start(bf16[2,8,8,16,6,1]{3,2,4,5,1,0:T(8,128)(2,1)} %copy.37) | copy-start | bytes 73732
  128.7 14.4 %collective-permute-start.17 = (f32[2,8,64,64]{2,3,1,0:T(8,128)S(1)}, f32[2,8,64,64]{2,3,1,0:T(8,128)S(1)}, u32[]{:S(2)}, u32[]{:S(2)}) collective-permute-start(f32[2,8,64,64]{2,3,1,0:T(8,128)S(1)} %fusion.19), channel_id=1, source_target_pairs={{0,1},{1,2},{2,3},{3,4},{4,5},{5,6},{6,7},{7,0},{8,9},{9,10},{10,1... | collective-permute-start | bytes 786440 | tf_op jit(solution)/shard_map/ppermute | solution.py:12
  135.7 6.1 %collective-permute-start.20 = (bf16[2,8,64,64]{3,2,1,0:T(8,128)(2,1)}, bf16[2,8,64,64]{3,2,1,0:T(8,128)(2,1)S(1)}, u32[]{:S(2)}, u32[]{:S(2)}) collective-permute-start(bf16[2,8,64,64]{3,2,1,0:T(8,128)(2,1)} %collective-permute-done.16), channel_id=1, source_target_pairs={{0,8},{8,16},{16,24},{24,0},{1,9},{9,17},{17,25},{25,1},{2,10},{10... | collective-permute-start | bytes 393224 | tf_op jit(solution)/shard_map/ppermute | solution.py:12
  138.1 7.6 %copy-start.10 = (bf16[2,8,8,16,6,1]{3,2,4,5,1,0:T(8,128)(2,1)S(1)}, bf16[2,8,8,16,6,1]{3,2,4,5,1,0:T(8,128)(2,1)}, u32[]{:S(2)}) copy-start(bf16[2,8,8,16,6,1]{3,2,4,5,1,0:T(8,128)(2,1)} %copy.41) | copy-start | bytes 73732
  145.4 13.7 %collective-permute-start.21 = (f32[2,8,64,64]{2,3,1,0:T(8,128)S(1)}, f32[2,8,64,64]{2,3,1,0:T(8,128)S(1)}, u32[]{:S(2)}, u32[]{:S(2)}) collective-permute-start(f32[2,8,64,64]{2,3,1,0:T(8,128)S(1)} %fusion.20), channel_id=1, source_target_pairs={{0,1},{1,2},{2,3},{3,4},{4,5},{5,6},{6,7},{7,0},{8,9},{9,10},{10,1... | collective-permute-start | bytes 786440 | tf_op jit(solution)/shard_map/ppermute | solution.py:12
  152.5 6.0 %collective-permute-start.24 = (bf16[2,8,64,64]{3,2,1,0:T(8,128)(2,1)S(1)}, bf16[2,8,64,64]{3,2,1,0:T(8,128)(2,1)}, u32[]{:S(2)}, u32[]{:S(2)}) collective-permute-start(bf16[2,8,64,64]{3,2,1,0:T(8,128)(2,1)S(1)} %collective-permute-done.20), channel_id=1, source_target_pairs={{0,8},{8,16},{16,24},{24,0},{1,9},{9,17},{17,25},{25,1},{2,10},{10... | collective-permute-start | bytes 393224 | tf_op jit(solution)/shard_map/ppermute | solution.py:12
  154.2 7.2 %copy-start.6 = (bf16[2,8,8,16,6,1]{3,2,4,5,1,0:T(8,128)(2,1)S(1)}, bf16[2,8,8,16,6,1]{3,2,4,5,1,0:T(8,128)(2,1)}, u32[]{:S(2)}) copy-start(bf16[2,8,8,16,6,1]{3,2,4,5,1,0:T(8,128)(2,1)} %copy.45) | copy-start | bytes 73732
  158.5 9.7 %collective-permute-start.28 = (bf16[2,8,64,64]{3,2,1,0:T(8,128)(2,1)}, bf16[2,8,64,64]{3,2,1,0:T(8,128)(2,1)S(1)}, u32[]{:S(2)}, u32[]{:S(2)}) collective-permute-start(bf16[2,8,64,64]{3,2,1,0:T(8,128)(2,1)} %collective-permute-done.24), channel_id=1, source_target_pairs={{0,8},{8,16},{16,24},{24,0},{1,9},{9,17},{17,25},{25,1},{2,10},{10... | collective-permute-start | bytes 393224 | tf_op jit(solution)/shard_map/ppermute | solution.py:12
  161.3 16.4 %collective-permute-start.25 = (f32[2,8,64,64]{2,3,1,0:T(8,128)S(1)}, f32[2,8,64,64]{2,3,1,0:T(8,128)S(1)}, u32[]{:S(2)}, u32[]{:S(2)}) collective-permute-start(f32[2,8,64,64]{2,3,1,0:T(8,128)S(1)} %fusion.21), channel_id=1, source_target_pairs={{0,1},{1,2},{2,3},{3,4},{4,5},{5,6},{6,7},{7,0},{8,9},{9,10},{10,1... | collective-permute-start | bytes 786440 | tf_op jit(solution)/shard_map/ppermute | solution.py:12
where the time goes:
time: 182 us; the launch traced here: 181 us
  waiting for transfers between devices  77.7 us (43%)
  local copies, waits for them, and re-layouts  44.8 us (25%)
  matrix products  40.9 us (22%)
  other arithmetic  11.6 us (6%)
  starting transfers between devices  5.71 us (3%)
    ppermute x29, waiting for transfers between devices, shifted(): return lax.ppermute(value, axis, pairs)  77.7 us
    dot_general x8, local copies, waits for them, and re-layouts, one_tick(): jnp.einsum('iaokb,kbyz->iaoyz', select, right, preferred_element_type=jnp...  33.2 us
    dot_general x8, matrix products, one_tick(): jnp.einsum('iaokb,kbyz->iaoyz', select, right, preferred_element_type=jnp...  22.6 us
    dot_general x8, matrix products, one_tick(): jnp.einsum('iaxy,iaoyz->ioxz', left, chosen, preferred_element_type=jnp.f...  18.3 us
    convert_element_type x8, local copies, waits for them, and re-layouts, one_tick(): select = jnp.einsum('iak,iokb->iaokb', pick_row, match).astype(jnp.bfloat16)  9.43 us
    convert_element_type x8, other arithmetic, one_tick(): select = jnp.einsum('iak,iokb->iaokb', pick_row, match).astype(jnp.bfloat16)  6.27 us
    ppermute x29, starting transfers between devices, shifted(): return lax.ppermute(value, axis, pairs)  5.71 us
    another operation x9, other arithmetic  5.3 us
  transfers between devices with their start and end apart: 29, of which 18 were waited for; matrix products, arithmetic and copies ran while one was open for 46% of the time, Pallas kernels for 0%

commit v1 on v0

--- a/solution.py
+++ b/solution.py
@@ -1,9 +1,17 @@
+import functools
+
 import jax
 import jax.numpy as jnp
 from jax import lax
+from jax.experimental import pallas as pl
+from jax.experimental.pallas import tpu as pltpu
 from jax.sharding import PartitionSpec as P
 
 TICKS = 8
+LANES = 128
+PAD = 16
+TOP = 32767.0
+GRAIN = 8192.0
 
 
 def shifted(value, axis, steps):
@@ -25,7 +33,7 @@
     return jnp.einsum("iaxy,iaoyz->ioxz", left, chosen, preferred_element_type=jnp.float32)
 
 
-def on_device(left_blocks, left_cols, right_blocks, right_cols, out_cols):
+def ring(left_blocks, left_cols, right_blocks, right_cols, out_cols):
     left = left_blocks[0, 0]
     left_index = left_cols[0, 0]
     right = right_blocks[0, 0]
@@ -41,6 +49,230 @@
     return total[None, None]
 
 
+def encode(value, code_ref, lanes):
+    rows = value.shape[0]
+    peak = jnp.maximum(jnp.max(jnp.abs(value), axis=0, keepdims=True), 2.0**-100)
+    power = jnp.floor(jnp.log2(peak))
+    grains = jnp.ceil(peak * jnp.exp2(-power) * GRAIN) + 1.0
+    factor = (TOP * GRAIN / grains) * jnp.exp2(-power)
+    code_ref[:rows, lanes] = jnp.round(value * factor).astype(jnp.int32).astype(jnp.int16)
+    row = lax.broadcasted_iota(jnp.int32, (PAD, value.shape[1]), 0)
+    scale = jnp.where(row == 0, power, grains).astype(jnp.int32)
+    code_ref[rows:, lanes] = scale.astype(jnp.int16)
+
+
+def decode(code_ref, lanes, rows):
+    power = code_ref[rows : rows + PAD, lanes].astype(jnp.int32).astype(jnp.float32)
+    scale = jnp.exp2(power[:1]) * (power[1:2] * (1.0 / (TOP * GRAIN)))
+    return code_ref[:rows, lanes].astype(jnp.int32).astype(jnp.float32) * scale
+
+
+def spread_left(packed_ref, rows, half, pairs, dense_ref):
+    blocks = packed_ref.shape[1] // LANES
+    for i in range(rows // half):
+        index = packed_ref[rows : rows + PAD, :].astype(jnp.float32)[i : i + 1, :].astype(jnp.int32)
+        side = lax.broadcasted_iota(jnp.int32, (1, LANES), 1) // half
+        here, there = [], []
+        for b in range(blocks):
+            column = index[:, b * LANES : (b + 1) * LANES]
+            here.append(column - side)
+            there.append(pltpu.roll(column, half, 1) - side)
+        data = [
+            packed_ref[i * half : (i + 1) * half, b * LANES : (b + 1) * LANES].astype(jnp.float32)
+            for b in range(blocks)
+        ]
+        turned = [pltpu.roll(d, half, 1) for d in data]
+        for m in range(pairs):
+            total = jnp.zeros((half, LANES), jnp.float32)
+            for b in range(blocks):
+                total = jnp.where(here[b] == 2 * m, data[b], total)
+                total = jnp.where(there[b] == 2 * m, turned[b], total)
+            dense_ref[i * half : (i + 1) * half, m * LANES : (m + 1) * LANES] = total.astype(
+                jnp.bfloat16
+            )
+
+
+def spread_right(cols_ref, right_ref, dense_ref):
+    _, _, kb, kept, half, _ = right_ref.shape
+    pairs = dense_ref.shape[1] // LANES
+    side = lax.broadcasted_iota(jnp.int32, (half, LANES), 1) // half
+    for k in range(kb):
+        blocks = []
+        for e in range(kept):
+            block = right_ref[0, 0, k, e].astype(jnp.float32)
+            blocks.append((jnp.concatenate([block, block], axis=1), cols_ref[0, 0, k, e]))
+        for m in range(pairs):
+            total = jnp.zeros((half, LANES), jnp.float32)
+            for block, col in blocks:
+                total = jnp.where(side == col - 2 * m, block, total)
+            dense_ref[k * half : (k + 1) * half, m * LANES : (m + 1) * LANES] = total.astype(
+                jnp.bfloat16
+            )
+
+
+def first_kernel(cols_ref, right_ref, packed_ref, dense_ref, code_ref, left_ref):
+    rows = left_ref.shape[0]
+    half = right_ref.shape[4]
+    spread_right(cols_ref, right_ref, dense_ref)
+    spread_left(packed_ref, rows, half, dense_ref.shape[0] // LANES, left_ref)
+    part = jnp.dot(left_ref[...], dense_ref[...], preferred_element_type=jnp.float32)
+    encode(part, code_ref, slice(None))
+
+
+def second_kernel(half, dense_ref, packed_ref, code_ref, left_ref):
+    rows = left_ref.shape[0]
+    spread_left(packed_ref, rows, half, left_ref.shape[1] // LANES, left_ref)
+    part = jnp.dot(left_ref[...], dense_ref[...], preferred_element_type=jnp.float32)
+    encode(part, code_ref, slice(None))
+
+
+def kept_kernel(half, dense_ref, near_ref, far_ref, a_ref, b_ref, left_ref):
+    rows = a_ref.shape[0]
+    pairs = left_ref.shape[1] // LANES
+    spread_left(near_ref, rows, half, pairs, left_ref.at[:rows])
+    spread_left(far_ref, rows, half, pairs, left_ref.at[rows:])
+    part = jnp.dot(left_ref[...], dense_ref[...], preferred_element_type=jnp.float32)
+    swap = (lax.axis_index("col") % 2) != (lax.axis_index("row") % 2)
+
+    @pl.when(swap)
+    def _():
+        a_ref[...] = part[rows:]
+        b_ref[...] = part[:rows]
+
+    @pl.when(jnp.logical_not(swap))
+    def _():
+        a_ref[...] = part[:rows]
+        b_ref[...] = part[rows:]
+
+
+def sum_kernel(half, odd, own_ref, one_ref, two_ref, three_ref, kept_ref, code_ref, a_ref, b_ref, wide_ref, out_ref):
+    rows, width = kept_ref.shape
+    pairs = width // LANES
+    for m in range(pairs):
+        lanes = slice(m * LANES, (m + 1) * LANES)
+        total = kept_ref[:, lanes] + decode(code_ref, lanes, rows)
+        wide_ref[m] = total
+        wide_ref[pairs + m] = pltpu.roll(total, half, 1)
+    even = (lax.axis_index("col") % 2) == odd
+    low = lax.broadcasted_iota(jnp.int32, (half, LANES), 1) < half
+    count = own_ref.shape[3]
+    for first, second, target in ((two_ref, one_ref, a_ref), (own_ref, three_ref, b_ref)):
+        for o in range(0, count, 2):
+            for i in range(rows // half):
+                picked = []
+                for side in range(2):
+                    j = jnp.where(even, first[0, 0, i, o + side], second[0, 0, i, o + side])
+                    slot = j // 2 + pairs * ((j + side) % 2)
+                    picked.append(wide_ref[slot, i * half : (i + 1) * half, :])
+                out_ref[i * half : (i + 1) * half, :] = jnp.where(low, picked[0], picked[1])
+            lanes = slice(o // 2 * LANES, (o // 2 + 1) * LANES)
+            encode(out_ref[...], target, lanes)
+
+
+def last_kernel(half, a_ref, b_ref, c_ref, d_ref, out_ref):
+    rows = a_ref.shape[0] - PAD
+    for m in range(a_ref.shape[1] // LANES):
+        lanes = slice(m * LANES, (m + 1) * LANES)
+        total = decode(a_ref, lanes, rows) + decode(b_ref, lanes, rows)
+        total = total + decode(c_ref, lanes, rows) + decode(d_ref, lanes, rows)
+        for i in range(rows // half):
+            part = total[i * half : (i + 1) * half]
+            out_ref[0, 0, i, 2 * m] = part[:, :half]
+            out_ref[0, 0, i, 2 * m + 1] = part[:, half:]
+
+
+VMEM = pl.BlockSpec(memory_space=pltpu.VMEM)
+SMEM = pl.BlockSpec(memory_space=pltpu.SMEM)
+PARAMS = pltpu.CompilerParams(vmem_limit_bytes=40 * 2**20)
+
+
+def grid_path(n_row, n_col, left_blocks, left_cols, right_blocks, right_cols, out_cols):
+    _, _, ib, nl, bs, _ = left_blocks.shape
+    kb = right_blocks.shape[2]
+    jb = kb
+    no = out_cols.shape[3]
+    rows = ib * bs
+
+    def send(value, to):
+        pairs = []
+        for r in range(n_row):
+            for c in range(n_col):
+                target = to(r, c)
+                pairs.append((r * n_col + c, target[0] * n_col + target[1]))
+        return lax.ppermute(value, ("row", "col"), pairs)
+
+    def along(even, odd):
+        return lambda r, c: (r, (c + 2 * (odd if c % 2 else even)) % n_col)
+
+    packed = left_blocks[0, 0].transpose(0, 2, 1, 3).reshape(rows, nl * bs)
+    index = jnp.repeat(left_cols[0, 0].astype(jnp.bfloat16), bs, axis=1)
+    packed = jnp.concatenate([packed, index, jnp.zeros((PAD - ib, nl * bs), jnp.bfloat16)], axis=0)
+    across = send(packed, lambda r, c: ((r + 2) % n_row, c))
+    near = send(packed, lambda r, c: (r ^ 1, c))
+    code = jax.ShapeDtypeStruct((rows + PAD, jb * bs), jnp.int16)
+    small = jax.ShapeDtypeStruct((rows + PAD, no * bs), jnp.int16)
+    wide = jax.ShapeDtypeStruct((rows, jb * bs), jnp.float32)
+    left_scratch = pltpu.VMEM((rows, kb * bs), jnp.bfloat16)
+    dense, code_one = pl.pallas_call(
+        first_kernel,
+        out_shape=(jax.ShapeDtypeStruct((kb * bs, jb * bs), jnp.bfloat16), code),
+        in_specs=[SMEM, VMEM, VMEM],
+        out_specs=(VMEM, VMEM),
+        scratch_shapes=[left_scratch],
+        compiler_params=PARAMS,
+        name="first",
+    )(right_cols, right_blocks, packed)
+    got_one = send(code_one, lambda r, c: (r, c ^ 1))
+    far = send(across, lambda r, c: (r ^ 1, c))
+    code_two = pl.pallas_call(
+        functools.partial(second_kernel, bs),
+        out_shape=code,
+        in_specs=[VMEM, VMEM],
+        out_specs=VMEM,
+        scratch_shapes=[left_scratch],
+        compiler_params=PARAMS,
+        name="second",
+    )(dense, across)
+    got_two = send(code_two, lambda r, c: (r, c ^ 1))
+    kept_a, kept_b = pl.pallas_call(
+        functools.partial(kept_kernel, bs),
+        out_shape=(wide, wide),
+        in_specs=[VMEM] * 3,
+        out_specs=(VMEM, VMEM),
+        scratch_shapes=[pltpu.VMEM((2 * rows, kb * bs), jnp.bfloat16)],
+        compiler_params=PARAMS,
+        name="kept",
+    )(dense, near, far)
+    pattern = [send(out_cols, along(-d, -d)) for d in (1, 2, -1)]
+
+    def summed(odd, kept, code):
+        return pl.pallas_call(
+            functools.partial(sum_kernel, bs, odd),
+            out_shape=(small, small),
+            in_specs=[SMEM] * 4 + [VMEM] * 2,
+            out_specs=(VMEM, VMEM),
+            scratch_shapes=[
+                pltpu.VMEM((2 * (jb * bs // LANES), rows, LANES), jnp.float32),
+                pltpu.VMEM((rows, LANES), jnp.float32),
+            ],
+            compiler_params=PARAMS,
+            name="sum",
+        )(out_cols, *pattern, kept, code)
+
+    a, b = summed(0, kept_a, got_one)
+    got = [send(a, along(2, 1)), send(b, along(0, -1))]
+    a, b = summed(1, kept_b, got_two)
+    got += [send(a, along(1, 2)), send(b, along(-1, 0))]
+    return pl.pallas_call(
+        functools.partial(last_kernel, bs),
+        out_shape=jax.ShapeDtypeStruct((1, 1, ib, no, bs, bs), jnp.float32),
+        in_specs=[VMEM] * 4,
+        out_specs=VMEM,
+        compiler_params=PARAMS,
+        name="last",
+    )(*got)
+
+
 def solution(mesh):
     in_specs = (
         P("row", "col", None, None, None, None),
@@ -50,6 +282,6 @@
         P("row", "col", None, None),
     )
     out_specs = P("row", "col", None, None, None, None)
-    return jax.shard_map(
-        on_device, mesh=mesh, in_specs=in_specs, out_specs=out_specs, check_vma=False
-    )
+    n_row, n_col = mesh.shape["row"], mesh.shape["col"]
+    body = functools.partial(grid_path, n_row, n_col) if (n_row, n_col) == (4, TICKS) else ring
+    return jax.shard_map(body, mesh=mesh, in_specs=in_specs, out_specs=out_specs, check_vma=False)

time: 182 us -> 40.2 us (0.22)
  waiting for transfers between devices: 77.7 us -> 8.22 us
  local copies, waits for them, and re-layouts: 44.8 us -> 3.75 us
  matrix products: 40.9 us -> 0 us
  starting transfers between devices: 5.71 us -> 18.3 us
  other arithmetic: 11.6 us -> 0.78 us
  Pallas kernels: 0 us -> 8.84 us
    ppermute x29 -> x12, waiting for transfers between devices: 77.7 us -> 8.22 us  [send(): return lax.ppermute(value, ('row', 'col'), pairs)]
    dot_general x16 -> x0, matrix products: 40.9 us -> none  [the longest x8 22.6 us: one_tick(): jnp.einsum('iaokb,kbyz->iaoyz', select, right, preferred_element_type=jnp...]
    dot_general x8 -> x0, local copies, waits for them, and re-layouts: 33.2 us -> none  [one_tick(): jnp.einsum('iaokb,kbyz->iaoyz', select, right, preferred_element_type=jnp...]
    ppermute x29 -> x12, starting transfers between devices: 5.71 us -> 18.3 us  [send(): return lax.ppermute(value, ('row', 'col'), pairs)]
    convert_element_type x8 -> x0, local copies, waits for them, and re-layouts: 9.43 us -> none  [one_tick(): select = jnp.einsum('iak,iokb->iaokb', pick_row, match).astype(jnp.bfloat16)]
    pallas_call x0 -> x6, Pallas kernels: none -> 8.84 us  [the longest x1 3.48 us: grid_path(): pl.pallas_call(first_kernel, out_shape=(jax.ShapeDtypeStruct((kb * bs, jb...]
    convert_element_type x8 -> x1, other arithmetic: 6.27 us -> 0.68 us  [grid_path(): index = jnp.repeat(left_cols[0, 0].astype(jnp.bfloat16), bs, axis=1)]
    another operation x9 -> x0, other arithmetic: 5.3 us -> none
  transfers between devices with their start and end apart: 29 -> 12, of which waited for: 18 -> 4; matrix products, arithmetic and copies ran while one was open for 46% -> 2% of each run, Pallas kernels for 0% -> 20%
where the time goes in v1:
time: 40.2 us; the launch traced here: 39.9 us
  starting transfers between devices  18.3 us (46%)
  Pallas kernels  8.84 us (22%)
  waiting for transfers between devices  8.22 us (20%)
  local copies, waits for them, and re-layouts  3.75 us (9%)
  other arithmetic  0.78 us (2%)
    ppermute x12, starting transfers between devices, send(): return lax.ppermute(value, ('row', 'col'), pairs)  18.3 us
    ppermute x12, waiting for transfers between devices, send(): return lax.ppermute(value, ('row', 'col'), pairs)  8.22 us
    pallas_call x1, Pallas kernels, grid_path(): pl.pallas_call(first_kernel, out_shape=(jax.ShapeDtypeStruct((kb * bs, jb...  3.48 us
    unnamed x5, local copies, waits for them, and re-layouts  2.17 us
    pallas_call x2, Pallas kernels, summed(): pl.pallas_call(functools.partial(sum_kernel, bs, odd), out_shape=(small,...  2.15 us
    pallas_call x1, Pallas kernels, grid_path(): pl.pallas_call(functools.partial(kept_kernel, bs), out_shape=(wide, wide)...  1.38 us
    transpose x1, local copies, waits for them, and re-layouts, grid_path(): packed = left_blocks[0, 0].transpose(0, 2, 1, 3).reshape(rows, nl * bs)  1.12 us
    pallas_call x1, Pallas kernels, grid_path(): pl.pallas_call(functools.partial(last_kernel, bs), out_shape=jax.ShapeDty...  1.01 us
  transfers between devices with their start and end apart: 12, of which 4 were waited for; matrix products, arithmetic and copies ran while one was open for 2% of the time, Pallas kernels for 20%

profile of v1, /device:TPU:0, one launch (start us, length us, event | category | flops | bytes accessed | tf_op | source)
XLA Modules:
  0.0 39.9 jit_solution(12750835566474059139)
XLA Ops:
  0.0 1.1 %copy.6 = bf16[2,64,8,64]{3,2,1,0:T(8,128)(2,1)S(1)} copy(bf16[2,64,8,64]{3,1,2,0:T(8,128)(2,1)} %bitcast.7) | data formatting | bytes 262144 | tf_op jit(solution)/shard_map/transpose | solution.py:207
  1.1 0.2 reshape.7
  1.3 0.7 %convert_bitcast_fusion = bf16[2,8]{1,0:T(2,128)(2,1)S(1)} fusion(s32[1,1,2,8]{3,2,1,0:T(2,128)} %param.6), kind=kLoop, calls=%fused_computation.1 | loop fusion | flops 16 | bytes 96 | tf_op jit(solution)/shard_map/convert_element_type | solution.py:208
  2.0 0.1 broadcast_in_dim.6
  2.1 0.1 reshape.8
  2.2 0.1 pad.2.clone
  2.3 0.1 maximum_maximum_fusion.packed_ref
  2.4 3.0 %collective-permute-start.4 = (bf16[144,512]{1,0:T(8,128)(2,1)S(1)}, bf16[144,512]{1,0:T(8,128)(2,1)S(1)}, u32[]{:S(2)}, u32[]{:S(2)}) collective-permute-start(bf16[144,512]{1,0:T(8,128)(2,1)S(1)} %maximum_maximum_fusion.packed_ref), channel_id=1, source_target_pairs={{0,16},{1,17},{2,18},{3,19},{4,20},{5,21},{6,22},{7,23},{8,24},{9,... | collective-permute-start | bytes 442376 | tf_op jit(solution)/shard_map/ppermute | solution.py:202
  5.4 0.8 %copy.7.cols_ref = s32[1,1,16,6]{3,2,1,0:T(8,128)S(1)} copy(s32[1,1,16,6]{2,1,3,0:T(1,128)} %param.8) | data formatting | bytes 768 | tf_op args[3]
  6.2 0.0 copy-start
  6.2 1.4 %copy-done = bf16[1,1,16,6,64,64]{5,4,3,2,1,0:T(8,128)(2,1)S(1)} copy-done((bf16[1,1,16,6,64,64]{5,4,3,2,1,0:T(8,128)(2,1)S(1)}, bf16[1,1,16,6,64,64]{5,4,3,2,1,0:T(8,128)(2,1)}, u32[]{:S(2)}) %copy-start) | copy-done | bytes 786456
  7.6 0.0 copy-start.1
  7.6 3.5 %first.1 = (bf16[1024,1024]{1,0:T(8,128)(2,1)S(1)}, s16[144,1024]{1,0:T(8,128)(2,1)S(1)}) custom-call(s32[1,1,16,6]{3,2,1,0:T(8,128)S(1)} %copy.7.cols_ref, bf16[1,1,16,6,64,64]{5,4,3,2,1,0:T(8,128)(2,1)S(1)} %copy-done, bf16[144,512]{1,0:T(8,128)(2,1)S(1)} %maximum_maximum_fusion.packed_ref), custom_call_target="tpu_custom_call" | custom-call | tf_op jit(solution)/shard_map/first/pallas_call | solution.py:216
  11.1 1.6 %collective-permute-start.6 = (s16[144,1024]{1,0:T(8,128)(2,1)S(1)}, s16[144,1024]{1,0:T(8,128)(2,1)S(1)}, u32[]{:S(2)}, u32[]{:S(2)}) collective-permute-start(s16[144,1024]{1,0:T(8,128)(2,1)S(1)} %get-tuple-element.15), channel_id=1, source_target_pairs={{0,1},{1,0},{2,3},{3,2},{4,5},{5,4},{6,7},{7,6},{8,9},{9,8},{10,11... | collective-permute-start | bytes 884744 | tf_op jit(solution)/shard_map/ppermute | solution.py:202
  12.6 0.0 collective-permute-done.4.packed_ref
  12.6 0.8 %second.1 = s16[144,1024]{1,0:T(8,128)(2,1)S(1)} custom-call(bf16[1024,1024]{1,0:T(8,128)(2,1)S(1)} %get-tuple-element.13.dense_ref, bf16[144,512]{1,0:T(8,128)(2,1)S(1)} %collective-permute-done.4.packed_ref), custom_call_target="tpu_custom_call" | custom-call | tf_op jit(solution)/shard_map/second/pallas_call | solution.py:227
  13.4 0.6 %collective-permute-start.9 = (s16[144,1024]{1,0:T(8,128)(2,1)S(1)}, s16[144,1024]{1,0:T(8,128)(2,1)S(1)}, u32[]{:S(2)}, u32[]{:S(2)}) collective-permute-start(s16[144,1024]{1,0:T(8,128)(2,1)S(1)} %second.1), channel_id=1, source_target_pairs={{0,1},{1,0},{2,3},{3,2},{4,5},{5,4},{6,7},{7,6},{8,9},{9,8},{10,11... | collective-permute-start | bytes 884744 | tf_op jit(solution)/shard_map/ppermute | solution.py:202
  14.0 0.0 collective-permute-start.3
  14.1 0.5 %collective-permute-start.5 = (bf16[144,512]{1,0:T(8,128)(2,1)S(1)}, bf16[144,512]{1,0:T(8,128)(2,1)S(1)}, u32[]{:S(2)}, u32[]{:S(2)}) collective-permute-start(bf16[144,512]{1,0:T(8,128)(2,1)S(1)} %collective-permute-done.4.packed_ref), channel_id=1, source_target_pairs={{0,8},{1,9},{2,10},{3,11},{4,12},{5,13},{6,14},{7,15},{8,0},{9,1},... | collective-permute-start | bytes 442376 | tf_op jit(solution)/shard_map/ppermute | solution.py:202
  14.6 0.0 copy-done.1
  14.6 3.6 %collective-permute-start = (s32[1,1,2,8]{3,2,1,0:T(2,128)S(1)}, s32[1,1,2,8]{3,2,1,0:T(2,128)S(1)}, u32[]{:S(2)}, u32[]{:S(2)}) collective-permute-start(s32[1,1,2,8]{3,2,1,0:T(2,128)S(1)} %copy-done.1), channel_id=1, source_target_pairs={{0,6},{1,7},{2,0},{3,1},{4,2},{5,3},{6,4},{7,5},{8,14},{9,15},{10,... | collective-permute-start | bytes 200 | tf_op jit(solution)/shard_map/ppermute | solution.py:202
  18.2 0.0 collective-permute-done.3.near_ref
  18.2 0.0 collective-permute-start.1
  18.2 0.0 collective-permute-done.5.far_ref
  18.2 1.4 %collective-permute-start.2 = (s32[1,1,2,8]{3,2,1,0:T(2,128)S(1)}, s32[1,1,2,8]{3,2,1,0:T(2,128)S(1)}, u32[]{:S(2)}, u32[]{:S(2)}) collective-permute-start(s32[1,1,2,8]{3,2,1,0:T(2,128)S(1)} %copy-done.1), channel_id=1, source_target_pairs={{0,2},{1,3},{2,4},{3,5},{4,6},{5,7},{6,0},{7,1},{8,10},{9,11},{10,... | collective-permute-start | bytes 200 | tf_op jit(solution)/shard_map/ppermute | solution.py:202
  19.6 1.4 %kept.1 = (f32[128,1024]{1,0:T(8,128)S(1)}, f32[128,1024]{1,0:T(8,128)S(1)}) custom-call(bf16[1024,1024]{1,0:T(8,128)(2,1)S(1)} %get-tuple-element.13.dense_ref, bf16[144,512]{1,0:T(8,128)(2,1)S(1)} %collective-permute-done.3.near_ref, bf16[144,512]{1,0:T(8,128)(2,1)S(1)} %collective-permute-done.5.far_ref), custom_call_target="tpu_custom_call" | custom-call | tf_op jit(solution)/shard_map/kept/pallas_call | solution.py:237
  21.0 0.0 collective-permute-done.one_ref
  21.0 1.6 %collective-permute-done.1.two_ref = s32[1,1,2,8]{3,2,1,0:T(2,128)S(1)} collective-permute-done((s32[1,1,2,8]{3,2,1,0:T(2,128)S(1)}, s32[1,1,2,8]{3,2,1,0:T(2,128)S(1)}, u32[]{:S(2)}, u32[]{:S(2)}) %collective-permute-start.1) | collective-permute-done | bytes 96 | tf_op jit(solution)/shard_map/ppermute | solution.py:202
  22.6 1.0 %collective-permute-done.2.three_ref = s32[1,1,2,8]{3,2,1,0:T(2,128)S(1)} collective-permute-done((s32[1,1,2,8]{3,2,1,0:T(2,128)S(1)}, s32[1,1,2,8]{3,2,1,0:T(2,128)S(1)}, u32[]{:S(2)}, u32[]{:S(2)}) %collective-permute-start.2) | collective-permute-done | bytes 96 | tf_op jit(solution)/shard_map/ppermute | solution.py:202
  23.6 0.0 collective-permute-done.6.code_ref
  23.6 1.1 %sum.2 = (s16[144,512]{1,0:T(8,128)(2,1)S(1)}, s16[144,512]{1,0:T(8,128)(2,1)S(1)}) custom-call(s32[1,1,2,8]{3,2,1,0:T(2,128)S(1)} %copy-done.1, s32[1,1,2,8]{3,2,1,0:T(2,128)S(1)} %collective-permute-done.one_ref, s32[1,1,2,8]{3,2,1,0:T(2,128)S(1)} %collective-permute-done.1.two_ref, s32[1,1,2,8]{3,2,1,0:T(2,128)S(1)} %collective-permute-done.2.three_ref, ...), custom_call_target="tpu_custom_call" | custom-call | tf_op jit(solution)/shard_map/sum/pallas_call | solution.py:249
  24.7 1.1 %collective-permute-start.7 = (s16[144,512]{1,0:T(8,128)(2,1)S(1)}, s16[144,512]{1,0:T(8,128)(2,1)S(1)}, u32[]{:S(2)}, u32[]{:S(2)}) collective-permute-start(s16[144,512]{1,0:T(8,128)(2,1)S(1)} %get-tuple-element.16), channel_id=1, source_target_pairs={{0,4},{1,3},{2,6},{3,5},{4,0},{5,7},{6,2},{7,1},{8,12},{9,11},{10,... | collective-permute-start | bytes 442376 | tf_op jit(solution)/shard_map/ppermute | solution.py:202
  25.8 0.7 %collective-permute-start.8 = (s16[144,512]{1,0:T(8,128)(2,1)S(1)}, s16[144,512]{1,0:T(8,128)(2,1)S(1)}, u32[]{:S(2)}, u32[]{:S(2)}) collective-permute-start(s16[144,512]{1,0:T(8,128)(2,1)S(1)} %get-tuple-element.17), channel_id=1, source_target_pairs={{0,0},{1,7},{2,2},{3,1},{4,4},{5,3},{6,6},{7,5},{8,8},{9,15},{10,1... | collective-permute-start | bytes 442376 | tf_op jit(solution)/shard_map/ppermute | solution.py:202
  26.5 0.0 collective-permute-done.9.code_ref
  26.5 1.1 %sum.3 = (s16[144,512]{1,0:T(8,128)(2,1)S(1)}, s16[144,512]{1,0:T(8,128)(2,1)S(1)}) custom-call(s32[1,1,2,8]{3,2,1,0:T(2,128)S(1)} %copy-done.1, s32[1,1,2,8]{3,2,1,0:T(2,128)S(1)} %collective-permute-done.one_ref, s32[1,1,2,8]{3,2,1,0:T(2,128)S(1)} %collective-permute-done.1.two_ref, s32[1,1,2,8]{3,2,1,0:T(2,128)S(1)} %collective-permute-done.2.three_ref, ...), custom_call_target="tpu_custom_call" | custom-call | tf_op jit(solution)/shard_map/sum/pallas_call | solution.py:249
  27.6 1.1 %collective-permute-start.10 = (s16[144,512]{1,0:T(8,128)(2,1)S(1)}, s16[144,512]{1,0:T(8,128)(2,1)S(1)}, u32[]{:S(2)}, u32[]{:S(2)}) collective-permute-start(s16[144,512]{1,0:T(8,128)(2,1)S(1)} %get-tuple-element.19), channel_id=1, source_target_pairs={{0,2},{1,5},{2,4},{3,7},{4,6},{5,1},{6,0},{7,3},{8,10},{9,13},{10,... | collective-permute-start | bytes 442376 | tf_op jit(solution)/shard_map/ppermute | solution.py:202
  28.6 4.7 %collective-permute-start.11 = (s16[144,512]{1,0:T(8,128)(2,1)S(1)}, s16[144,512]{1,0:T(8,128)(2,1)S(1)}, u32[]{:S(2)}, u32[]{:S(2)}) collective-permute-start(s16[144,512]{1,0:T(8,128)(2,1)S(1)} %get-tuple-element.20), channel_id=1, source_target_pairs={{0,6},{1,1},{2,0},{3,3},{4,2},{5,5},{6,4},{7,7},{8,14},{9,9},{10,8... | collective-permute-start | bytes 442376 | tf_op jit(solution)/shard_map/ppermute | solution.py:202
  33.3 2.8 %collective-permute-done.7.a_ref = s16[144,512]{1,0:T(8,128)(2,1)S(1)} collective-permute-done((s16[144,512]{1,0:T(8,128)(2,1)S(1)}, s16[144,512]{1,0:T(8,128)(2,1)S(1)}, u32[]{:S(2)}, u32[]{:S(2)}) %collective-permute-start.7) | collective-permute-done | bytes 147488 | tf_op jit(solution)/shard_map/ppermute | solution.py:202
  36.1 0.0 collective-permute-done.8.b_ref
  36.1 0.0 collective-permute-done.10.c_ref
  36.1 2.8 %collective-permute-done.11.d_ref = s16[144,512]{1,0:T(8,128)(2,1)S(1)} collective-permute-done((s16[144,512]{1,0:T(8,128)(2,1)S(1)}, s16[144,512]{1,0:T(8,128)(2,1)S(1)}, u32[]{:S(2)}, u32[]{:S(2)}) %collective-permute-start.11) | collective-permute-done | bytes 147488 | tf_op jit(solution)/shard_map/ppermute | solution.py:202
  38.9 1.0 %last.1 = f32[1,1,2,8,64,64]{5,4,3,2,1,0:T(8,128)} custom-call(s16[144,512]{1,0:T(8,128)(2,1)S(1)} %collective-permute-done.7.a_ref, s16[144,512]{1,0:T(8,128)(2,1)S(1)} %collective-permute-done.8.b_ref, s16[144,512]{1,0:T(8,128)(2,1)S(1)} %collective-permute-done.10.c_ref, s16[144,512]{1,0:T(8,128)(2,1)S(1)} %collective-permute-done.11.d_ref), custom_call_target="tpu_custom_call" | custom-call | tf_op jit(solution)/shard_map/last/pallas_call | solution.py:266
  (1 shorter events, 0.0 us)
Async XLA Ops:
  2.4 10.3 %collective-permute-start.4 = (bf16[144,512]{1,0:T(8,128)(2,1)S(1)}, bf16[144,512]{1,0:T(8,128)(2,1)S(1)}, u32[]{:S(2)}, u32[]{:S(2)}) collective-permute-start(bf16[144,512]{1,0:T(8,128)(2,1)S(1)} %maximum_maximum_fusion.packed_ref), channel_id=1, source_target_pairs={{0,16},{1,17},{2,18},{3,19},{4,20},{5,21},{6,22},{7,23},{8,24},{9,... | collective-permute-start | bytes 442376 | tf_op jit(solution)/shard_map/ppermute | solution.py:202
  6.2 1.4 %copy-start = (bf16[1,1,16,6,64,64]{5,4,3,2,1,0:T(8,128)(2,1)S(1)}, bf16[1,1,16,6,64,64]{5,4,3,2,1,0:T(8,128)(2,1)}, u32[]{:S(2)}) copy-start(bf16[1,1,16,6,64,64]{5,4,3,2,1,0:T(8,128)(2,1)} %right_ref.1) | copy-start | bytes 2359300
  7.6 7.0 %copy-start.1 = (s32[1,1,2,8]{3,2,1,0:T(2,128)S(1)}, s32[1,1,2,8]{3,2,1,0:T(2,128)}, u32[]{:S(2)}) copy-start(s32[1,1,2,8]{3,2,1,0:T(2,128)} %own_ref.3) | copy-start | bytes 196
  11.1 12.6 %collective-permute-start.6 = (s16[144,1024]{1,0:T(8,128)(2,1)S(1)}, s16[144,1024]{1,0:T(8,128)(2,1)S(1)}, u32[]{:S(2)}, u32[]{:S(2)}) collective-permute-start(s16[144,1024]{1,0:T(8,128)(2,1)S(1)} %get-tuple-element.15), channel_id=1, source_target_pairs={{0,1},{1,0},{2,3},{3,2},{4,5},{5,4},{6,7},{7,6},{8,9},{9,8},{10,11... | collective-permute-start | bytes 884744 | tf_op jit(solution)/shard_map/ppermute | solution.py:202
  13.4 13.0 %collective-permute-start.9 = (s16[144,1024]{1,0:T(8,128)(2,1)S(1)}, s16[144,1024]{1,0:T(8,128)(2,1)S(1)}, u32[]{:S(2)}, u32[]{:S(2)}) collective-permute-start(s16[144,1024]{1,0:T(8,128)(2,1)S(1)} %second.1), channel_id=1, source_target_pairs={{0,1},{1,0},{2,3},{3,2},{4,5},{5,4},{6,7},{7,6},{8,9},{9,8},{10,11... | collective-permute-start | bytes 884744 | tf_op jit(solution)/shard_map/ppermute | solution.py:202
  14.0 4.1 %collective-permute-start.3 = (bf16[144,512]{1,0:T(8,128)(2,1)S(1)}, bf16[144,512]{1,0:T(8,128)(2,1)S(1)}, u32[]{:S(2)}, u32[]{:S(2)}) collective-permute-start(bf16[144,512]{1,0:T(8,128)(2,1)S(1)} %maximum_maximum_fusion.packed_ref), channel_id=1, source_target_pairs={{0,8},{1,9},{2,10},{3,11},{4,12},{5,13},{6,14},{7,15},{8,0},{9,1},... | collective-permute-start | bytes 442376 | tf_op jit(solution)/shard_map/ppermute | solution.py:202
  14.1 4.1 %collective-permute-start.5 = (bf16[144,512]{1,0:T(8,128)(2,1)S(1)}, bf16[144,512]{1,0:T(8,128)(2,1)S(1)}, u32[]{:S(2)}, u32[]{:S(2)}) collective-permute-start(bf16[144,512]{1,0:T(8,128)(2,1)S(1)} %collective-permute-done.4.packed_ref), channel_id=1, source_target_pairs={{0,8},{1,9},{2,10},{3,11},{4,12},{5,13},{6,14},{7,15},{8,0},{9,1},... | collective-permute-start | bytes 442376 | tf_op jit(solution)/shard_map/ppermute | solution.py:202
  14.6 6.4 %collective-permute-start = (s32[1,1,2,8]{3,2,1,0:T(2,128)S(1)}, s32[1,1,2,8]{3,2,1,0:T(2,128)S(1)}, u32[]{:S(2)}, u32[]{:S(2)}) collective-permute-start(s32[1,1,2,8]{3,2,1,0:T(2,128)S(1)} %copy-done.1), channel_id=1, source_target_pairs={{0,6},{1,7},{2,0},{3,1},{4,2},{5,3},{6,4},{7,5},{8,14},{9,15},{10,... | collective-permute-start | bytes 200 | tf_op jit(solution)/shard_map/ppermute | solution.py:202
  18.2 4.5 %collective-permute-start.1 = (s32[1,1,2,8]{3,2,1,0:T(2,128)S(1)}, s32[1,1,2,8]{3,2,1,0:T(2,128)S(1)}, u32[]{:S(2)}, u32[]{:S(2)}) collective-permute-start(s32[1,1,2,8]{3,2,1,0:T(2,128)S(1)} %copy-done.1), channel_id=1, source_target_pairs={{0,4},{1,5},{2,6},{3,7},{4,0},{5,1},{6,2},{7,3},{8,12},{9,13},{10,... | collective-permute-start | bytes 200 | tf_op jit(solution)/shard_map/ppermute | solution.py:202
  18.2 5.4 %collective-permute-start.2 = (s32[1,1,2,8]{3,2,1,0:T(2,128)S(1)}, s32[1,1,2,8]{3,2,1,0:T(2,128)S(1)}, u32[]{:S(2)}, u32[]{:S(2)}) collective-permute-start(s32[1,1,2,8]{3,2,1,0:T(2,128)S(1)} %copy-done.1), channel_id=1, source_target_pairs={{0,2},{1,3},{2,4},{3,5},{4,6},{5,7},{6,0},{7,1},{8,10},{9,11},{10,... | collective-permute-start | bytes 200 | tf_op jit(solution)/shard_map/ppermute | solution.py:202
  24.7 11.4 %collective-permute-start.7 = (s16[144,512]{1,0:T(8,128)(2,1)S(1)}, s16[144,512]{1,0:T(8,128)(2,1)S(1)}, u32[]{:S(2)}, u32[]{:S(2)}) collective-permute-start(s16[144,512]{1,0:T(8,128)(2,1)S(1)} %get-tuple-element.16), channel_id=1, source_target_pairs={{0,4},{1,3},{2,6},{3,5},{4,0},{5,7},{6,2},{7,1},{8,12},{9,11},{10,... | collective-permute-start | bytes 442376 | tf_op jit(solution)/shard_map/ppermute | solution.py:202
  25.8 10.3 %collective-permute-start.8 = (s16[144,512]{1,0:T(8,128)(2,1)S(1)}, s16[144,512]{1,0:T(8,128)(2,1)S(1)}, u32[]{:S(2)}, u32[]{:S(2)}) collective-permute-start(s16[144,512]{1,0:T(8,128)(2,1)S(1)} %get-tuple-element.17), channel_id=1, source_target_pairs={{0,0},{1,7},{2,2},{3,1},{4,4},{5,3},{6,6},{7,5},{8,8},{9,15},{10,1... | collective-permute-start | bytes 442376 | tf_op jit(solution)/shard_map/ppermute | solution.py:202
  27.6 8.6 %collective-permute-start.10 = (s16[144,512]{1,0:T(8,128)(2,1)S(1)}, s16[144,512]{1,0:T(8,128)(2,1)S(1)}, u32[]{:S(2)}, u32[]{:S(2)}) collective-permute-start(s16[144,512]{1,0:T(8,128)(2,1)S(1)} %get-tuple-element.19), channel_id=1, source_target_pairs={{0,2},{1,5},{2,4},{3,7},{4,6},{5,1},{6,0},{7,3},{8,10},{9,13},{10,... | collective-permute-start | bytes 442376 | tf_op jit(solution)/shard_map/ppermute | solution.py:202
  28.6 10.3 %collective-permute-start.11 = (s16[144,512]{1,0:T(8,128)(2,1)S(1)}, s16[144,512]{1,0:T(8,128)(2,1)S(1)}, u32[]{:S(2)}, u32[]{:S(2)}) collective-permute-start(s16[144,512]{1,0:T(8,128)(2,1)S(1)} %get-tuple-element.20), channel_id=1, source_target_pairs={{0,6},{1,1},{2,0},{3,3},{4,2},{5,5},{6,4},{7,7},{8,14},{9,9},{10,8... | collective-permute-start | bytes 442376 | tf_op jit(solution)/shard_map/ppermute | solution.py:202

commit v2 on v0

--- a/solution.py
+++ b/solution.py
@@ -1,9 +1,17 @@
+import functools
+
 import jax
 import jax.numpy as jnp
 from jax import lax
+from jax.experimental import pallas as pl
+from jax.experimental.pallas import tpu as pltpu
 from jax.sharding import PartitionSpec as P
 
 TICKS = 8
+LANES = 128
+PAD = 16
+TOP = 32767.0
+GRAIN = 8192.0
 
 
 def shifted(value, axis, steps):
@@ -25,7 +33,7 @@
     return jnp.einsum("iaxy,iaoyz->ioxz", left, chosen, preferred_element_type=jnp.float32)
 
 
-def on_device(left_blocks, left_cols, right_blocks, right_cols, out_cols):
+def ring(left_blocks, left_cols, right_blocks, right_cols, out_cols):
     left = left_blocks[0, 0]
     left_index = left_cols[0, 0]
     right = right_blocks[0, 0]
@@ -41,6 +49,330 @@
     return total[None, None]
 
 
+def encode(parts, code_ref):
+    rows = parts[0].shape[0]
+    row = lax.broadcasted_iota(jnp.int32, (PAD, LANES), 0)
+    scales = jnp.zeros((PAD, LANES), jnp.float32)
+    for m, value in enumerate(parts):
+        peak = jnp.maximum(jnp.max(jnp.abs(value), axis=0, keepdims=True), 2.0**-100)
+        power = jnp.floor(jnp.log2(peak))
+        shrink = jnp.exp2(-power)
+        grains = jnp.ceil(peak * shrink * GRAIN) + 1.0
+        factor = (TOP * GRAIN / grains) * shrink
+        code_ref[m * rows : (m + 1) * rows] = jnp.round(value * factor).astype(jnp.int16)
+        scales = jnp.where(row == m, power, jnp.where(row == PAD // 2 + m, grains, scales))
+    code_ref[len(parts) * rows :] = scales.astype(jnp.int16)
+
+
+def decoded(code_ref, rows):
+    count = code_ref.shape[0] // rows
+    tile = code_ref[count * rows :].astype(jnp.float32)
+    scales = jnp.exp2(tile[: PAD // 2]) * (tile[PAD // 2 :] * (1.0 / (TOP * GRAIN)))
+    for m in range(count):
+        yield code_ref[m * rows : (m + 1) * rows].astype(jnp.float32) * scales[m : m + 1]
+
+
+def spread_left(packed_ref, rows, half, dense_ref):
+    side = lax.broadcasted_iota(jnp.int32, (1, LANES), 1) // half
+    index = packed_ref[rows : rows + PAD, :].astype(jnp.float32)
+    for i in range(rows // half):
+        here, there, data, turned = [], [], [], []
+        for b in range(packed_ref.shape[1] // LANES):
+            lanes = slice(b * LANES, (b + 1) * LANES)
+            column = index[i : i + 1, lanes].astype(jnp.int32)
+            here.append(jnp.broadcast_to(column - side, (PAD, LANES)))
+            there.append(jnp.broadcast_to(pltpu.roll(column, half, 1) - side, (PAD, LANES)))
+            data.append(packed_ref[i * half : (i + 1) * half, lanes])
+            turned.append(pltpu.roll(data[-1], half, 1))
+        for m in range(dense_ref.shape[1] // LANES):
+            masks = [(h == 2 * m, t == 2 * m) for h, t in zip(here, there)]
+            for top in range(0, half, PAD):
+                total = jnp.zeros((PAD, LANES), jnp.bfloat16)
+                for b, (stays, turns) in enumerate(masks):
+                    total = jnp.where(stays, data[b][top : top + PAD], total)
+                    total = jnp.where(turns, turned[b][top : top + PAD], total)
+                rows_of = slice(i * half + top, i * half + top + PAD)
+                dense_ref[rows_of, m * LANES : (m + 1) * LANES] = total
+
+
+def product(left, dense_ref):
+    found = []
+    for m in range(0, dense_ref.shape[0], 2):
+        pair = jnp.concatenate([dense_ref[m], dense_ref[m + 1]], axis=1)
+        part = jnp.dot(left, pair, preferred_element_type=jnp.float32)
+        found += [part[:, :LANES], part[:, LANES:]]
+    return found
+
+
+def place(blocks, dense_ref):
+    half = blocks[0][0].shape[0]
+    side = lax.broadcasted_iota(jnp.int32, (half, LANES), 1) // half
+    work = []
+    for block, row, col in blocks:
+        both = jnp.concatenate([block.astype(jnp.float32)]*2, axis=1).astype(jnp.bfloat16)
+        at = (lax.shift_right_logical(col, 1), slice(row * half, (row + 1) * half))
+        work.append((at, jnp.where(side == (col & 1), both, dense_ref[at])))
+    for at, value in work:
+        dense_ref[at] = value
+
+
+def first_kernel(
+    right_cols_hbm,
+    left_cols_hbm,
+    left_hbm,
+    right_hbm,
+    dense_ref,
+    code_ref,
+    packed_ref,
+    left_ref,
+    right_cols_ref,
+    left_cols_ref,
+    left_raw,
+    right_raw,
+    sem,
+):
+    ib, nl, half, _ = left_raw.shape
+    kb, kept, _, _ = right_raw.shape
+    rows = ib * half
+    parts = sem.shape[0] - 3
+    step = kb // parts
+    pairs = [(left_cols_hbm, left_cols_ref), (left_hbm.at[0, 0], left_raw), (right_cols_hbm, right_cols_ref)]
+    for part in range(parts):
+        here = pl.ds(part * step, step)
+        pairs.append((right_hbm.at[0, 0, here], right_raw.at[here]))
+    copies = [pltpu.make_async_copy(*pair, sem.at[n]) for n, pair in enumerate(pairs)]
+    for copy in copies:
+        copy.start()
+    left_ref[...] = jnp.zeros_like(left_ref)
+    dense_ref[...] = jnp.zeros_like(dense_ref)
+    copies[0].wait()
+    copies[1].wait()
+    side = lax.broadcasted_iota(jnp.int32, (PAD, LANES), 1) // half
+    row = lax.broadcasted_iota(jnp.int32, (PAD, LANES), 0)
+    for b in range(nl // 2):
+        lanes = slice(b * LANES, (b + 1) * LANES)
+        index = jnp.zeros((PAD, LANES), jnp.int32)
+        for i in range(ib):
+            pair = jnp.concatenate([left_raw[i, 2 * b], left_raw[i, 2 * b + 1]], axis=1)
+            packed_ref[i * half : (i + 1) * half, lanes] = pair
+            cols = jnp.where(side == 0, left_cols_ref[0, 0, i, 2 * b], left_cols_ref[0, 0, i, 2 * b + 1])
+            index = jnp.where(row == i, cols, index)
+        packed_ref[rows:, lanes] = index.astype(jnp.float32).astype(jnp.bfloat16)
+    for a in range(nl):
+        place([(left_raw[i, a], i, left_cols_ref[0, 0, i, a]) for i in range(ib)], left_ref)
+    copies[2].wait()
+    for part in range(parts):
+        copies[part + 3].wait()
+        for e in range(kept):
+            ks = range(part * step, (part + 1) * step)
+            place([(right_raw[k, e], k, right_cols_ref[0, e, 0, k]) for k in ks], dense_ref)
+    left = jnp.concatenate([left_ref[m] for m in range(left_ref.shape[0])], axis=1)
+    encode(product(left, dense_ref), code_ref)
+
+
+def second_kernel(half, dense_ref, packed_ref, own_cols_ref, one_cols_ref, *refs):
+    *code_refs, pair_ref, left_ref = refs
+    pair_ref[0] = own_cols_ref[0]
+    pair_ref[1] = one_cols_ref[0]
+    spread_left(packed_ref, left_ref.shape[0], half, left_ref)
+    found = product(left_ref[...], dense_ref)
+    for i, code_ref in enumerate(code_refs):
+        encode([part[i * half : (i + 1) * half] for part in found], code_ref)
+
+
+def swapped():
+    return (lax.axis_index("col") + lax.axis_index("row")) % 2
+
+
+def near_kernel(half, dense_ref, packed_ref, kept_ref, left_ref):
+    spread_left(packed_ref, left_ref.shape[0], half, left_ref)
+    slot = swapped()
+    for m, part in enumerate(product(left_ref[...], dense_ref)):
+        kept_ref[slot, m] = part
+
+
+def far_kernel(half, dense_ref, packed_ref, _, kept_ref, left_ref):
+    spread_left(packed_ref, left_ref.shape[0], half, left_ref)
+    slot = 1 - swapped()
+    for m, part in enumerate(product(left_ref[...], dense_ref)):
+        kept_ref[slot, m] = part
+
+
+def sum_kernel(half, odd, first, own_ref, one_ref, far_ref, kept_ref, code_ref, *refs):
+    pairs = kept_ref.shape[1]
+    rows = (code_ref.shape[0] - PAD) // pairs
+    if odd:
+        held_ref, a_ref, b_ref, keep_ref, wide_ref, new_ref = refs
+        held_refs, new_refs = [held_ref], [new_ref]
+    else:
+        a_ref, *new_refs, wide_ref = refs
+    for m, part in enumerate(decoded(code_ref, rows)):
+        total = kept_ref[odd, m, first * half : first * half + rows] + part
+        wide_ref[m] = total
+        wide_ref[pairs + m] = pltpu.roll(total, half, 1)
+    low = lax.broadcasted_iota(jnp.int32, (half, LANES), 1) < half
+    stays = (lax.axis_index("col") % 2) == odd
+
+    def pick(near, i, o):
+        picked = []
+        for side in range(2):
+            at = (0, first + i, o + side)
+            if near:
+                j = jnp.where(stays, own_ref[(0, *at)], one_ref[(0, *at)])
+            else:
+                j = jnp.where(stays, far_ref[(0, *at)], far_ref[(1, *at)])
+            slot = lax.shift_right_logical(j, 1) + pairs * ((j + side) & 1)
+            picked.append(wide_ref[slot, i * half : (i + 1) * half, :])
+        return jnp.where(low, picked[0], picked[1])
+
+    count = own_ref.shape[3]
+    blocks = range(rows // half)
+    encode([jnp.concatenate([pick(False, i, o) for i in blocks], axis=0) for o in range(0, count, 2)], a_ref)
+    for i, new_ref in zip(blocks, new_refs):
+        encode([pick(True, i, o) for o in range(0, count, 2)], new_ref)
+    if odd:
+        b_ref[...] = jnp.where(stays, held_ref[...], new_ref[...])
+        keep_ref[...] = jnp.where(stays, new_ref[...], held_ref[...])
+
+
+def last_kernel(half, whole_ref, *refs):
+    *part_refs, out_ref = refs
+    ib = out_ref.shape[2]
+    parts = [[decoded(ref, half) for ref in part_refs[i::ib]] for i in range(ib)]
+    for m, whole in enumerate(decoded(whole_ref, ib * half)):
+        for i in range(ib):
+            total = whole[i * half : (i + 1) * half]
+            for part in parts[i]:
+                total = total + next(part)
+            out_ref[0, 0, i, 2 * m] = total[:, :half]
+            out_ref[0, 0, i, 2 * m + 1] = total[:, half:]
+
+
+VMEM = pl.BlockSpec(memory_space=pltpu.VMEM)
+SMEM = pl.BlockSpec(memory_space=pltpu.SMEM)
+HBM = pl.BlockSpec(memory_space=pltpu.HBM)
+PARTS = 4
+PARAMS = pltpu.CompilerParams(vmem_limit_bytes=40 * 2**20)
+
+
+def grid_path(n_row, n_col, left_blocks, left_cols, right_blocks, right_cols, out_cols):
+    _, _, ib, nl, bs, _ = left_blocks.shape
+    kb = right_blocks.shape[2]
+    jb = kb
+    no = out_cols.shape[3]
+    rows = ib * bs
+
+    def send(value, to):
+        pairs = []
+        for r in range(n_row):
+            for c in range(n_col):
+                target = to(r, c)
+                pairs.append((r * n_col + c, target[0] * n_col + target[1]))
+        return lax.ppermute(value, ("row", "col"), pairs)
+
+    def along(even, odd):
+        return lambda r, c: (r, c ^ (2 * (odd if c % 2 else even)))
+
+    wide_cols, no_cols = jb * bs // LANES, no * bs // LANES
+    code = jax.ShapeDtypeStruct((wide_cols * rows + PAD, LANES), jnp.int16)
+    code_part = jax.ShapeDtypeStruct((wide_cols * bs + PAD, LANES), jnp.int16)
+    small = jax.ShapeDtypeStruct((no_cols * rows + PAD, LANES), jnp.int16)
+    small_part = jax.ShapeDtypeStruct((no_cols * bs + PAD, LANES), jnp.int16)
+    both = jax.ShapeDtypeStruct((2, wide_cols, rows, LANES), jnp.float32)
+    left_scratch = pltpu.VMEM((rows, kb * bs), jnp.bfloat16)
+    operands = (right_cols.transpose(0, 3, 1, 2), left_cols, left_blocks, right_blocks)
+    dense, code_one, packed = pl.pallas_call(
+        first_kernel,
+        out_shape=(
+            jax.ShapeDtypeStruct((wide_cols, kb * bs, LANES), jnp.bfloat16),
+            code,
+            jax.ShapeDtypeStruct((rows + PAD, nl * bs), jnp.bfloat16),
+        ),
+        in_specs=[HBM] * 4,
+        out_specs=(VMEM, VMEM, VMEM),
+        scratch_shapes=[
+            pltpu.VMEM((kb * bs // LANES, rows, LANES), jnp.bfloat16),
+            pltpu.SMEM((1, right_cols.shape[3], 1, kb), jnp.int32),
+            pltpu.SMEM(left_cols.shape[:2] + (ib, nl), jnp.int32),
+            pltpu.VMEM(left_blocks.shape[2:], jnp.bfloat16),
+            pltpu.VMEM(right_blocks.shape[2:], jnp.bfloat16),
+            pltpu.SemaphoreType.DMA((PARTS + 3,)),
+        ],
+        compiler_params=PARAMS,
+        name="first",
+    )(*(pltpu.with_memory_space_constraint(a, pltpu.HBM) for a in operands))
+    got_one = send(code_one, lambda r, c: (r, c ^ 1))
+    across = send(packed, lambda r, c: ((r + 2) % n_row, c))
+    near = send(packed, lambda r, c: (r ^ 1, c))
+    kept = pl.pallas_call(
+        functools.partial(near_kernel, bs),
+        out_shape=both,
+        in_specs=[VMEM, VMEM],
+        out_specs=VMEM,
+        scratch_shapes=[left_scratch],
+        compiler_params=PARAMS,
+        name="near",
+    )(dense, near)
+    kept, own_cols = lax.optimization_barrier((kept, out_cols))
+    one_cols = send(own_cols, along(1, 1))
+    across, kept, one_cols = lax.optimization_barrier((across, kept, one_cols))
+    far = send(across, lambda r, c: (r ^ 1, c))
+    *codes, pair_cols = pl.pallas_call(
+        functools.partial(second_kernel, bs),
+        out_shape=(*(ib * (code_part,)), jax.ShapeDtypeStruct((2, *out_cols.shape[1:]), jnp.int32)),
+        in_specs=[VMEM] * 4,
+        out_specs=(ib + 1) * (VMEM,),
+        scratch_shapes=[left_scratch],
+        compiler_params=PARAMS,
+        name="second",
+    )(dense, across, own_cols, one_cols)
+    got_two = [send(code, lambda r, c: (r, c ^ 1)) for code in codes]
+    far_cols = send(pair_cols, along(2, 2))
+    kept = pl.pallas_call(
+        functools.partial(far_kernel, bs),
+        out_shape=both,
+        in_specs=[VMEM, VMEM, HBM],
+        out_specs=VMEM,
+        scratch_shapes=[left_scratch],
+        input_output_aliases={2: 0},
+        compiler_params=PARAMS,
+        name="far",
+    )(dense, far, kept)
+
+    def summed(odd, first, code, *held):
+        if odd:
+            outs = 3 * (small_part,)
+        else:
+            outs = (small, *(ib * (small_part,)))
+        scratch = [pltpu.VMEM((2 * wide_cols, rows if not odd else bs, LANES), jnp.float32)]
+        scratch += odd * [pltpu.VMEM(small_part.shape, small_part.dtype)]
+        return pl.pallas_call(
+            functools.partial(sum_kernel, bs, odd, first),
+            out_shape=outs,
+            in_specs=[SMEM] * 3 + [VMEM] * (2 + odd),
+            out_specs=len(outs) * (VMEM,),
+            scratch_shapes=scratch,
+            compiler_params=PARAMS,
+            name="sum",
+        )(own_cols, one_cols, far_cols, kept, code, *held)
+
+    a, *held = summed(0, 0, got_one)
+    whole = send(a, along(2, 3))
+    parts = []
+    for i in range(ib):
+        a, b, keep = summed(1, i, got_two[i], held[i])
+        parts.append((send(a, along(3, 2)), send(b, along(1, 1)), keep))
+    got = [whole, *(part for group in zip(*parts) for part in group)]
+    return pl.pallas_call(
+        functools.partial(last_kernel, bs),
+        out_shape=jax.ShapeDtypeStruct((1, 1, ib, no, bs, bs), jnp.float32),
+        in_specs=[VMEM] * len(got),
+        out_specs=VMEM,
+        compiler_params=PARAMS,
+        name="last",
+    )(*got)
+
+
 def solution(mesh):
     in_specs = (
         P("row", "col", None, None, None, None),
@@ -50,6 +382,6 @@
         P("row", "col", None, None),
     )
     out_specs = P("row", "col", None, None, None, None)
-    return jax.shard_map(
-        on_device, mesh=mesh, in_specs=in_specs, out_specs=out_specs, check_vma=False
-    )
+    n_row, n_col = mesh.shape["row"], mesh.shape["col"]
+    body = functools.partial(grid_path, n_row, n_col) if (n_row, n_col) == (4, TICKS) else ring
+    return jax.shard_map(body, mesh=mesh, in_specs=in_specs, out_specs=out_specs, check_vma=False)

time: 182 us -> 35.1 us (0.19)
  waiting for transfers between devices: 77.7 us -> 7.31 us
  local copies, waits for them, and re-layouts: 44.8 us -> 0.01 us
  matrix products: 40.9 us -> 0 us
  starting transfers between devices: 5.71 us -> 18.7 us
  other arithmetic: 11.6 us -> 0 us
  Pallas kernels: 0 us -> 8.85 us
    ppermute x29 -> x13, waiting for transfers between devices: 77.7 us -> 7.31 us  [send(): return lax.ppermute(value, ('row', 'col'), pairs)]
    dot_general x16 -> x0, matrix products: 40.9 us -> none  [the longest x8 22.6 us: one_tick(): jnp.einsum('iaokb,kbyz->iaoyz', select, right, preferred_element_type=jnp...]
    dot_general x8 -> x0, local copies, waits for them, and re-layouts: 33.2 us -> none  [one_tick(): jnp.einsum('iaokb,kbyz->iaoyz', select, right, preferred_element_type=jnp...]
    ppermute x29 -> x13, starting transfers between devices: 5.71 us -> 18.7 us  [send(): return lax.ppermute(value, ('row', 'col'), pairs)]
    convert_element_type x8 -> x0, local copies, waits for them, and re-layouts: 9.43 us -> none  [one_tick(): select = jnp.einsum('iak,iokb->iaokb', pick_row, match).astype(jnp.bfloat16)]
    pallas_call x0 -> x8, Pallas kernels: none -> 8.85 us  [the longest x3 2.76 us: summed(): pl.pallas_call(functools.partial(sum_kernel, bs, odd, first), out_shape=o...]
    convert_element_type x8 -> x0, other arithmetic: 6.27 us -> none  [one_tick(): select = jnp.einsum('iak,iokb->iaokb', pick_row, match).astype(jnp.bfloat16)]
    another operation x9 -> x0, other arithmetic: 5.3 us -> none
  transfers between devices with their start and end apart: 29 -> 13, of which waited for: 18 -> 7; matrix products, arithmetic and copies ran while one was open for 46% -> 0% of each run, Pallas kernels for 0% -> 15%
where the time goes in v2:
time: 35.1 us; the launch traced here: 34.9 us
  starting transfers between devices  18.7 us (53%)
  Pallas kernels  8.85 us (25%)
  waiting for transfers between devices  7.31 us (21%)
    ppermute x13, starting transfers between devices, send(): return lax.ppermute(value, ('row', 'col'), pairs)  18.7 us
    ppermute x13, waiting for transfers between devices, send(): return lax.ppermute(value, ('row', 'col'), pairs)  7.31 us
    pallas_call x3, Pallas kernels, summed(): pl.pallas_call(functools.partial(sum_kernel, bs, odd, first), out_shape=o...  2.76 us
    pallas_call x1, Pallas kernels, grid_path(): pl.pallas_call(first_kernel, out_shape=(jax.ShapeDtypeStruct((wide_cols,...  2.66 us
    pallas_call x1, Pallas kernels, grid_path(): pl.pallas_call(functools.partial(last_kernel, bs), out_shape=jax.ShapeDty...  1 us
    pallas_call x1, Pallas kernels, grid_path(): pl.pallas_call(functools.partial(second_kernel, bs), out_shape=(*ib * (co...  0.88 us
    pallas_call x1, Pallas kernels, grid_path(): pl.pallas_call(functools.partial(near_kernel, bs), out_shape=both, in_spe...  0.77 us
    pallas_call x1, Pallas kernels, grid_path(): pl.pallas_call(functools.partial(far_kernel, bs), out_shape=both, in_spec...  0.77 us
  transfers between devices with their start and end apart: 13, of which 7 were waited for; matrix products, arithmetic and copies ran while one was open for 0% of the time, Pallas kernels for 15%

profile of v2, /device:TPU:0, one launch (start us, length us, event | category | flops | bytes accessed | tf_op | source)
XLA Modules:
  0.0 34.9 jit_solution(2673709331616453745)
XLA Ops:
  0.0 2.7 %first.1 = (bf16[8,1024,128]{2,1,0:T(8,128)(2,1)S(1)}, s16[1040,128]{1,0:T(8,128)(2,1)S(1)}, bf16[144,512]{1,0:T(8,128)(2,1)S(1)}) custom-call(s32[1,6,1,16]{3,2,1,0:T(1,128)} %bitcast.1, s32[1,1,2,8]{3,2,1,0:T(2,128)} %left_cols_hbm.1, bf16[1,1,2,8,64,64]{5,4,3,2,1,0:T(8,128)(2,1)} %left_hbm.1, bf16[1,1,16,6,64,64]{5,4,3,2,1,0:T(8,128)(2,1)} %right_hbm.1), custom_call_target="tpu_custom_call" | custom-call | tf_op jit(solution)/shard_map/first/pallas_call | solution.py:284
  2.7 0.0 copy-start
  2.7 0.5 %collective-permute-start = (bf16[144,512]{1,0:T(8,128)(2,1)S(1)}, bf16[144,512]{1,0:T(8,128)(2,1)S(1)}, u32[]{:S(2)}, u32[]{:S(2)}) collective-permute-start(bf16[144,512]{1,0:T(8,128)(2,1)S(1)} %get-tuple-element.26), channel_id=1, source_target_pairs={{0,8},{1,9},{2,10},{3,11},{4,12},{5,13},{6,14},{7,15},{8,0},{9,1},... | collective-permute-start | bytes 442376 | tf_op jit(solution)/shard_map/ppermute | solution.py:271
  3.2 2.6 %collective-permute-start.1 = (bf16[144,512]{1,0:T(8,128)(2,1)S(1)}, bf16[144,512]{1,0:T(8,128)(2,1)S(1)}, u32[]{:S(2)}, u32[]{:S(2)}) collective-permute-start(bf16[144,512]{1,0:T(8,128)(2,1)S(1)} %get-tuple-element.26), channel_id=1, source_target_pairs={{0,16},{1,17},{2,18},{3,19},{4,20},{5,21},{6,22},{7,23},{8,24},{9,... | collective-permute-start | bytes 442376 | tf_op jit(solution)/shard_map/ppermute | solution.py:271
  5.8 1.5 %collective-permute-start.5 = (s16[1040,128]{1,0:T(8,128)(2,1)S(1)}, s16[1040,128]{1,0:T(8,128)(2,1)S(1)}, u32[]{:S(2)}, u32[]{:S(2)}) collective-permute-start(s16[1040,128]{1,0:T(8,128)(2,1)S(1)} %get-tuple-element.33), channel_id=1, source_target_pairs={{0,1},{1,0},{2,3},{3,2},{4,5},{5,4},{6,7},{7,6},{8,9},{9,8},{10,11... | collective-permute-start | bytes 798728 | tf_op jit(solution)/shard_map/ppermute | solution.py:271
  7.3 0.0 collective-permute-done.packed_ref
  7.3 0.8 %near.1._ = f32[2,8,128,128]{3,2,1,0:T(8,128)S(1)} custom-call(bf16[8,1024,128]{2,1,0:T(8,128)(2,1)S(1)} %get-tuple-element.25.dense_ref, bf16[144,512]{1,0:T(8,128)(2,1)S(1)} %collective-permute-done.packed_ref), custom_call_target="tpu_custom_call" | custom-call | tf_op jit(solution)/shard_map/near/pallas_call | solution.py:307
  8.1 0.0 copy-done
  8.1 1.6 %collective-permute-start.2 = (s32[1,1,2,8]{3,2,1,0:T(2,128)S(1)}, s32[1,1,2,8]{3,2,1,0:T(2,128)S(1)}, u32[]{:S(2)}, u32[]{:S(2)}) collective-permute-start(s32[1,1,2,8]{3,2,1,0:T(2,128)S(1)} %copy-done), channel_id=1, source_target_pairs={{0,2},{1,3},{2,0},{3,1},{4,6},{5,7},{6,4},{7,5},{8,10},{9,11},{10,... | collective-permute-start | bytes 200 | tf_op jit(solution)/shard_map/ppermute | solution.py:271
  9.7 0.5 %collective-permute-done.1.packed_ref = bf16[144,512]{1,0:T(8,128)(2,1)S(1)} collective-permute-done((bf16[144,512]{1,0:T(8,128)(2,1)S(1)}, bf16[144,512]{1,0:T(8,128)(2,1)S(1)}, u32[]{:S(2)}, u32[]{:S(2)}) %collective-permute-start.1) | collective-permute-done | bytes 147488 | tf_op jit(solution)/shard_map/ppermute | solution.py:271
  10.2 1.5 %collective-permute-done.2.one_cols_ref.one_ref = s32[1,1,2,8]{3,2,1,0:T(2,128)S(1)} collective-permute-done((s32[1,1,2,8]{3,2,1,0:T(2,128)S(1)}, s32[1,1,2,8]{3,2,1,0:T(2,128)S(1)}, u32[]{:S(2)}, u32[]{:S(2)}) %collective-permute-start.2) | collective-permute-done | bytes 96 | tf_op jit(solution)/shard_map/ppermute | solution.py:271
  11.7 0.0 collective-permute-start.4
  11.7 0.9 %second.1 = (s16[528,128]{1,0:T(8,128)(2,1)S(1)}, s16[528,128]{1,0:T(8,128)(2,1)S(1)}, s32[2,1,2,8]{3,2,1,0:T(2,128)S(1)}) custom-call(bf16[8,1024,128]{2,1,0:T(8,128)(2,1)S(1)} %get-tuple-element.25.dense_ref, bf16[144,512]{1,0:T(8,128)(2,1)S(1)} %collective-permute-done.1.packed_ref, s32[1,1,2,8]{3,2,1,0:T(2,128)S(1)} %copy-done, ...), custom_call_target="tpu_custom_call" | custom-call | tf_op jit(solution)/shard_map/second/pallas_call | solution.py:320
  12.6 0.6 %collective-permute-start.7 = (s16[528,128]{1,0:T(8,128)(2,1)S(1)}, s16[528,128]{1,0:T(8,128)(2,1)S(1)}, u32[]{:S(2)}, u32[]{:S(2)}) collective-permute-start(s16[528,128]{1,0:T(8,128)(2,1)S(1)} %get-tuple-element.35), channel_id=1, source_target_pairs={{0,1},{1,0},{2,3},{3,2},{4,5},{5,4},{6,7},{7,6},{8,9},{9,8},{10,11... | collective-permute-start | bytes 405512 | tf_op jit(solution)/shard_map/ppermute | solution.py:271
  13.2 1.5 %collective-permute-start.9 = (s16[528,128]{1,0:T(8,128)(2,1)S(1)}, s16[528,128]{1,0:T(8,128)(2,1)S(1)}, u32[]{:S(2)}, u32[]{:S(2)}) collective-permute-start(s16[528,128]{1,0:T(8,128)(2,1)S(1)} %get-tuple-element.38), channel_id=1, source_target_pairs={{0,1},{1,0},{2,3},{3,2},{4,5},{5,4},{6,7},{7,6},{8,9},{9,8},{10,11... | collective-permute-start | bytes 405512 | tf_op jit(solution)/shard_map/ppermute | solution.py:271
  14.7 2.6 %collective-permute-start.3 = (s32[2,1,2,8]{3,2,1,0:T(2,128)S(1)}, s32[2,1,2,8]{3,2,1,0:T(2,128)S(1)}, u32[]{:S(2)}, u32[]{:S(2)}) collective-permute-start(s32[2,1,2,8]{3,2,1,0:T(2,128)S(1)} %get-tuple-element.31), channel_id=1, source_target_pairs={{0,4},{1,5},{2,6},{3,7},{4,0},{5,1},{6,2},{7,3},{8,12},{9,13},{10,... | collective-permute-start | bytes 392 | tf_op jit(solution)/shard_map/ppermute | solution.py:271
  17.3 0.0 collective-permute-done.4.packed_ref
  17.3 0.8 %far.1.kept_ref = f32[2,8,128,128]{3,2,1,0:T(8,128)S(1)} custom-call(bf16[8,1024,128]{2,1,0:T(8,128)(2,1)S(1)} %get-tuple-element.25.dense_ref, bf16[144,512]{1,0:T(8,128)(2,1)S(1)} %collective-permute-done.4.packed_ref, f32[2,8,128,128]{3,2,1,0:T(8,128)S(1)} %near.1._), custom_call_target="tpu_custom_call", output_to_operand_aliasing={{}: (2, {})} | custom-call | tf_op jit(solution)/shard_map/far/pallas_call | solution.py:331
  18.1 1.1 %collective-permute-done.3.far_ref = s32[2,1,2,8]{3,2,1,0:T(2,128)S(1)} collective-permute-done((s32[2,1,2,8]{3,2,1,0:T(2,128)S(1)}, s32[2,1,2,8]{3,2,1,0:T(2,128)S(1)}, u32[]{:S(2)}, u32[]{:S(2)}) %collective-permute-start.3) | collective-permute-done | bytes 160 | tf_op jit(solution)/shard_map/ppermute | solution.py:271
  19.2 0.0 collective-permute-done.5.code_ref
  19.2 1.0 %sum.3 = (s16[528,128]{1,0:T(8,128)(2,1)S(1)}, s16[272,128]{1,0:T(8,128)(2,1)S(1)}, s16[272,128]{1,0:T(8,128)(2,1)S(1)}) custom-call(s32[1,1,2,8]{3,2,1,0:T(2,128)S(1)} %copy-done, s32[1,1,2,8]{3,2,1,0:T(2,128)S(1)} %collective-permute-done.2.one_cols_ref.one_ref, s32[2,1,2,8]{3,2,1,0:T(2,128)S(1)} %collective-permute-done.3.far_ref, ...), custom_call_target="tpu_custom_call" | custom-call | tf_op jit(solution)/shard_map/sum/pallas_call | solution.py:349
  20.2 2.6 %collective-permute-start.6 = (s16[528,128]{1,0:T(8,128)(2,1)S(1)}, s16[528,128]{1,0:T(8,128)(2,1)S(1)}, u32[]{:S(2)}, u32[]{:S(2)}) collective-permute-start(s16[528,128]{1,0:T(8,128)(2,1)S(1)} %get-tuple-element.34), channel_id=1, source_target_pairs={{0,4},{1,7},{2,6},{3,5},{4,0},{5,3},{6,2},{7,1},{8,12},{9,15},{10,... | collective-permute-start | bytes 405512 | tf_op jit(solution)/shard_map/ppermute | solution.py:271
  22.9 0.0 collective-permute-done.7.code_ref
  22.9 0.9 %sum.4 = (s16[272,128]{1,0:T(8,128)(2,1)S(1)}, s16[272,128]{1,0:T(8,128)(2,1)S(1)}, s16[272,128]{1,0:T(8,128)(2,1)S(1)}) custom-call(s32[1,1,2,8]{3,2,1,0:T(2,128)S(1)} %copy-done, s32[1,1,2,8]{3,2,1,0:T(2,128)S(1)} %collective-permute-done.2.one_cols_ref.one_ref, s32[2,1,2,8]{3,2,1,0:T(2,128)S(1)} %collective-permute-done.3.far_ref, ...), custom_call_target="tpu_custom_call" | custom-call | tf_op jit(solution)/shard_map/sum/pallas_call | solution.py:349
  23.7 1.4 %collective-permute-start.8 = (s16[272,128]{1,0:T(8,128)(2,1)S(1)}, s16[272,128]{1,0:T(8,128)(2,1)S(1)}, u32[]{:S(2)}, u32[]{:S(2)}) collective-permute-start(s16[272,128]{1,0:T(8,128)(2,1)S(1)} %get-tuple-element.37), channel_id=1, source_target_pairs={{0,6},{1,5},{2,4},{3,7},{4,2},{5,1},{6,0},{7,3},{8,14},{9,13},{10,... | collective-permute-start | bytes 208904 | tf_op jit(solution)/shard_map/ppermute | solution.py:271
  25.2 0.3 collective-permute-start.11
  25.5 0.0 collective-permute-done.9.code_ref
  25.5 0.9 %sum.5 = (s16[272,128]{1,0:T(8,128)(2,1)S(1)}, s16[272,128]{1,0:T(8,128)(2,1)S(1)}, s16[272,128]{1,0:T(8,128)(2,1)S(1)}) custom-call(s32[1,1,2,8]{3,2,1,0:T(2,128)S(1)} %copy-done, s32[1,1,2,8]{3,2,1,0:T(2,128)S(1)} %collective-permute-done.2.one_cols_ref.one_ref, s32[2,1,2,8]{3,2,1,0:T(2,128)S(1)} %collective-permute-done.3.far_ref, ...), custom_call_target="tpu_custom_call" | custom-call | tf_op jit(solution)/shard_map/sum/pallas_call | solution.py:349
  26.3 2.9 %collective-permute-start.10 = (s16[272,128]{1,0:T(8,128)(2,1)S(1)}, s16[272,128]{1,0:T(8,128)(2,1)S(1)}, u32[]{:S(2)}, u32[]{:S(2)}) collective-permute-start(s16[272,128]{1,0:T(8,128)(2,1)S(1)} %get-tuple-element.40), channel_id=1, source_target_pairs={{0,6},{1,5},{2,4},{3,7},{4,2},{5,1},{6,0},{7,3},{8,14},{9,13},{10,... | collective-permute-start | bytes 208904 | tf_op jit(solution)/shard_map/ppermute | solution.py:271
  29.3 0.5 %collective-permute-start.12 = (s16[272,128]{1,0:T(8,128)(2,1)S(1)}, s16[272,128]{1,0:T(8,128)(2,1)S(1)}, u32[]{:S(2)}, u32[]{:S(2)}) collective-permute-start(s16[272,128]{1,0:T(8,128)(2,1)S(1)} %get-tuple-element.42), channel_id=1, source_target_pairs={{0,2},{1,3},{2,0},{3,1},{4,6},{5,7},{6,4},{7,5},{8,10},{9,11},{10,... | collective-permute-start | bytes 208904 | tf_op jit(solution)/shard_map/ppermute | solution.py:271
  29.7 1.0 %collective-permute-done.8.refs_0_ = s16[272,128]{1,0:T(8,128)(2,1)S(1)} collective-permute-done((s16[272,128]{1,0:T(8,128)(2,1)S(1)}, s16[272,128]{1,0:T(8,128)(2,1)S(1)}, u32[]{:S(2)}, u32[]{:S(2)}) %collective-permute-start.8) | collective-permute-done | bytes 69664 | tf_op jit(solution)/shard_map/ppermute | solution.py:271
  30.7 1.4 %collective-permute-done.11.refs_2_ = s16[272,128]{1,0:T(8,128)(2,1)S(1)} collective-permute-done((s16[272,128]{1,0:T(8,128)(2,1)S(1)}, s16[272,128]{1,0:T(8,128)(2,1)S(1)}, u32[]{:S(2)}, u32[]{:S(2)}) %collective-permute-start.11) | collective-permute-done | bytes 69664 | tf_op jit(solution)/shard_map/ppermute | solution.py:271
  32.2 0.8 %collective-permute-done.10.refs_1_ = s16[272,128]{1,0:T(8,128)(2,1)S(1)} collective-permute-done((s16[272,128]{1,0:T(8,128)(2,1)S(1)}, s16[272,128]{1,0:T(8,128)(2,1)S(1)}, u32[]{:S(2)}, u32[]{:S(2)}) %collective-permute-start.10) | collective-permute-done | bytes 69664 | tf_op jit(solution)/shard_map/ppermute | solution.py:271
  33.0 0.9 %collective-permute-done.12.refs_3_ = s16[272,128]{1,0:T(8,128)(2,1)S(1)} collective-permute-done((s16[272,128]{1,0:T(8,128)(2,1)S(1)}, s16[272,128]{1,0:T(8,128)(2,1)S(1)}, u32[]{:S(2)}, u32[]{:S(2)}) %collective-permute-start.12) | collective-permute-done | bytes 69664 | tf_op jit(solution)/shard_map/ppermute | solution.py:271
  33.9 0.0 collective-permute-done.6.whole_ref
  33.9 1.0 %last.1 = f32[1,1,2,8,64,64]{5,4,3,2,1,0:T(8,128)} custom-call(s16[528,128]{1,0:T(8,128)(2,1)S(1)} %collective-permute-done.6.whole_ref, s16[272,128]{1,0:T(8,128)(2,1)S(1)} %collective-permute-done.8.refs_0_, s16[272,128]{1,0:T(8,128)(2,1)S(1)} %collective-permute-done.10.refs_1_, s16[272,128]{1,0:T(8,128)(2,1)S(1)} %collective-permute-done.11.refs_2_, ...), custom_call_target="tpu_custom_call" | custom-call | tf_op jit(solution)/shard_map/last/pallas_call | solution.py:366
Async XLA Ops:
  2.7 5.4 %copy-start = (s32[1,1,2,8]{3,2,1,0:T(2,128)S(1)}, s32[1,1,2,8]{3,2,1,0:T(2,128)}, u32[]{:S(2)}) copy-start(s32[1,1,2,8]{3,2,1,0:T(2,128)} %own_ref.2) | copy-start | bytes 196
  2.7 4.6 %collective-permute-start = (bf16[144,512]{1,0:T(8,128)(2,1)S(1)}, bf16[144,512]{1,0:T(8,128)(2,1)S(1)}, u32[]{:S(2)}, u32[]{:S(2)}) collective-permute-start(bf16[144,512]{1,0:T(8,128)(2,1)S(1)} %get-tuple-element.26), channel_id=1, source_target_pairs={{0,8},{1,9},{2,10},{3,11},{4,12},{5,13},{6,14},{7,15},{8,0},{9,1},... | collective-permute-start | bytes 442376 | tf_op jit(solution)/shard_map/ppermute | solution.py:271
  3.2 7.0 %collective-permute-start.1 = (bf16[144,512]{1,0:T(8,128)(2,1)S(1)}, bf16[144,512]{1,0:T(8,128)(2,1)S(1)}, u32[]{:S(2)}, u32[]{:S(2)}) collective-permute-start(bf16[144,512]{1,0:T(8,128)(2,1)S(1)} %get-tuple-element.26), channel_id=1, source_target_pairs={{0,16},{1,17},{2,18},{3,19},{4,20},{5,21},{6,22},{7,23},{8,24},{9,... | collective-permute-start | bytes 442376 | tf_op jit(solution)/shard_map/ppermute | solution.py:271
  5.8 13.4 %collective-permute-start.5 = (s16[1040,128]{1,0:T(8,128)(2,1)S(1)}, s16[1040,128]{1,0:T(8,128)(2,1)S(1)}, u32[]{:S(2)}, u32[]{:S(2)}) collective-permute-start(s16[1040,128]{1,0:T(8,128)(2,1)S(1)} %get-tuple-element.33), channel_id=1, source_target_pairs={{0,1},{1,0},{2,3},{3,2},{4,5},{5,4},{6,7},{7,6},{8,9},{9,8},{10,11... | collective-permute-start | bytes 798728 | tf_op jit(solution)/shard_map/ppermute | solution.py:271
  8.1 3.6 %collective-permute-start.2 = (s32[1,1,2,8]{3,2,1,0:T(2,128)S(1)}, s32[1,1,2,8]{3,2,1,0:T(2,128)S(1)}, u32[]{:S(2)}, u32[]{:S(2)}) collective-permute-start(s32[1,1,2,8]{3,2,1,0:T(2,128)S(1)} %copy-done), channel_id=1, source_target_pairs={{0,2},{1,3},{2,0},{3,1},{4,6},{5,7},{6,4},{7,5},{8,10},{9,11},{10,... | collective-permute-start | bytes 200 | tf_op jit(solution)/shard_map/ppermute | solution.py:271
  11.7 5.6 %collective-permute-start.4 = (bf16[144,512]{1,0:T(8,128)(2,1)S(1)}, bf16[144,512]{1,0:T(8,128)(2,1)S(1)}, u32[]{:S(2)}, u32[]{:S(2)}) collective-permute-start(bf16[144,512]{1,0:T(8,128)(2,1)S(1)} %collective-permute-done.1.packed_ref), channel_id=1, source_target_pairs={{0,8},{1,9},{2,10},{3,11},{4,12},{5,13},{6,14},{7,15},{8,0},{9,1},... | collective-permute-start | bytes 442376 | tf_op jit(solution)/shard_map/ppermute | solution.py:271
  12.6 10.3 %collective-permute-start.7 = (s16[528,128]{1,0:T(8,128)(2,1)S(1)}, s16[528,128]{1,0:T(8,128)(2,1)S(1)}, u32[]{:S(2)}, u32[]{:S(2)}) collective-permute-start(s16[528,128]{1,0:T(8,128)(2,1)S(1)} %get-tuple-element.35), channel_id=1, source_target_pairs={{0,1},{1,0},{2,3},{3,2},{4,5},{5,4},{6,7},{7,6},{8,9},{9,8},{10,11... | collective-permute-start | bytes 405512 | tf_op jit(solution)/shard_map/ppermute | solution.py:271
  13.2 12.2 %collective-permute-start.9 = (s16[528,128]{1,0:T(8,128)(2,1)S(1)}, s16[528,128]{1,0:T(8,128)(2,1)S(1)}, u32[]{:S(2)}, u32[]{:S(2)}) collective-permute-start(s16[528,128]{1,0:T(8,128)(2,1)S(1)} %get-tuple-element.38), channel_id=1, source_target_pairs={{0,1},{1,0},{2,3},{3,2},{4,5},{5,4},{6,7},{7,6},{8,9},{9,8},{10,11... | collective-permute-start | bytes 405512 | tf_op jit(solution)/shard_map/ppermute | solution.py:271
  14.7 4.5 %collective-permute-start.3 = (s32[2,1,2,8]{3,2,1,0:T(2,128)S(1)}, s32[2,1,2,8]{3,2,1,0:T(2,128)S(1)}, u32[]{:S(2)}, u32[]{:S(2)}) collective-permute-start(s32[2,1,2,8]{3,2,1,0:T(2,128)S(1)} %get-tuple-element.31), channel_id=1, source_target_pairs={{0,4},{1,5},{2,6},{3,7},{4,0},{5,1},{6,2},{7,3},{8,12},{9,13},{10,... | collective-permute-start | bytes 392 | tf_op jit(solution)/shard_map/ppermute | solution.py:271
  20.2 13.7 %collective-permute-start.6 = (s16[528,128]{1,0:T(8,128)(2,1)S(1)}, s16[528,128]{1,0:T(8,128)(2,1)S(1)}, u32[]{:S(2)}, u32[]{:S(2)}) collective-permute-start(s16[528,128]{1,0:T(8,128)(2,1)S(1)} %get-tuple-element.34), channel_id=1, source_target_pairs={{0,4},{1,7},{2,6},{3,5},{4,0},{5,3},{6,2},{7,1},{8,12},{9,15},{10,... | collective-permute-start | bytes 405512 | tf_op jit(solution)/shard_map/ppermute | solution.py:271
  23.7 7.0 %collective-permute-start.8 = (s16[272,128]{1,0:T(8,128)(2,1)S(1)}, s16[272,128]{1,0:T(8,128)(2,1)S(1)}, u32[]{:S(2)}, u32[]{:S(2)}) collective-permute-start(s16[272,128]{1,0:T(8,128)(2,1)S(1)} %get-tuple-element.37), channel_id=1, source_target_pairs={{0,6},{1,5},{2,4},{3,7},{4,2},{5,1},{6,0},{7,3},{8,14},{9,13},{10,... | collective-permute-start | bytes 208904 | tf_op jit(solution)/shard_map/ppermute | solution.py:271
  25.2 7.0 %collective-permute-start.11 = (s16[272,128]{1,0:T(8,128)(2,1)S(1)}, s16[272,128]{1,0:T(8,128)(2,1)S(1)}, u32[]{:S(2)}, u32[]{:S(2)}) collective-permute-start(s16[272,128]{1,0:T(8,128)(2,1)S(1)} %get-tuple-element.41), channel_id=1, source_target_pairs={{0,2},{1,3},{2,0},{3,1},{4,6},{5,7},{6,4},{7,5},{8,10},{9,11},{10,... | collective-permute-start | bytes 208904 | tf_op jit(solution)/shard_map/ppermute | solution.py:271
  26.3 6.6 %collective-permute-start.10 = (s16[272,128]{1,0:T(8,128)(2,1)S(1)}, s16[272,128]{1,0:T(8,128)(2,1)S(1)}, u32[]{:S(2)}, u32[]{:S(2)}) collective-permute-start(s16[272,128]{1,0:T(8,128)(2,1)S(1)} %get-tuple-element.40), channel_id=1, source_target_pairs={{0,6},{1,5},{2,4},{3,7},{4,2},{5,1},{6,0},{7,3},{8,14},{9,13},{10,... | collective-permute-start | bytes 208904 | tf_op jit(solution)/shard_map/ppermute | solution.py:271
  29.3 4.6 %collective-permute-start.12 = (s16[272,128]{1,0:T(8,128)(2,1)S(1)}, s16[272,128]{1,0:T(8,128)(2,1)S(1)}, u32[]{:S(2)}, u32[]{:S(2)}) collective-permute-start(s16[272,128]{1,0:T(8,128)(2,1)S(1)} %get-tuple-element.42), channel_id=1, source_target_pairs={{0,2},{1,3},{2,0},{3,1},{4,6},{5,7},{6,4},{7,5},{8,10},{9,11},{10,... | collective-permute-start | bytes 208904 | tf_op jit(solution)/shard_map/ppermute | solution.py:271

commit v3 on v2

--- a/solution.py
+++ b/solution.py
@@ -116,68 +116,57 @@
         dense_ref[at] = value
 
 
-def first_kernel(
-    right_cols_hbm,
-    left_cols_hbm,
-    left_hbm,
-    right_hbm,
-    dense_ref,
-    code_ref,
-    packed_ref,
-    left_ref,
-    right_cols_ref,
-    left_cols_ref,
-    left_raw,
-    right_raw,
-    sem,
-):
-    ib, nl, half, _ = left_raw.shape
-    kb, kept, _, _ = right_raw.shape
+def pack_kernel(cols_hbm, left_hbm, packed_ref, cols_ref, left_ref, sem):
+    ib, nl, half, _ = left_ref.shape
     rows = ib * half
-    parts = sem.shape[0] - 3
+    copies = [
+        pltpu.make_async_copy(cols_hbm, cols_ref, sem.at[0]),
+        pltpu.make_async_copy(left_hbm.at[0, 0], left_ref, sem.at[1]),
+    ]
+    for copy in copies:
+        copy.start()
+    side = lax.broadcasted_iota(jnp.int32, (PAD, LANES), 1) // half
+    row = lax.broadcasted_iota(jnp.int32, (PAD, LANES), 0)
+    copies[0].wait()
+    for b in range(nl // 2):
+        index = jnp.zeros((PAD, LANES), jnp.int32)
+        for i in range(ib):
+            cols = jnp.where(side == 0, cols_ref[0, 0, i, 2 * b], cols_ref[0, 0, i, 2 * b + 1])
+            index = jnp.where(row == i, cols, index)
+        packed_ref[rows:, b * LANES : (b + 1) * LANES] = index.astype(jnp.float32).astype(jnp.bfloat16)
+    copies[1].wait()
+    for b in range(nl // 2):
+        for i in range(ib):
+            pair = jnp.concatenate([left_ref[i, 2 * b], left_ref[i, 2 * b + 1]], axis=1)
+            packed_ref[i * half : (i + 1) * half, b * LANES : (b + 1) * LANES] = pair
+
+
+def first_kernel(cols_hbm, right_hbm, packed_ref, dense_ref, code_ref, left_ref, cols_ref, right_ref, sem):
+    kb, kept, half, _ = right_ref.shape
+    rows = left_ref.shape[0]
+    parts = sem.shape[0] - 1
     step = kb // parts
-    pairs = [(left_cols_hbm, left_cols_ref), (left_hbm.at[0, 0], left_raw), (right_cols_hbm, right_cols_ref)]
+    pairs = [(cols_hbm, cols_ref)]
     for part in range(parts):
         here = pl.ds(part * step, step)
-        pairs.append((right_hbm.at[0, 0, here], right_raw.at[here]))
+        pairs.append((right_hbm.at[0, 0, here], right_ref.at[here]))
     copies = [pltpu.make_async_copy(*pair, sem.at[n]) for n, pair in enumerate(pairs)]
     for copy in copies:
         copy.start()
-    left_ref[...] = jnp.zeros_like(left_ref)
     dense_ref[...] = jnp.zeros_like(dense_ref)
+    spread_left(packed_ref, rows, half, left_ref)
     copies[0].wait()
-    copies[1].wait()
-    side = lax.broadcasted_iota(jnp.int32, (PAD, LANES), 1) // half
-    row = lax.broadcasted_iota(jnp.int32, (PAD, LANES), 0)
-    for b in range(nl // 2):
-        lanes = slice(b * LANES, (b + 1) * LANES)
-        index = jnp.zeros((PAD, LANES), jnp.int32)
-        for i in range(ib):
-            pair = jnp.concatenate([left_raw[i, 2 * b], left_raw[i, 2 * b + 1]], axis=1)
-            packed_ref[i * half : (i + 1) * half, lanes] = pair
-            cols = jnp.where(side == 0, left_cols_ref[0, 0, i, 2 * b], left_cols_ref[0, 0, i, 2 * b + 1])
-            index = jnp.where(row == i, cols, index)
-        packed_ref[rows:, lanes] = index.astype(jnp.float32).astype(jnp.bfloat16)
-    for a in range(nl):
-        place([(left_raw[i, a], i, left_cols_ref[0, 0, i, a]) for i in range(ib)], left_ref)
-    copies[2].wait()
     for part in range(parts):
-        copies[part + 3].wait()
+        copies[part + 1].wait()
         for e in range(kept):
             ks = range(part * step, (part + 1) * step)
-            place([(right_raw[k, e], k, right_cols_ref[0, e, 0, k]) for k in ks], dense_ref)
-    left = jnp.concatenate([left_ref[m] for m in range(left_ref.shape[0])], axis=1)
-    encode(product(left, dense_ref), code_ref)
-
-
-def second_kernel(half, dense_ref, packed_ref, own_cols_ref, one_cols_ref, *refs):
-    *code_refs, pair_ref, left_ref = refs
-    pair_ref[0] = own_cols_ref[0]
-    pair_ref[1] = one_cols_ref[0]
+            place([(right_ref[k, e], k, cols_ref[0, e, 0, k]) for k in ks], dense_ref)
+    encode(product(left_ref[...], dense_ref), code_ref)
+
+
+def second_kernel(half, dense_ref, packed_ref, code_ref, left_ref):
     spread_left(packed_ref, left_ref.shape[0], half, left_ref)
-    found = product(left_ref[...], dense_ref)
-    for i, code_ref in enumerate(code_refs):
-        encode([part[i * half : (i + 1) * half] for part in found], code_ref)
+    encode(product(left_ref[...], dense_ref), code_ref)
 
 
 def swapped():
@@ -198,16 +187,14 @@
         kept_ref[slot, m] = part
 
 
-def sum_kernel(half, odd, first, own_ref, one_ref, far_ref, kept_ref, code_ref, *refs):
-    pairs = kept_ref.shape[1]
-    rows = (code_ref.shape[0] - PAD) // pairs
+def sum_kernel(half, odd, own_ref, one_ref, far_ref, kept_ref, code_ref, *refs):
     if odd:
         held_ref, a_ref, b_ref, keep_ref, wide_ref, new_ref = refs
-        held_refs, new_refs = [held_ref], [new_ref]
     else:
-        a_ref, *new_refs, wide_ref = refs
+        a_ref, new_ref, wide_ref = refs
+    _, pairs, rows, _ = kept_ref.shape
     for m, part in enumerate(decoded(code_ref, rows)):
-        total = kept_ref[odd, m, first * half : first * half + rows] + part
+        total = kept_ref[odd, m] + part
         wide_ref[m] = total
         wide_ref[pairs + m] = pltpu.roll(total, half, 1)
     low = lax.broadcasted_iota(jnp.int32, (half, LANES), 1) < half
@@ -216,36 +203,29 @@
     def pick(near, i, o):
         picked = []
         for side in range(2):
-            at = (0, first + i, o + side)
-            if near:
-                j = jnp.where(stays, own_ref[(0, *at)], one_ref[(0, *at)])
-            else:
-                j = jnp.where(stays, far_ref[(0, *at)], far_ref[(1, *at)])
+            at = (0, 0, i, o + side)
+            j = jnp.where(stays, own_ref[at], one_ref[at]) if near else far_ref[at]
             slot = lax.shift_right_logical(j, 1) + pairs * ((j + side) & 1)
             picked.append(wide_ref[slot, i * half : (i + 1) * half, :])
         return jnp.where(low, picked[0], picked[1])
 
-    count = own_ref.shape[3]
-    blocks = range(rows // half)
-    encode([jnp.concatenate([pick(False, i, o) for i in blocks], axis=0) for o in range(0, count, 2)], a_ref)
-    for i, new_ref in zip(blocks, new_refs):
-        encode([pick(True, i, o) for o in range(0, count, 2)], new_ref)
+    for near, target in ((False, a_ref), (True, new_ref)):
+        steps = range(0, own_ref.shape[3], 2)
+        encode([jnp.concatenate([pick(near, i, o) for i in range(rows // half)], axis=0) for o in steps], target)
     if odd:
         b_ref[...] = jnp.where(stays, held_ref[...], new_ref[...])
         keep_ref[...] = jnp.where(stays, new_ref[...], held_ref[...])
 
 
-def last_kernel(half, whole_ref, *refs):
-    *part_refs, out_ref = refs
+def last_kernel(half, a_ref, b_ref, c_ref, own_ref, out_ref):
     ib = out_ref.shape[2]
-    parts = [[decoded(ref, half) for ref in part_refs[i::ib]] for i in range(ib)]
-    for m, whole in enumerate(decoded(whole_ref, ib * half)):
+    arrived = [decoded(ref, ib * half) for ref in (a_ref, b_ref, c_ref, own_ref)]
+    for m, (a, b, c, own) in enumerate(zip(*arrived)):
+        total = (a + own) + (b + c)
         for i in range(ib):
-            total = whole[i * half : (i + 1) * half]
-            for part in parts[i]:
-                total = total + next(part)
-            out_ref[0, 0, i, 2 * m] = total[:, :half]
-            out_ref[0, 0, i, 2 * m + 1] = total[:, half:]
+            part = total[i * half : (i + 1) * half]
+            out_ref[0, 0, i, 2 * m] = part[:, :half]
+            out_ref[0, 0, i, 2 * m + 1] = part[:, half:]
 
 
 VMEM = pl.BlockSpec(memory_space=pltpu.VMEM)
@@ -275,35 +255,43 @@
 
     wide_cols, no_cols = jb * bs // LANES, no * bs // LANES
     code = jax.ShapeDtypeStruct((wide_cols * rows + PAD, LANES), jnp.int16)
-    code_part = jax.ShapeDtypeStruct((wide_cols * bs + PAD, LANES), jnp.int16)
     small = jax.ShapeDtypeStruct((no_cols * rows + PAD, LANES), jnp.int16)
-    small_part = jax.ShapeDtypeStruct((no_cols * bs + PAD, LANES), jnp.int16)
     both = jax.ShapeDtypeStruct((2, wide_cols, rows, LANES), jnp.float32)
     left_scratch = pltpu.VMEM((rows, kb * bs), jnp.bfloat16)
-    operands = (right_cols.transpose(0, 3, 1, 2), left_cols, left_blocks, right_blocks)
-    dense, code_one, packed = pl.pallas_call(
-        first_kernel,
-        out_shape=(
-            jax.ShapeDtypeStruct((wide_cols, kb * bs, LANES), jnp.bfloat16),
-            code,
-            jax.ShapeDtypeStruct((rows + PAD, nl * bs), jnp.bfloat16),
-        ),
-        in_specs=[HBM] * 4,
-        out_specs=(VMEM, VMEM, VMEM),
+    def in_hbm(*arrays):
+        return [pltpu.with_memory_space_constraint(array, pltpu.HBM) for array in arrays]
+
+    packed = pl.pallas_call(
+        pack_kernel,
+        out_shape=jax.ShapeDtypeStruct((rows + PAD, nl * bs), jnp.bfloat16),
+        in_specs=[HBM] * 2,
+        out_specs=VMEM,
         scratch_shapes=[
-            pltpu.VMEM((kb * bs // LANES, rows, LANES), jnp.bfloat16),
-            pltpu.SMEM((1, right_cols.shape[3], 1, kb), jnp.int32),
             pltpu.SMEM(left_cols.shape[:2] + (ib, nl), jnp.int32),
             pltpu.VMEM(left_blocks.shape[2:], jnp.bfloat16),
+            pltpu.SemaphoreType.DMA((2,)),
+        ],
+        compiler_params=PARAMS,
+        name="pack",
+    )(*in_hbm(left_cols, left_blocks))
+    dense, code_one = pl.pallas_call(
+        first_kernel,
+        out_shape=(jax.ShapeDtypeStruct((wide_cols, kb * bs, LANES), jnp.bfloat16), code),
+        in_specs=[HBM, HBM, VMEM],
+        out_specs=(VMEM, VMEM),
+        scratch_shapes=[
+            left_scratch,
+            pltpu.SMEM((1, right_cols.shape[3], 1, kb), jnp.int32),
             pltpu.VMEM(right_blocks.shape[2:], jnp.bfloat16),
-            pltpu.SemaphoreType.DMA((PARTS + 3,)),
+            pltpu.SemaphoreType.DMA((PARTS + 1,)),
         ],
         compiler_params=PARAMS,
         name="first",
-    )(*(pltpu.with_memory_space_constraint(a, pltpu.HBM) for a in operands))
+    )(*in_hbm(right_cols.transpose(0, 3, 1, 2), right_blocks), packed)
     got_one = send(code_one, lambda r, c: (r, c ^ 1))
     across = send(packed, lambda r, c: ((r + 2) % n_row, c))
     near = send(packed, lambda r, c: (r ^ 1, c))
+    own_cols = out_cols
     kept = pl.pallas_call(
         functools.partial(near_kernel, bs),
         out_shape=both,
@@ -313,21 +301,19 @@
         compiler_params=PARAMS,
         name="near",
     )(dense, near)
-    kept, own_cols = lax.optimization_barrier((kept, out_cols))
     one_cols = send(own_cols, along(1, 1))
-    across, kept, one_cols = lax.optimization_barrier((across, kept, one_cols))
+    far_cols = [send(own_cols, along(2, 3)), send(own_cols, along(3, 2))]
     far = send(across, lambda r, c: (r ^ 1, c))
-    *codes, pair_cols = pl.pallas_call(
+    code_two = pl.pallas_call(
         functools.partial(second_kernel, bs),
-        out_shape=(*(ib * (code_part,)), jax.ShapeDtypeStruct((2, *out_cols.shape[1:]), jnp.int32)),
-        in_specs=[VMEM] * 4,
-        out_specs=(ib + 1) * (VMEM,),
+        out_shape=code,
+        in_specs=[VMEM] * 2,
+        out_specs=VMEM,
         scratch_shapes=[left_scratch],
         compiler_params=PARAMS,
         name="second",
-    )(dense, across, own_cols, one_cols)
-    got_two = [send(code, lambda r, c: (r, c ^ 1)) for code in codes]
-    far_cols = send(pair_cols, along(2, 2))
+    )(dense, across)
+    got_two = send(code_two, lambda r, c: (r, c ^ 1))
     kept = pl.pallas_call(
         functools.partial(far_kernel, bs),
         out_shape=both,
@@ -339,30 +325,23 @@
         name="far",
     )(dense, far, kept)
 
-    def summed(odd, first, code, *held):
-        if odd:
-            outs = 3 * (small_part,)
-        else:
-            outs = (small, *(ib * (small_part,)))
-        scratch = [pltpu.VMEM((2 * wide_cols, rows if not odd else bs, LANES), jnp.float32)]
-        scratch += odd * [pltpu.VMEM(small_part.shape, small_part.dtype)]
+    def summed(odd, code, *held):
+        scratch = [pltpu.VMEM((2 * wide_cols, rows, LANES), jnp.float32)]
+        scratch += odd * [pltpu.VMEM(small.shape, small.dtype)]
         return pl.pallas_call(
-            functools.partial(sum_kernel, bs, odd, first),
-            out_shape=outs,
+            functools.partial(sum_kernel, bs, odd),
+            out_shape=(2 + odd) * (small,),
             in_specs=[SMEM] * 3 + [VMEM] * (2 + odd),
-            out_specs=len(outs) * (VMEM,),
+            out_specs=(2 + odd) * (VMEM,),
             scratch_shapes=scratch,
             compiler_params=PARAMS,
             name="sum",
-        )(own_cols, one_cols, far_cols, kept, code, *held)
-
-    a, *held = summed(0, 0, got_one)
-    whole = send(a, along(2, 3))
-    parts = []
-    for i in range(ib):
-        a, b, keep = summed(1, i, got_two[i], held[i])
-        parts.append((send(a, along(3, 2)), send(b, along(1, 1)), keep))
-    got = [whole, *(part for group in zip(*parts) for part in group)]
+        )(own_cols, one_cols, far_cols[odd], kept, code, *held)
+
+    a, held = summed(0, got_one)
+    got = [send(a, along(2, 3))]
+    a, b, own = summed(1, got_two, held)
+    got += [send(a, along(3, 2)), send(b, along(1, 1)), own]
     return pl.pallas_call(
         functools.partial(last_kernel, bs),
         out_shape=jax.ShapeDtypeStruct((1, 1, ib, no, bs, bs), jnp.float32),

time: 35.1 us -> 33.1 us (0.943)
  starting transfers between devices: 18.7 us -> 16.6 us
    ppermute x13 -> x11, starting transfers between devices: 18.7 us -> 16.6 us  [send(): return lax.ppermute(value, ('row', 'col'), pairs)]
    ppermute x13 -> x11, waiting for transfers between devices: 7.31 us -> 7.3 us  [send(): return lax.ppermute(value, ('row', 'col'), pairs)]
  transfers between devices with their start and end apart: 13 -> 11, of which waited for: 7 -> 3; matrix products, arithmetic and copies ran while one was open for 0% -> 0% of each run, Pallas kernels for 15% -> 21%
where the time goes in v3:
time: 33.1 us; the launch traced here: 32.9 us
  starting transfers between devices  16.6 us (50%)
  Pallas kernels  8.95 us (27%)
  waiting for transfers between devices  7.3 us (22%)
    ppermute x11, starting transfers between devices, send(): return lax.ppermute(value, ('row', 'col'), pairs)  16.6 us
    ppermute x11, waiting for transfers between devices, send(): return lax.ppermute(value, ('row', 'col'), pairs)  7.3 us
    pallas_call x1, Pallas kernels, grid_path(): pl.pallas_call(first_kernel, out_shape=(jax.ShapeDtypeStruct((wide_cols,...  2.48 us
    pallas_call x2, Pallas kernels, summed(): pl.pallas_call(functools.partial(sum_kernel, bs, odd), out_shape=(2 + odd...  2 us
    pallas_call x1, Pallas kernels, grid_path(): pl.pallas_call(pack_kernel, out_shape=jax.ShapeDtypeStruct((rows + PAD, n...  1.07 us
    pallas_call x1, Pallas kernels, grid_path(): pl.pallas_call(functools.partial(last_kernel, bs), out_shape=jax.ShapeDty...  1 us
    pallas_call x1, Pallas kernels, grid_path(): pl.pallas_call(functools.partial(second_kernel, bs), out_shape=code, in_s...  0.86 us
    pallas_call x1, Pallas kernels, grid_path(): pl.pallas_call(functools.partial(near_kernel, bs), out_shape=both, in_spe...  0.77 us
  transfers between devices with their start and end apart: 11, of which 3 were waited for; matrix products, arithmetic and copies ran while one was open for 0% of the time, Pallas kernels for 21%

profile of v3, /device:TPU:0, one launch (start us, length us, event | category | flops | bytes accessed | tf_op | source)
XLA Modules:
  0.0 32.9 jit_solution(18123102279375590132)
XLA Ops:
  0.0 1.1 %pack.1.packed_ref = bf16[144,512]{1,0:T(8,128)(2,1)S(1)} custom-call(s32[1,1,2,8]{3,2,1,0:T(2,128)} %cols_hbm.1, bf16[1,1,2,8,64,64]{5,4,3,2,1,0:T(8,128)(2,1)} %left_hbm.1), custom_call_target="tpu_custom_call" | custom-call | tf_op jit(solution)/shard_map/pack/pallas_call | solution.py:264
  1.1 3.0 %collective-permute-start.2 = (bf16[144,512]{1,0:T(8,128)(2,1)S(1)}, bf16[144,512]{1,0:T(8,128)(2,1)S(1)}, u32[]{:S(2)}, u32[]{:S(2)}) collective-permute-start(bf16[144,512]{1,0:T(8,128)(2,1)S(1)} %pack.1.packed_ref), channel_id=1, source_target_pairs={{0,16},{1,17},{2,18},{3,19},{4,20},{5,21},{6,22},{7,23},{8,24},{9,... | collective-permute-start | bytes 442376 | tf_op jit(solution)/shard_map/ppermute | solution.py:251
  4.1 0.0 copy-start
  4.1 2.5 %first.1 = (bf16[8,1024,128]{2,1,0:T(8,128)(2,1)S(1)}, s16[1040,128]{1,0:T(8,128)(2,1)S(1)}) custom-call(s32[1,6,1,16]{3,2,1,0:T(1,128)} %bitcast.1, bf16[1,1,16,6,64,64]{5,4,3,2,1,0:T(8,128)(2,1)} %right_hbm.1, bf16[144,512]{1,0:T(8,128)(2,1)S(1)} %pack.1.packed_ref), custom_call_target="tpu_custom_call" | custom-call | tf_op jit(solution)/shard_map/first/pallas_call | solution.py:277
  6.6 1.6 %collective-permute-start.5 = (s16[1040,128]{1,0:T(8,128)(2,1)S(1)}, s16[1040,128]{1,0:T(8,128)(2,1)S(1)}, u32[]{:S(2)}, u32[]{:S(2)}) collective-permute-start(s16[1040,128]{1,0:T(8,128)(2,1)S(1)} %get-tuple-element.13), channel_id=1, source_target_pairs={{0,1},{1,0},{2,3},{3,2},{4,5},{5,4},{6,7},{7,6},{8,9},{9,8},{10,11... | collective-permute-start | bytes 798728 | tf_op jit(solution)/shard_map/ppermute | solution.py:251
  8.2 0.0 collective-permute-done.2.packed_ref
  8.2 0.9 %second.1 = s16[1040,128]{1,0:T(8,128)(2,1)S(1)} custom-call(bf16[8,1024,128]{2,1,0:T(8,128)(2,1)S(1)} %get-tuple-element.12.dense_ref, bf16[144,512]{1,0:T(8,128)(2,1)S(1)} %collective-permute-done.2.packed_ref), custom_call_target="tpu_custom_call" | custom-call | tf_op jit(solution)/shard_map/second/pallas_call | solution.py:307
  9.0 1.6 %collective-permute-start.8 = (s16[1040,128]{1,0:T(8,128)(2,1)S(1)}, s16[1040,128]{1,0:T(8,128)(2,1)S(1)}, u32[]{:S(2)}, u32[]{:S(2)}) collective-permute-start(s16[1040,128]{1,0:T(8,128)(2,1)S(1)} %second.1), channel_id=1, source_target_pairs={{0,1},{1,0},{2,3},{3,2},{4,5},{5,4},{6,7},{7,6},{8,9},{9,8},{10,11... | collective-permute-start | bytes 798728 | tf_op jit(solution)/shard_map/ppermute | solution.py:251
  10.6 0.0 collective-permute-start.4
  10.6 0.5 %collective-permute-start.3 = (bf16[144,512]{1,0:T(8,128)(2,1)S(1)}, bf16[144,512]{1,0:T(8,128)(2,1)S(1)}, u32[]{:S(2)}, u32[]{:S(2)}) collective-permute-start(bf16[144,512]{1,0:T(8,128)(2,1)S(1)} %collective-permute-done.2.packed_ref), channel_id=1, source_target_pairs={{0,8},{1,9},{2,10},{3,11},{4,12},{5,13},{6,14},{7,15},{8,0},{9,1},... | collective-permute-start | bytes 442376 | tf_op jit(solution)/shard_map/ppermute | solution.py:251
  11.1 0.0 copy-done
  11.1 1.6 %collective-permute-start = (s32[1,1,2,8]{3,2,1,0:T(2,128)S(1)}, s32[1,1,2,8]{3,2,1,0:T(2,128)S(1)}, u32[]{:S(2)}, u32[]{:S(2)}) collective-permute-start(s32[1,1,2,8]{3,2,1,0:T(2,128)S(1)} %copy-done), channel_id=1, source_target_pairs={{0,2},{1,3},{2,0},{3,1},{4,6},{5,7},{6,4},{7,5},{8,10},{9,11},{10,... | collective-permute-start | bytes 200 | tf_op jit(solution)/shard_map/ppermute | solution.py:251
  12.7 0.0 collective-permute-done.4.packed_ref
  12.7 2.6 %collective-permute-start.1 = (s32[1,1,2,8]{3,2,1,0:T(2,128)S(1)}, s32[1,1,2,8]{3,2,1,0:T(2,128)S(1)}, u32[]{:S(2)}, u32[]{:S(2)}) collective-permute-start(s32[1,1,2,8]{3,2,1,0:T(2,128)S(1)} %copy-done), channel_id=1, source_target_pairs={{0,4},{1,7},{2,6},{3,5},{4,0},{5,3},{6,2},{7,1},{8,12},{9,15},{10,... | collective-permute-start | bytes 200 | tf_op jit(solution)/shard_map/ppermute | solution.py:251
  15.3 0.8 %near.1._ = f32[2,8,128,128]{3,2,1,0:T(8,128)S(1)} custom-call(bf16[8,1024,128]{2,1,0:T(8,128)(2,1)S(1)} %get-tuple-element.12.dense_ref, bf16[144,512]{1,0:T(8,128)(2,1)S(1)} %collective-permute-done.4.packed_ref), custom_call_target="tpu_custom_call" | custom-call | tf_op jit(solution)/shard_map/near/pallas_call | solution.py:295
  16.1 0.0 collective-permute-done.3.packed_ref
  16.1 0.7 %collective-permute-start.7 = (s32[1,1,2,8]{3,2,1,0:T(2,128)S(1)}, s32[1,1,2,8]{3,2,1,0:T(2,128)S(1)}, u32[]{:S(2)}, u32[]{:S(2)}) collective-permute-start(s32[1,1,2,8]{3,2,1,0:T(2,128)S(1)} %copy-done), channel_id=1, source_target_pairs={{0,6},{1,5},{2,4},{3,7},{4,2},{5,1},{6,0},{7,3},{8,14},{9,13},{10,... | collective-permute-start | bytes 200 | tf_op jit(solution)/shard_map/ppermute | solution.py:251
  16.8 0.8 %far.1.kept_ref = f32[2,8,128,128]{3,2,1,0:T(8,128)S(1)} custom-call(bf16[8,1024,128]{2,1,0:T(8,128)(2,1)S(1)} %get-tuple-element.12.dense_ref, bf16[144,512]{1,0:T(8,128)(2,1)S(1)} %collective-permute-done.3.packed_ref, f32[2,8,128,128]{3,2,1,0:T(8,128)S(1)} %near.1._), custom_call_target="tpu_custom_call", output_to_operand_aliasing={{}: (2, {})} | custom-call | tf_op jit(solution)/shard_map/far/pallas_call | solution.py:317
  17.6 0.0 collective-permute-done.one_ref
  17.6 0.0 collective-permute-done.1.far_ref
  17.6 0.0 collective-permute-done.5.code_ref
  17.6 1.0 %sum.2 = (s16[528,128]{1,0:T(8,128)(2,1)S(1)}, s16[528,128]{1,0:T(8,128)(2,1)S(1)}) custom-call(s32[1,1,2,8]{3,2,1,0:T(2,128)S(1)} %copy-done, s32[1,1,2,8]{3,2,1,0:T(2,128)S(1)} %collective-permute-done.one_ref, s32[1,1,2,8]{3,2,1,0:T(2,128)S(1)} %collective-permute-done.1.far_ref, f32[2,8,128,128]{3,2,1,0:T(8,128)S(1)} %far.1.kept_ref, ...), custom_call_target="tpu_custom_call" | custom-call | tf_op jit(solution)/shard_map/sum/pallas_call | solution.py:331
  18.6 2.2 %collective-permute-start.6 = (s16[528,128]{1,0:T(8,128)(2,1)S(1)}, s16[528,128]{1,0:T(8,128)(2,1)S(1)}, u32[]{:S(2)}, u32[]{:S(2)}) collective-permute-start(s16[528,128]{1,0:T(8,128)(2,1)S(1)} %get-tuple-element.14), channel_id=1, source_target_pairs={{0,4},{1,7},{2,6},{3,5},{4,0},{5,3},{6,2},{7,1},{8,12},{9,15},{10,... | collective-permute-start | bytes 405512 | tf_op jit(solution)/shard_map/ppermute | solution.py:251
  20.8 0.7 %collective-permute-done.7.far_ref = s32[1,1,2,8]{3,2,1,0:T(2,128)S(1)} collective-permute-done((s32[1,1,2,8]{3,2,1,0:T(2,128)S(1)}, s32[1,1,2,8]{3,2,1,0:T(2,128)S(1)}, u32[]{:S(2)}, u32[]{:S(2)}) %collective-permute-start.7) | collective-permute-done | bytes 96 | tf_op jit(solution)/shard_map/ppermute | solution.py:251
  21.5 0.0 collective-permute-done.8.code_ref
  21.5 1.0 %sum.3 = (s16[528,128]{1,0:T(8,128)(2,1)S(1)}, s16[528,128]{1,0:T(8,128)(2,1)S(1)}, s16[528,128]{1,0:T(8,128)(2,1)S(1)}) custom-call(s32[1,1,2,8]{3,2,1,0:T(2,128)S(1)} %copy-done, s32[1,1,2,8]{3,2,1,0:T(2,128)S(1)} %collective-permute-done.one_ref, s32[1,1,2,8]{3,2,1,0:T(2,128)S(1)} %collective-permute-done.7.far_ref, f32[2,8,128,128]{3,2,1,0:T(8,128)S(1)} %far.1.kept_ref, ...), custom_call_target="tpu_custom_call" | custom-call | tf_op jit(solution)/shard_map/sum/pallas_call | solution.py:331
  22.5 1.0 %collective-permute-start.10 = (s16[528,128]{1,0:T(8,128)(2,1)S(1)}, s16[528,128]{1,0:T(8,128)(2,1)S(1)}, u32[]{:S(2)}, u32[]{:S(2)}) collective-permute-start(s16[528,128]{1,0:T(8,128)(2,1)S(1)} %get-tuple-element.17), channel_id=1, source_target_pairs={{0,2},{1,3},{2,0},{3,1},{4,6},{5,7},{6,4},{7,5},{8,10},{9,11},{10,... | collective-permute-start | bytes 405512 | tf_op jit(solution)/shard_map/ppermute | solution.py:251
  23.5 1.9 %collective-permute-start.9 = (s16[528,128]{1,0:T(8,128)(2,1)S(1)}, s16[528,128]{1,0:T(8,128)(2,1)S(1)}, u32[]{:S(2)}, u32[]{:S(2)}) collective-permute-start(s16[528,128]{1,0:T(8,128)(2,1)S(1)} %get-tuple-element.16), channel_id=1, source_target_pairs={{0,6},{1,5},{2,4},{3,7},{4,2},{5,1},{6,0},{7,3},{8,14},{9,13},{10,... | collective-permute-start | bytes 405512 | tf_op jit(solution)/shard_map/ppermute | solution.py:251
  25.4 3.9 %collective-permute-done.6.a_ref = s16[528,128]{1,0:T(8,128)(2,1)S(1)} collective-permute-done((s16[528,128]{1,0:T(8,128)(2,1)S(1)}, s16[528,128]{1,0:T(8,128)(2,1)S(1)}, u32[]{:S(2)}, u32[]{:S(2)}) %collective-permute-start.6) | collective-permute-done | bytes 135200 | tf_op jit(solution)/shard_map/ppermute | solution.py:251
  29.2 2.7 %collective-permute-done.10.c_ref = s16[528,128]{1,0:T(8,128)(2,1)S(1)} collective-permute-done((s16[528,128]{1,0:T(8,128)(2,1)S(1)}, s16[528,128]{1,0:T(8,128)(2,1)S(1)}, u32[]{:S(2)}, u32[]{:S(2)}) %collective-permute-start.10) | collective-permute-done | bytes 135200 | tf_op jit(solution)/shard_map/ppermute | solution.py:251
  31.9 0.0 collective-permute-done.9.b_ref
  31.9 1.0 %last.1 = f32[1,1,2,8,64,64]{5,4,3,2,1,0:T(8,128)} custom-call(s16[528,128]{1,0:T(8,128)(2,1)S(1)} %collective-permute-done.6.a_ref, s16[528,128]{1,0:T(8,128)(2,1)S(1)} %collective-permute-done.9.b_ref, s16[528,128]{1,0:T(8,128)(2,1)S(1)} %collective-permute-done.10.c_ref, s16[528,128]{1,0:T(8,128)(2,1)S(1)} %get-tuple-element.18.own_ref), custom_call_target="tpu_custom_call" | custom-call | tf_op jit(solution)/shard_map/last/pallas_call | solution.py:345
Async XLA Ops:
  1.1 7.1 %collective-permute-start.2 = (bf16[144,512]{1,0:T(8,128)(2,1)S(1)}, bf16[144,512]{1,0:T(8,128)(2,1)S(1)}, u32[]{:S(2)}, u32[]{:S(2)}) collective-permute-start(bf16[144,512]{1,0:T(8,128)(2,1)S(1)} %pack.1.packed_ref), channel_id=1, source_target_pairs={{0,16},{1,17},{2,18},{3,19},{4,20},{5,21},{6,22},{7,23},{8,24},{9,... | collective-permute-start | bytes 442376 | tf_op jit(solution)/shard_map/ppermute | solution.py:251
  4.1 7.0 %copy-start = (s32[1,1,2,8]{3,2,1,0:T(2,128)S(1)}, s32[1,1,2,8]{3,2,1,0:T(2,128)}, u32[]{:S(2)}) copy-start(s32[1,1,2,8]{3,2,1,0:T(2,128)} %own_ref.3) | copy-start | bytes 196
  6.6 11.0 %collective-permute-start.5 = (s16[1040,128]{1,0:T(8,128)(2,1)S(1)}, s16[1040,128]{1,0:T(8,128)(2,1)S(1)}, u32[]{:S(2)}, u32[]{:S(2)}) collective-permute-start(s16[1040,128]{1,0:T(8,128)(2,1)S(1)} %get-tuple-element.13), channel_id=1, source_target_pairs={{0,1},{1,0},{2,3},{3,2},{4,5},{5,4},{6,7},{7,6},{8,9},{9,8},{10,11... | collective-permute-start | bytes 798728 | tf_op jit(solution)/shard_map/ppermute | solution.py:251
  9.0 12.5 %collective-permute-start.8 = (s16[1040,128]{1,0:T(8,128)(2,1)S(1)}, s16[1040,128]{1,0:T(8,128)(2,1)S(1)}, u32[]{:S(2)}, u32[]{:S(2)}) collective-permute-start(s16[1040,128]{1,0:T(8,128)(2,1)S(1)} %second.1), channel_id=1, source_target_pairs={{0,1},{1,0},{2,3},{3,2},{4,5},{5,4},{6,7},{7,6},{8,9},{9,8},{10,11... | collective-permute-start | bytes 798728 | tf_op jit(solution)/shard_map/ppermute | solution.py:251
  10.6 2.1 %collective-permute-start.4 = (bf16[144,512]{1,0:T(8,128)(2,1)S(1)}, bf16[144,512]{1,0:T(8,128)(2,1)S(1)}, u32[]{:S(2)}, u32[]{:S(2)}) collective-permute-start(bf16[144,512]{1,0:T(8,128)(2,1)S(1)} %pack.1.packed_ref), channel_id=1, source_target_pairs={{0,8},{1,9},{2,10},{3,11},{4,12},{5,13},{6,14},{7,15},{8,0},{9,1},... | collective-permute-start | bytes 442376 | tf_op jit(solution)/shard_map/ppermute | solution.py:251
  10.6 5.5 %collective-permute-start.3 = (bf16[144,512]{1,0:T(8,128)(2,1)S(1)}, bf16[144,512]{1,0:T(8,128)(2,1)S(1)}, u32[]{:S(2)}, u32[]{:S(2)}) collective-permute-start(bf16[144,512]{1,0:T(8,128)(2,1)S(1)} %collective-permute-done.2.packed_ref), channel_id=1, source_target_pairs={{0,8},{1,9},{2,10},{3,11},{4,12},{5,13},{6,14},{7,15},{8,0},{9,1},... | collective-permute-start | bytes 442376 | tf_op jit(solution)/shard_map/ppermute | solution.py:251
  11.1 6.4 %collective-permute-start = (s32[1,1,2,8]{3,2,1,0:T(2,128)S(1)}, s32[1,1,2,8]{3,2,1,0:T(2,128)S(1)}, u32[]{:S(2)}, u32[]{:S(2)}) collective-permute-start(s32[1,1,2,8]{3,2,1,0:T(2,128)S(1)} %copy-done), channel_id=1, source_target_pairs={{0,2},{1,3},{2,0},{3,1},{4,6},{5,7},{6,4},{7,5},{8,10},{9,11},{10,... | collective-permute-start | bytes 200 | tf_op jit(solution)/shard_map/ppermute | solution.py:251
  12.7 4.9 %collective-permute-start.1 = (s32[1,1,2,8]{3,2,1,0:T(2,128)S(1)}, s32[1,1,2,8]{3,2,1,0:T(2,128)S(1)}, u32[]{:S(2)}, u32[]{:S(2)}) collective-permute-start(s32[1,1,2,8]{3,2,1,0:T(2,128)S(1)} %copy-done), channel_id=1, source_target_pairs={{0,4},{1,7},{2,6},{3,5},{4,0},{5,3},{6,2},{7,1},{8,12},{9,15},{10,... | collective-permute-start | bytes 200 | tf_op jit(solution)/shard_map/ppermute | solution.py:251
  16.1 5.4 %collective-permute-start.7 = (s32[1,1,2,8]{3,2,1,0:T(2,128)S(1)}, s32[1,1,2,8]{3,2,1,0:T(2,128)S(1)}, u32[]{:S(2)}, u32[]{:S(2)}) collective-permute-start(s32[1,1,2,8]{3,2,1,0:T(2,128)S(1)} %copy-done), channel_id=1, source_target_pairs={{0,6},{1,5},{2,4},{3,7},{4,2},{5,1},{6,0},{7,3},{8,14},{9,13},{10,... | collective-permute-start | bytes 200 | tf_op jit(solution)/shard_map/ppermute | solution.py:251
  18.6 10.7 %collective-permute-start.6 = (s16[528,128]{1,0:T(8,128)(2,1)S(1)}, s16[528,128]{1,0:T(8,128)(2,1)S(1)}, u32[]{:S(2)}, u32[]{:S(2)}) collective-permute-start(s16[528,128]{1,0:T(8,128)(2,1)S(1)} %get-tuple-element.14), channel_id=1, source_target_pairs={{0,4},{1,7},{2,6},{3,5},{4,0},{5,3},{6,2},{7,1},{8,12},{9,15},{10,... | collective-permute-start | bytes 405512 | tf_op jit(solution)/shard_map/ppermute | solution.py:251
  22.5 9.4 %collective-permute-start.10 = (s16[528,128]{1,0:T(8,128)(2,1)S(1)}, s16[528,128]{1,0:T(8,128)(2,1)S(1)}, u32[]{:S(2)}, u32[]{:S(2)}) collective-permute-start(s16[528,128]{1,0:T(8,128)(2,1)S(1)} %get-tuple-element.17), channel_id=1, source_target_pairs={{0,2},{1,3},{2,0},{3,1},{4,6},{5,7},{6,4},{7,5},{8,10},{9,11},{10,... | collective-permute-start | bytes 405512 | tf_op jit(solution)/shard_map/ppermute | solution.py:251
  23.5 8.5 %collective-permute-start.9 = (s16[528,128]{1,0:T(8,128)(2,1)S(1)}, s16[528,128]{1,0:T(8,128)(2,1)S(1)}, u32[]{:S(2)}, u32[]{:S(2)}) collective-permute-start(s16[528,128]{1,0:T(8,128)(2,1)S(1)} %get-tuple-element.16), channel_id=1, source_target_pairs={{0,6},{1,5},{2,4},{3,7},{4,2},{5,1},{6,0},{7,3},{8,14},{9,13},{10,... | collective-permute-start | bytes 405512 | tf_op jit(solution)/shard_map/ppermute | solution.py:251

commit v4 on v3

--- a/solution.py
+++ b/solution.py
@@ -141,7 +141,9 @@
             packed_ref[i * half : (i + 1) * half, b * LANES : (b + 1) * LANES] = pair
 
 
-def first_kernel(cols_hbm, right_hbm, packed_ref, dense_ref, code_ref, left_ref, cols_ref, right_ref, sem):
+def first_kernel(
+    cols_hbm, right_hbm, packed_ref, dense_ref, code_ref, left_ref, cols_ref, right_ref, sem
+):
     kb, kept, half, _ = right_ref.shape
     rows = left_ref.shape[0]
     parts = sem.shape[0] - 1
@@ -232,6 +234,7 @@
 SMEM = pl.BlockSpec(memory_space=pltpu.SMEM)
 HBM = pl.BlockSpec(memory_space=pltpu.HBM)
 PARTS = 4
+COST = pl.CostEstimate(flops=2000000000, bytes_accessed=20000000, transcendentals=0)
 PARAMS = pltpu.CompilerParams(vmem_limit_bytes=40 * 2**20)
 
 
@@ -274,9 +277,13 @@
         compiler_params=PARAMS,
         name="pack",
     )(*in_hbm(left_cols, left_blocks))
+    one_cols = send(out_cols, along(1, 1))
     dense, code_one = pl.pallas_call(
         first_kernel,
-        out_shape=(jax.ShapeDtypeStruct((wide_cols, kb * bs, LANES), jnp.bfloat16), code),
+        out_shape=(
+            jax.ShapeDtypeStruct((wide_cols, kb * bs, LANES), jnp.bfloat16),
+            code,
+        ),
         in_specs=[HBM, HBM, VMEM],
         out_specs=(VMEM, VMEM),
         scratch_shapes=[
@@ -290,19 +297,17 @@
     )(*in_hbm(right_cols.transpose(0, 3, 1, 2), right_blocks), packed)
     got_one = send(code_one, lambda r, c: (r, c ^ 1))
     across = send(packed, lambda r, c: ((r + 2) % n_row, c))
+    dense, packed = lax.optimization_barrier((dense, packed))
     near = send(packed, lambda r, c: (r ^ 1, c))
-    own_cols = out_cols
     kept = pl.pallas_call(
         functools.partial(near_kernel, bs),
         out_shape=both,
-        in_specs=[VMEM, VMEM],
+        in_specs=[VMEM] * 2,
         out_specs=VMEM,
         scratch_shapes=[left_scratch],
         compiler_params=PARAMS,
         name="near",
     )(dense, near)
-    one_cols = send(own_cols, along(1, 1))
-    far_cols = [send(own_cols, along(2, 3)), send(own_cols, along(3, 2))]
     far = send(across, lambda r, c: (r ^ 1, c))
     code_two = pl.pallas_call(
         functools.partial(second_kernel, bs),
@@ -313,6 +318,7 @@
         compiler_params=PARAMS,
         name="second",
     )(dense, across)
+    far_cols = (send(out_cols, along(2, 3)), send(out_cols, along(3, 2)))
     got_two = send(code_two, lambda r, c: (r, c ^ 1))
     kept = pl.pallas_call(
         functools.partial(far_kernel, bs),
@@ -335,8 +341,9 @@
             out_specs=(2 + odd) * (VMEM,),
             scratch_shapes=scratch,
             compiler_params=PARAMS,
+            cost_estimate=None if odd else COST,
             name="sum",
-        )(own_cols, one_cols, far_cols[odd], kept, code, *held)
+        )(out_cols, one_cols, far_cols[odd], kept, code, *held)
 
     a, held = summed(0, got_one)
     got = [send(a, along(2, 3))]

time: 33.1 us -> 32.1 us (0.970)
  waiting for transfers between devices: 7.3 us -> 6.32 us
    ppermute x11, waiting for transfers between devices: 7.3 us -> 6.32 us  [send(): return lax.ppermute(value, ('row', 'col'), pairs)]
  transfers between devices with their start and end apart: 11 -> 11, of which waited for: 3 -> 3; matrix products, arithmetic and copies ran while one was open for 0% -> 0% of each run, Pallas kernels for 21% -> 22%
where the time goes in v4:
time: 32.1 us; the launch traced here: 31.9 us
  starting transfers between devices  16.6 us (52%)
  Pallas kernels  8.96 us (28%)
  waiting for transfers between devices  6.32 us (20%)
    ppermute x11, starting transfers between devices, send(): return lax.ppermute(value, ('row', 'col'), pairs)  16.6 us
    ppermute x11, waiting for transfers between devices, send(): return lax.ppermute(value, ('row', 'col'), pairs)  6.32 us
    pallas_call x1, Pallas kernels, grid_path(): pl.pallas_call(first_kernel, out_shape=(jax.ShapeDtypeStruct((wide_cols,...  2.48 us
    pallas_call x2, Pallas kernels, summed(): pl.pallas_call(functools.partial(sum_kernel, bs, odd), out_shape=(2 + odd...  2 us
    pallas_call x1, Pallas kernels, grid_path(): pl.pallas_call(pack_kernel, out_shape=jax.ShapeDtypeStruct((rows + PAD, n...  1.07 us
    pallas_call x1, Pallas kernels, grid_path(): pl.pallas_call(functools.partial(last_kernel, bs), out_shape=jax.ShapeDty...  1 us
    pallas_call x1, Pallas kernels, grid_path(): pl.pallas_call(functools.partial(second_kernel, bs), out_shape=code, in_s...  0.86 us
    pallas_call x1, Pallas kernels, grid_path(): pl.pallas_call(functools.partial(near_kernel, bs), out_shape=both, in_spe...  0.78 us
  transfers between devices with their start and end apart: 11, of which 3 were waited for; matrix products, arithmetic and copies ran while one was open for 0% of the time, Pallas kernels for 22%

profile of v4, /device:TPU:0, one launch (start us, length us, event | category | flops | bytes accessed | tf_op | source)
XLA Modules:
  0.0 31.9 jit_solution(5130125227869420068)
XLA Ops:
  0.0 1.1 %pack.1.packed_ref = bf16[144,512]{1,0:T(8,128)(2,1)S(1)} custom-call(s32[1,1,2,8]{3,2,1,0:T(2,128)} %cols_hbm.1, bf16[1,1,2,8,64,64]{5,4,3,2,1,0:T(8,128)(2,1)} %left_hbm.1), custom_call_target="tpu_custom_call" | custom-call | tf_op jit(solution)/shard_map/pack/pallas_call | solution.py:267
  1.1 3.0 %collective-permute-start.2 = (bf16[144,512]{1,0:T(8,128)(2,1)S(1)}, bf16[144,512]{1,0:T(8,128)(2,1)S(1)}, u32[]{:S(2)}, u32[]{:S(2)}) collective-permute-start(bf16[144,512]{1,0:T(8,128)(2,1)S(1)} %pack.1.packed_ref), channel_id=1, source_target_pairs={{0,16},{1,17},{2,18},{3,19},{4,20},{5,21},{6,22},{7,23},{8,24},{9,... | collective-permute-start | bytes 442376 | tf_op jit(solution)/shard_map/ppermute | solution.py:254
  4.1 0.0 copy-start
  4.1 2.5 %first.1 = (bf16[8,1024,128]{2,1,0:T(8,128)(2,1)S(1)}, s16[1040,128]{1,0:T(8,128)(2,1)S(1)}) custom-call(s32[1,6,1,16]{3,2,1,0:T(1,128)} %bitcast.1, bf16[1,1,16,6,64,64]{5,4,3,2,1,0:T(8,128)(2,1)} %right_hbm.1, bf16[144,512]{1,0:T(8,128)(2,1)S(1)} %pack.1.packed_ref), custom_call_target="tpu_custom_call" | custom-call | tf_op jit(solution)/shard_map/first/pallas_call | solution.py:281
  6.6 1.6 %collective-permute-start.5 = (s16[1040,128]{1,0:T(8,128)(2,1)S(1)}, s16[1040,128]{1,0:T(8,128)(2,1)S(1)}, u32[]{:S(2)}, u32[]{:S(2)}) collective-permute-start(s16[1040,128]{1,0:T(8,128)(2,1)S(1)} %get-tuple-element.17), channel_id=1, source_target_pairs={{0,1},{1,0},{2,3},{3,2},{4,5},{5,4},{6,7},{7,6},{8,9},{9,8},{10,11... | collective-permute-start | bytes 798728 | tf_op jit(solution)/shard_map/ppermute | solution.py:254
  8.2 0.0 collective-permute-start.4
  8.2 0.0 collective-permute-done.2.packed_ref
  8.2 0.5 %collective-permute-start.3 = (bf16[144,512]{1,0:T(8,128)(2,1)S(1)}, bf16[144,512]{1,0:T(8,128)(2,1)S(1)}, u32[]{:S(2)}, u32[]{:S(2)}) collective-permute-start(bf16[144,512]{1,0:T(8,128)(2,1)S(1)} %collective-permute-done.2.packed_ref), channel_id=1, source_target_pairs={{0,8},{1,9},{2,10},{3,11},{4,12},{5,13},{6,14},{7,15},{8,0},{9,1},... | collective-permute-start | bytes 442376 | tf_op jit(solution)/shard_map/ppermute | solution.py:254
  8.7 0.9 %second.1 = s16[1040,128]{1,0:T(8,128)(2,1)S(1)} custom-call(bf16[8,1024,128]{2,1,0:T(8,128)(2,1)S(1)} %get-tuple-element.15.dense_ref, bf16[144,512]{1,0:T(8,128)(2,1)S(1)} %collective-permute-done.2.packed_ref), custom_call_target="tpu_custom_call" | custom-call | tf_op jit(solution)/shard_map/second/pallas_call | solution.py:312
  9.5 1.1 %collective-permute-start.8 = (s16[1040,128]{1,0:T(8,128)(2,1)S(1)}, s16[1040,128]{1,0:T(8,128)(2,1)S(1)}, u32[]{:S(2)}, u32[]{:S(2)}) collective-permute-start(s16[1040,128]{1,0:T(8,128)(2,1)S(1)} %second.1), channel_id=1, source_target_pairs={{0,1},{1,0},{2,3},{3,2},{4,5},{5,4},{6,7},{7,6},{8,9},{9,8},{10,11... | collective-permute-start | bytes 798728 | tf_op jit(solution)/shard_map/ppermute | solution.py:254
  10.6 0.0 copy-done
  10.6 1.6 %collective-permute-start = (s32[1,1,2,8]{3,2,1,0:T(2,128)S(1)}, s32[1,1,2,8]{3,2,1,0:T(2,128)S(1)}, u32[]{:S(2)}, u32[]{:S(2)}) collective-permute-start(s32[1,1,2,8]{3,2,1,0:T(2,128)S(1)} %copy-done), channel_id=1, source_target_pairs={{0,2},{1,3},{2,0},{3,1},{4,6},{5,7},{6,4},{7,5},{8,10},{9,11},{10,... | collective-permute-start | bytes 200 | tf_op jit(solution)/shard_map/ppermute | solution.py:254
  12.2 0.0 collective-permute-done.4.packed_ref
  12.2 2.6 %collective-permute-start.1 = (s32[1,1,2,8]{3,2,1,0:T(2,128)S(1)}, s32[1,1,2,8]{3,2,1,0:T(2,128)S(1)}, u32[]{:S(2)}, u32[]{:S(2)}) collective-permute-start(s32[1,1,2,8]{3,2,1,0:T(2,128)S(1)} %copy-done), channel_id=1, source_target_pairs={{0,4},{1,7},{2,6},{3,5},{4,0},{5,3},{6,2},{7,1},{8,12},{9,15},{10,... | collective-permute-start | bytes 200 | tf_op jit(solution)/shard_map/ppermute | solution.py:254
  14.8 0.8 %near.1._ = f32[2,8,128,128]{3,2,1,0:T(8,128)S(1)} custom-call(bf16[8,1024,128]{2,1,0:T(8,128)(2,1)S(1)} %get-tuple-element.15.dense_ref, bf16[144,512]{1,0:T(8,128)(2,1)S(1)} %collective-permute-done.4.packed_ref), custom_call_target="tpu_custom_call" | custom-call | tf_op jit(solution)/shard_map/near/pallas_call | solution.py:302
  15.6 0.0 collective-permute-done.3.packed_ref
  15.6 0.3 collective-permute-start.7
  15.9 0.8 %far.1.kept_ref = f32[2,8,128,128]{3,2,1,0:T(8,128)S(1)} custom-call(bf16[8,1024,128]{2,1,0:T(8,128)(2,1)S(1)} %get-tuple-element.15.dense_ref, bf16[144,512]{1,0:T(8,128)(2,1)S(1)} %collective-permute-done.3.packed_ref, f32[2,8,128,128]{3,2,1,0:T(8,128)S(1)} %near.1._), custom_call_target="tpu_custom_call", output_to_operand_aliasing={{}: (2, {})} | custom-call | tf_op jit(solution)/shard_map/far/pallas_call | solution.py:323
  16.6 0.0 collective-permute-done.one_ref
  16.6 0.0 collective-permute-done.1.far_ref
  16.7 0.0 collective-permute-done.5.code_ref
  16.7 1.0 %sum.2 = (s16[528,128]{1,0:T(8,128)(2,1)S(1)}, s16[528,128]{1,0:T(8,128)(2,1)S(1)}) custom-call(s32[1,1,2,8]{3,2,1,0:T(2,128)S(1)} %copy-done, s32[1,1,2,8]{3,2,1,0:T(2,128)S(1)} %collective-permute-done.one_ref, s32[1,1,2,8]{3,2,1,0:T(2,128)S(1)} %collective-permute-done.1.far_ref, f32[2,8,128,128]{3,2,1,0:T(8,128)S(1)} %far.1.kept_ref, ...), custom_call_target="tpu_custom_call" | custom-call | flops 2000000000 | bytes 20000000 | tf_op jit(solution)/shard_map/sum/pallas_call | solution.py:337
  17.7 2.6 %collective-permute-start.6 = (s16[528,128]{1,0:T(8,128)(2,1)S(1)}, s16[528,128]{1,0:T(8,128)(2,1)S(1)}, u32[]{:S(2)}, u32[]{:S(2)}) collective-permute-start(s16[528,128]{1,0:T(8,128)(2,1)S(1)} %get-tuple-element.18), channel_id=1, source_target_pairs={{0,4},{1,7},{2,6},{3,5},{4,0},{5,3},{6,2},{7,1},{8,12},{9,15},{10,... | collective-permute-start | bytes 405512 | tf_op jit(solution)/shard_map/ppermute | solution.py:254
  20.3 0.7 %collective-permute-done.7.far_ref = s32[1,1,2,8]{3,2,1,0:T(2,128)S(1)} collective-permute-done((s32[1,1,2,8]{3,2,1,0:T(2,128)S(1)}, s32[1,1,2,8]{3,2,1,0:T(2,128)S(1)}, u32[]{:S(2)}, u32[]{:S(2)}) %collective-permute-start.7) | collective-permute-done | bytes 96 | tf_op jit(solution)/shard_map/ppermute | solution.py:254
  21.0 0.0 collective-permute-done.8.code_ref
  21.0 1.0 %sum.3 = (s16[528,128]{1,0:T(8,128)(2,1)S(1)}, s16[528,128]{1,0:T(8,128)(2,1)S(1)}, s16[528,128]{1,0:T(8,128)(2,1)S(1)}) custom-call(s32[1,1,2,8]{3,2,1,0:T(2,128)S(1)} %copy-done, s32[1,1,2,8]{3,2,1,0:T(2,128)S(1)} %collective-permute-done.one_ref, s32[1,1,2,8]{3,2,1,0:T(2,128)S(1)} %collective-permute-done.7.far_ref, f32[2,8,128,128]{3,2,1,0:T(8,128)S(1)} %far.1.kept_ref, ...), custom_call_target="tpu_custom_call" | custom-call | tf_op jit(solution)/shard_map/sum/pallas_call | solution.py:337
  22.0 0.9 %collective-permute-start.10 = (s16[528,128]{1,0:T(8,128)(2,1)S(1)}, s16[528,128]{1,0:T(8,128)(2,1)S(1)}, u32[]{:S(2)}, u32[]{:S(2)}) collective-permute-start(s16[528,128]{1,0:T(8,128)(2,1)S(1)} %get-tuple-element.21), channel_id=1, source_target_pairs={{0,2},{1,3},{2,0},{3,1},{4,6},{5,7},{6,4},{7,5},{8,10},{9,11},{10,... | collective-permute-start | bytes 405512 | tf_op jit(solution)/shard_map/ppermute | solution.py:254
  23.0 2.4 %collective-permute-start.9 = (s16[528,128]{1,0:T(8,128)(2,1)S(1)}, s16[528,128]{1,0:T(8,128)(2,1)S(1)}, u32[]{:S(2)}, u32[]{:S(2)}) collective-permute-start(s16[528,128]{1,0:T(8,128)(2,1)S(1)} %get-tuple-element.20), channel_id=1, source_target_pairs={{0,6},{1,5},{2,4},{3,7},{4,2},{5,1},{6,0},{7,3},{8,14},{9,13},{10,... | collective-permute-start | bytes 405512 | tf_op jit(solution)/shard_map/ppermute | solution.py:254
  25.4 3.6 %collective-permute-done.6.a_ref = s16[528,128]{1,0:T(8,128)(2,1)S(1)} collective-permute-done((s16[528,128]{1,0:T(8,128)(2,1)S(1)}, s16[528,128]{1,0:T(8,128)(2,1)S(1)}, u32[]{:S(2)}, u32[]{:S(2)}) %collective-permute-start.6) | collective-permute-done | bytes 135200 | tf_op jit(solution)/shard_map/ppermute | solution.py:254
  29.0 2.0 %collective-permute-done.10.c_ref = s16[528,128]{1,0:T(8,128)(2,1)S(1)} collective-permute-done((s16[528,128]{1,0:T(8,128)(2,1)S(1)}, s16[528,128]{1,0:T(8,128)(2,1)S(1)}, u32[]{:S(2)}, u32[]{:S(2)}) %collective-permute-start.10) | collective-permute-done | bytes 135200 | tf_op jit(solution)/shard_map/ppermute | solution.py:254
  30.9 0.0 collective-permute-done.9.b_ref
  30.9 1.0 %last.1 = f32[1,1,2,8,64,64]{5,4,3,2,1,0:T(8,128)} custom-call(s16[528,128]{1,0:T(8,128)(2,1)S(1)} %collective-permute-done.6.a_ref, s16[528,128]{1,0:T(8,128)(2,1)S(1)} %collective-permute-done.9.b_ref, s16[528,128]{1,0:T(8,128)(2,1)S(1)} %collective-permute-done.10.c_ref, s16[528,128]{1,0:T(8,128)(2,1)S(1)} %get-tuple-element.22.own_ref), custom_call_target="tpu_custom_call" | custom-call | tf_op jit(solution)/shard_map/last/pallas_call | solution.py:352
Async XLA Ops:
  1.1 7.1 %collective-permute-start.2 = (bf16[144,512]{1,0:T(8,128)(2,1)S(1)}, bf16[144,512]{1,0:T(8,128)(2,1)S(1)}, u32[]{:S(2)}, u32[]{:S(2)}) collective-permute-start(bf16[144,512]{1,0:T(8,128)(2,1)S(1)} %pack.1.packed_ref), channel_id=1, source_target_pairs={{0,16},{1,17},{2,18},{3,19},{4,20},{5,21},{6,22},{7,23},{8,24},{9,... | collective-permute-start | bytes 442376 | tf_op jit(solution)/shard_map/ppermute | solution.py:254
  4.1 6.5 %copy-start = (s32[1,1,2,8]{3,2,1,0:T(2,128)S(1)}, s32[1,1,2,8]{3,2,1,0:T(2,128)}, u32[]{:S(2)}) copy-start(s32[1,1,2,8]{3,2,1,0:T(2,128)} %own_ref.3) | copy-start | bytes 196
  6.6 10.1 %collective-permute-start.5 = (s16[1040,128]{1,0:T(8,128)(2,1)S(1)}, s16[1040,128]{1,0:T(8,128)(2,1)S(1)}, u32[]{:S(2)}, u32[]{:S(2)}) collective-permute-start(s16[1040,128]{1,0:T(8,128)(2,1)S(1)} %get-tuple-element.17), channel_id=1, source_target_pairs={{0,1},{1,0},{2,3},{3,2},{4,5},{5,4},{6,7},{7,6},{8,9},{9,8},{10,11... | collective-permute-start | bytes 798728 | tf_op jit(solution)/shard_map/ppermute | solution.py:254
  8.2 4.0 %collective-permute-start.4 = (bf16[144,512]{1,0:T(8,128)(2,1)S(1)}, bf16[144,512]{1,0:T(8,128)(2,1)S(1)}, u32[]{:S(2)}, u32[]{:S(2)}) collective-permute-start(bf16[144,512]{1,0:T(8,128)(2,1)S(1)} %pack.1.packed_ref), channel_id=1, source_target_pairs={{0,8},{1,9},{2,10},{3,11},{4,12},{5,13},{6,14},{7,15},{8,0},{9,1},... | collective-permute-start | bytes 442376 | tf_op jit(solution)/shard_map/ppermute | solution.py:254
  8.2 7.4 %collective-permute-start.3 = (bf16[144,512]{1,0:T(8,128)(2,1)S(1)}, bf16[144,512]{1,0:T(8,128)(2,1)S(1)}, u32[]{:S(2)}, u32[]{:S(2)}) collective-permute-start(bf16[144,512]{1,0:T(8,128)(2,1)S(1)} %collective-permute-done.2.packed_ref), channel_id=1, source_target_pairs={{0,8},{1,9},{2,10},{3,11},{4,12},{5,13},{6,14},{7,15},{8,0},{9,1},... | collective-permute-start | bytes 442376 | tf_op jit(solution)/shard_map/ppermute | solution.py:254
  9.5 11.5 %collective-permute-start.8 = (s16[1040,128]{1,0:T(8,128)(2,1)S(1)}, s16[1040,128]{1,0:T(8,128)(2,1)S(1)}, u32[]{:S(2)}, u32[]{:S(2)}) collective-permute-start(s16[1040,128]{1,0:T(8,128)(2,1)S(1)} %second.1), channel_id=1, source_target_pairs={{0,1},{1,0},{2,3},{3,2},{4,5},{5,4},{6,7},{7,6},{8,9},{9,8},{10,11... | collective-permute-start | bytes 798728 | tf_op jit(solution)/shard_map/ppermute | solution.py:254
  10.6 6.0 %collective-permute-start = (s32[1,1,2,8]{3,2,1,0:T(2,128)S(1)}, s32[1,1,2,8]{3,2,1,0:T(2,128)S(1)}, u32[]{:S(2)}, u32[]{:S(2)}) collective-permute-start(s32[1,1,2,8]{3,2,1,0:T(2,128)S(1)} %copy-done), channel_id=1, source_target_pairs={{0,2},{1,3},{2,0},{3,1},{4,6},{5,7},{6,4},{7,5},{8,10},{9,11},{10,... | collective-permute-start | bytes 200 | tf_op jit(solution)/shard_map/ppermute | solution.py:254
  12.2 4.5 %collective-permute-start.1 = (s32[1,1,2,8]{3,2,1,0:T(2,128)S(1)}, s32[1,1,2,8]{3,2,1,0:T(2,128)S(1)}, u32[]{:S(2)}, u32[]{:S(2)}) collective-permute-start(s32[1,1,2,8]{3,2,1,0:T(2,128)S(1)} %copy-done), channel_id=1, source_target_pairs={{0,4},{1,7},{2,6},{3,5},{4,0},{5,3},{6,2},{7,1},{8,12},{9,15},{10,... | collective-permute-start | bytes 200 | tf_op jit(solution)/shard_map/ppermute | solution.py:254
  15.6 5.4 %collective-permute-start.7 = (s32[1,1,2,8]{3,2,1,0:T(2,128)S(1)}, s32[1,1,2,8]{3,2,1,0:T(2,128)S(1)}, u32[]{:S(2)}, u32[]{:S(2)}) collective-permute-start(s32[1,1,2,8]{3,2,1,0:T(2,128)S(1)} %copy-done), channel_id=1, source_target_pairs={{0,6},{1,5},{2,4},{3,7},{4,2},{5,1},{6,0},{7,3},{8,14},{9,13},{10,... | collective-permute-start | bytes 200 | tf_op jit(solution)/shard_map/ppermute | solution.py:254
  17.7 11.3 %collective-permute-start.6 = (s16[528,128]{1,0:T(8,128)(2,1)S(1)}, s16[528,128]{1,0:T(8,128)(2,1)S(1)}, u32[]{:S(2)}, u32[]{:S(2)}) collective-permute-start(s16[528,128]{1,0:T(8,128)(2,1)S(1)} %get-tuple-element.18), channel_id=1, source_target_pairs={{0,4},{1,7},{2,6},{3,5},{4,0},{5,3},{6,2},{7,1},{8,12},{9,15},{10,... | collective-permute-start | bytes 405512 | tf_op jit(solution)/shard_map/ppermute | solution.py:254
  22.0 8.9 %collective-permute-start.10 = (s16[528,128]{1,0:T(8,128)(2,1)S(1)}, s16[528,128]{1,0:T(8,128)(2,1)S(1)}, u32[]{:S(2)}, u32[]{:S(2)}) collective-permute-start(s16[528,128]{1,0:T(8,128)(2,1)S(1)} %get-tuple-element.21), channel_id=1, source_target_pairs={{0,2},{1,3},{2,0},{3,1},{4,6},{5,7},{6,4},{7,5},{8,10},{9,11},{10,... | collective-permute-start | bytes 405512 | tf_op jit(solution)/shard_map/ppermute | solution.py:254
  23.0 8.0 %collective-permute-start.9 = (s16[528,128]{1,0:T(8,128)(2,1)S(1)}, s16[528,128]{1,0:T(8,128)(2,1)S(1)}, u32[]{:S(2)}, u32[]{:S(2)}) collective-permute-start(s16[528,128]{1,0:T(8,128)(2,1)S(1)} %get-tuple-element.20), channel_id=1, source_target_pairs={{0,6},{1,5},{2,4},{3,7},{4,2},{5,1},{6,0},{7,3},{8,14},{9,13},{10,... | collective-permute-start | bytes 405512 | tf_op jit(solution)/shard_map/ppermute | solution.py:254

commit v5 on v4

--- a/solution.py
+++ b/solution.py
@@ -74,15 +74,15 @@
 
 def spread_left(packed_ref, rows, half, dense_ref):
     side = lax.broadcasted_iota(jnp.int32, (1, LANES), 1) // half
-    index = packed_ref[rows : rows + PAD, :].astype(jnp.float32)
+    count = packed_ref.shape[0] // rows
+    index = packed_ref[count * rows :].astype(jnp.float32)
     for i in range(rows // half):
         here, there, data, turned = [], [], [], []
-        for b in range(packed_ref.shape[1] // LANES):
-            lanes = slice(b * LANES, (b + 1) * LANES)
-            column = index[i : i + 1, lanes].astype(jnp.int32)
+        for b in range(count):
+            column = index[i * count + b : i * count + b + 1].astype(jnp.int32)
             here.append(jnp.broadcast_to(column - side, (PAD, LANES)))
             there.append(jnp.broadcast_to(pltpu.roll(column, half, 1) - side, (PAD, LANES)))
-            data.append(packed_ref[i * half : (i + 1) * half, lanes])
+            data.append(packed_ref[b * rows + i * half : b * rows + (i + 1) * half])
             turned.append(pltpu.roll(data[-1], half, 1))
         for m in range(dense_ref.shape[1] // LANES):
             masks = [(h == 2 * m, t == 2 * m) for h, t in zip(here, there)]
@@ -118,27 +118,26 @@
 
 def pack_kernel(cols_hbm, left_hbm, packed_ref, cols_ref, left_ref, sem):
     ib, nl, half, _ = left_ref.shape
-    rows = ib * half
-    copies = [
-        pltpu.make_async_copy(cols_hbm, cols_ref, sem.at[0]),
-        pltpu.make_async_copy(left_hbm.at[0, 0], left_ref, sem.at[1]),
-    ]
+    rows, count = ib * half, nl // 2
+    copies = [pltpu.make_async_copy(cols_hbm, cols_ref, sem.at[ib])]
+    for i in range(ib):
+        copies.append(pltpu.make_async_copy(left_hbm.at[0, 0, i], left_ref.at[i], sem.at[i]))
     for copy in copies:
         copy.start()
     side = lax.broadcasted_iota(jnp.int32, (PAD, LANES), 1) // half
     row = lax.broadcasted_iota(jnp.int32, (PAD, LANES), 0)
+    index = jnp.zeros((PAD, LANES), jnp.int32)
     copies[0].wait()
-    for b in range(nl // 2):
-        index = jnp.zeros((PAD, LANES), jnp.int32)
-        for i in range(ib):
+    for i in range(ib):
+        for b in range(count):
             cols = jnp.where(side == 0, cols_ref[0, 0, i, 2 * b], cols_ref[0, 0, i, 2 * b + 1])
-            index = jnp.where(row == i, cols, index)
-        packed_ref[rows:, b * LANES : (b + 1) * LANES] = index.astype(jnp.float32).astype(jnp.bfloat16)
-    copies[1].wait()
-    for b in range(nl // 2):
-        for i in range(ib):
+            index = jnp.where(row == i * count + b, cols, index)
+    packed_ref[count * rows :] = index.astype(jnp.float32).astype(jnp.bfloat16)
+    for i in range(ib):
+        copies[1 + i].wait()
+        for b in range(count):
             pair = jnp.concatenate([left_ref[i, 2 * b], left_ref[i, 2 * b + 1]], axis=1)
-            packed_ref[i * half : (i + 1) * half, b * LANES : (b + 1) * LANES] = pair
+            packed_ref[b * rows + i * half : b * rows + (i + 1) * half] = pair
 
 
 def first_kernel(
@@ -175,18 +174,14 @@
     return (lax.axis_index("col") + lax.axis_index("row")) % 2
 
 
-def near_kernel(half, dense_ref, packed_ref, kept_ref, left_ref):
-    spread_left(packed_ref, left_ref.shape[0], half, left_ref)
+def kept_kernel(half, dense_ref, near_ref, far_ref, kept_ref, left_ref):
+    _, _, rows, _ = kept_ref.shape
+    spread_left(near_ref, rows, half, left_ref.at[:rows])
+    spread_left(far_ref, rows, half, left_ref.at[rows:])
     slot = swapped()
     for m, part in enumerate(product(left_ref[...], dense_ref)):
-        kept_ref[slot, m] = part
-
-
-def far_kernel(half, dense_ref, packed_ref, _, kept_ref, left_ref):
-    spread_left(packed_ref, left_ref.shape[0], half, left_ref)
-    slot = 1 - swapped()
-    for m, part in enumerate(product(left_ref[...], dense_ref)):
-        kept_ref[slot, m] = part
+        kept_ref[slot, m] = part[:rows]
+        kept_ref[1 - slot, m] = part[rows:]
 
 
 def sum_kernel(half, odd, own_ref, one_ref, far_ref, kept_ref, code_ref, *refs):
@@ -266,13 +261,13 @@
 
     packed = pl.pallas_call(
         pack_kernel,
-        out_shape=jax.ShapeDtypeStruct((rows + PAD, nl * bs), jnp.bfloat16),
+        out_shape=jax.ShapeDtypeStruct((nl * bs // LANES * rows + PAD, LANES), jnp.bfloat16),
         in_specs=[HBM] * 2,
         out_specs=VMEM,
         scratch_shapes=[
             pltpu.SMEM(left_cols.shape[:2] + (ib, nl), jnp.int32),
             pltpu.VMEM(left_blocks.shape[2:], jnp.bfloat16),
-            pltpu.SemaphoreType.DMA((2,)),
+            pltpu.SemaphoreType.DMA((ib + 1,)),
         ],
         compiler_params=PARAMS,
         name="pack",
@@ -299,15 +294,6 @@
     across = send(packed, lambda r, c: ((r + 2) % n_row, c))
     dense, packed = lax.optimization_barrier((dense, packed))
     near = send(packed, lambda r, c: (r ^ 1, c))
-    kept = pl.pallas_call(
-        functools.partial(near_kernel, bs),
-        out_shape=both,
-        in_specs=[VMEM] * 2,
-        out_specs=VMEM,
-        scratch_shapes=[left_scratch],
-        compiler_params=PARAMS,
-        name="near",
-    )(dense, near)
     far = send(across, lambda r, c: (r ^ 1, c))
     code_two = pl.pallas_call(
         functools.partial(second_kernel, bs),
@@ -321,15 +307,14 @@
     far_cols = (send(out_cols, along(2, 3)), send(out_cols, along(3, 2)))
     got_two = send(code_two, lambda r, c: (r, c ^ 1))
     kept = pl.pallas_call(
-        functools.partial(far_kernel, bs),
+        functools.partial(kept_kernel, bs),
         out_shape=both,
-        in_specs=[VMEM, VMEM, HBM],
+        in_specs=[VMEM] * 3,
         out_specs=VMEM,
-        scratch_shapes=[left_scratch],
-        input_output_aliases={2: 0},
-        compiler_params=PARAMS,
-        name="far",
-    )(dense, far, kept)
+        scratch_shapes=[pltpu.VMEM((2 * rows, kb * bs), jnp.bfloat16)],
+        compiler_params=PARAMS,
+        name="kept",
+    )(dense, near, far)
 
     def summed(odd, code, *held):
         scratch = [pltpu.VMEM((2 * wide_cols, rows, LANES), jnp.float32)]

time: 32.1 us -> 31.7 us (0.988)
  waiting for transfers between devices: 6.32 us -> 5.63 us
  starting transfers between devices: 16.6 us -> 17 us
    ppermute x11, waiting for transfers between devices: 6.32 us -> 5.63 us  [send(): return lax.ppermute(value, ('row', 'col'), pairs)]
    ppermute x11, starting transfers between devices: 16.6 us -> 17 us  [send(): return lax.ppermute(value, ('row', 'col'), pairs)]
    pallas_call x3 -> x2, Pallas kernels: 2.62 us -> 2.43 us  [the longest x1 1.33 us: grid_path(): pl.pallas_call(functools.partial(kept_kernel, bs), out_shape=both, in_spe...]
  transfers between devices with their start and end apart: 11 -> 11, of which waited for: 3 -> 5; matrix products, arithmetic and copies ran while one was open for 0% -> 0% of each run, Pallas kernels for 22% -> 21%
where the time goes in v5:
time: 31.7 us; the launch traced here: 31.5 us
  starting transfers between devices  17 us (54%)
  Pallas kernels  8.79 us (28%)
  waiting for transfers between devices  5.63 us (18%)
    ppermute x11, starting transfers between devices, send(): return lax.ppermute(value, ('row', 'col'), pairs)  17 us
    ppermute x11, waiting for transfers between devices, send(): return lax.ppermute(value, ('row', 'col'), pairs)  5.63 us
    pallas_call x1, Pallas kernels, grid_path(): pl.pallas_call(first_kernel, out_shape=(jax.ShapeDtypeStruct((wide_cols,...  2.49 us
    pallas_call x2, Pallas kernels, summed(): pl.pallas_call(functools.partial(sum_kernel, bs, odd), out_shape=(2 + odd...  1.99 us
    pallas_call x1, Pallas kernels, grid_path(): pl.pallas_call(functools.partial(kept_kernel, bs), out_shape=both, in_spe...  1.33 us
    pallas_call x1, Pallas kernels, grid_path(): pl.pallas_call(pack_kernel, out_shape=jax.ShapeDtypeStruct((nl * bs // LA...  1.1 us
    pallas_call x1, Pallas kernels, grid_path(): pl.pallas_call(functools.partial(last_kernel, bs), out_shape=jax.ShapeDty...  1 us
    pallas_call x1, Pallas kernels, grid_path(): pl.pallas_call(functools.partial(second_kernel, bs), out_shape=code, in_s...  0.87 us
  transfers between devices with their start and end apart: 11, of which 5 were waited for; matrix products, arithmetic and copies ran while one was open for 0% of the time, Pallas kernels for 21%

profile of v5, /device:TPU:0, one launch (start us, length us, event | category | flops | bytes accessed | tf_op | source)
XLA Modules:
  0.0 31.5 jit_solution(4916319907698878879)
XLA Ops:
  0.0 1.1 %pack.1.packed_ref = bf16[528,128]{1,0:T(8,128)(2,1)S(1)} custom-call(s32[1,1,2,8]{3,2,1,0:T(2,128)} %cols_hbm.1, bf16[1,1,2,8,64,64]{5,4,3,2,1,0:T(8,128)(2,1)} %left_hbm.1), custom_call_target="tpu_custom_call" | custom-call | tf_op jit(solution)/shard_map/pack/pallas_call | solution.py:262
  1.1 3.0 %collective-permute-start.3 = (bf16[528,128]{1,0:T(8,128)(2,1)S(1)}, bf16[528,128]{1,0:T(8,128)(2,1)S(1)}, u32[]{:S(2)}, u32[]{:S(2)}) collective-permute-start(bf16[528,128]{1,0:T(8,128)(2,1)S(1)} %pack.1.packed_ref), channel_id=1, source_target_pairs={{0,16},{1,17},{2,18},{3,19},{4,20},{5,21},{6,22},{7,23},{8,24},{9,... | collective-permute-start | bytes 405512 | tf_op jit(solution)/shard_map/ppermute | solution.py:249
  4.1 0.0 copy-start
  4.1 2.5 %first.1 = (bf16[8,1024,128]{2,1,0:T(8,128)(2,1)S(1)}, s16[1040,128]{1,0:T(8,128)(2,1)S(1)}) custom-call(s32[1,6,1,16]{3,2,1,0:T(1,128)} %bitcast.1, bf16[1,1,16,6,64,64]{5,4,3,2,1,0:T(8,128)(2,1)} %right_hbm.1, bf16[528,128]{1,0:T(8,128)(2,1)S(1)} %pack.1.packed_ref), custom_call_target="tpu_custom_call" | custom-call | tf_op jit(solution)/shard_map/first/pallas_call | solution.py:276
  6.6 1.6 %collective-permute-start.5 = (s16[1040,128]{1,0:T(8,128)(2,1)S(1)}, s16[1040,128]{1,0:T(8,128)(2,1)S(1)}, u32[]{:S(2)}, u32[]{:S(2)}) collective-permute-start(s16[1040,128]{1,0:T(8,128)(2,1)S(1)} %get-tuple-element.17), channel_id=1, source_target_pairs={{0,1},{1,0},{2,3},{3,2},{4,5},{5,4},{6,7},{7,6},{8,9},{9,8},{10,11... | collective-permute-start | bytes 798728 | tf_op jit(solution)/shard_map/ppermute | solution.py:249
  8.2 0.0 collective-permute-start.2
  8.2 0.0 collective-permute-done.3.packed_ref
  8.2 0.5 %collective-permute-start.4 = (bf16[528,128]{1,0:T(8,128)(2,1)S(1)}, bf16[528,128]{1,0:T(8,128)(2,1)S(1)}, u32[]{:S(2)}, u32[]{:S(2)}) collective-permute-start(bf16[528,128]{1,0:T(8,128)(2,1)S(1)} %collective-permute-done.3.packed_ref), channel_id=1, source_target_pairs={{0,8},{1,9},{2,10},{3,11},{4,12},{5,13},{6,14},{7,15},{8,0},{9,1},... | collective-permute-start | bytes 405512 | tf_op jit(solution)/shard_map/ppermute | solution.py:249
  8.7 0.9 %second.1 = s16[1040,128]{1,0:T(8,128)(2,1)S(1)} custom-call(bf16[8,1024,128]{2,1,0:T(8,128)(2,1)S(1)} %get-tuple-element.15.dense_ref, bf16[528,128]{1,0:T(8,128)(2,1)S(1)} %collective-permute-done.3.packed_ref), custom_call_target="tpu_custom_call" | custom-call | tf_op jit(solution)/shard_map/second/pallas_call | solution.py:298
  9.6 0.8 %collective-permute-start.8 = (s16[1040,128]{1,0:T(8,128)(2,1)S(1)}, s16[1040,128]{1,0:T(8,128)(2,1)S(1)}, u32[]{:S(2)}, u32[]{:S(2)}) collective-permute-start(s16[1040,128]{1,0:T(8,128)(2,1)S(1)} %second.1), channel_id=1, source_target_pairs={{0,1},{1,0},{2,3},{3,2},{4,5},{5,4},{6,7},{7,6},{8,9},{9,8},{10,11... | collective-permute-start | bytes 798728 | tf_op jit(solution)/shard_map/ppermute | solution.py:249
  10.4 0.0 copy-done
  10.4 1.6 %collective-permute-start = (s32[1,1,2,8]{3,2,1,0:T(2,128)S(1)}, s32[1,1,2,8]{3,2,1,0:T(2,128)S(1)}, u32[]{:S(2)}, u32[]{:S(2)}) collective-permute-start(s32[1,1,2,8]{3,2,1,0:T(2,128)S(1)} %copy-done), channel_id=1, source_target_pairs={{0,2},{1,3},{2,0},{3,1},{4,6},{5,7},{6,4},{7,5},{8,10},{9,11},{10,... | collective-permute-start | bytes 200 | tf_op jit(solution)/shard_map/ppermute | solution.py:249
  12.0 0.0 collective-permute-done.2.near_ref
  12.0 2.6 %collective-permute-start.1 = (s32[1,1,2,8]{3,2,1,0:T(2,128)S(1)}, s32[1,1,2,8]{3,2,1,0:T(2,128)S(1)}, u32[]{:S(2)}, u32[]{:S(2)}) collective-permute-start(s32[1,1,2,8]{3,2,1,0:T(2,128)S(1)} %copy-done), channel_id=1, source_target_pairs={{0,4},{1,7},{2,6},{3,5},{4,0},{5,3},{6,2},{7,1},{8,12},{9,15},{10,... | collective-permute-start | bytes 200 | tf_op jit(solution)/shard_map/ppermute | solution.py:249
  14.6 0.0 collective-permute-done.4.far_ref
  14.6 0.2 collective-permute-start.7
  14.8 1.3 %kept.1.kept_ref = f32[2,8,128,128]{3,2,1,0:T(8,128)S(1)} custom-call(bf16[8,1024,128]{2,1,0:T(8,128)(2,1)S(1)} %get-tuple-element.15.dense_ref, bf16[528,128]{1,0:T(8,128)(2,1)S(1)} %collective-permute-done.2.near_ref, bf16[528,128]{1,0:T(8,128)(2,1)S(1)} %collective-permute-done.4.far_ref), custom_call_target="tpu_custom_call" | custom-call | tf_op jit(solution)/shard_map/kept/pallas_call | solution.py:309
  16.1 0.0 collective-permute-done.one_ref
  16.1 0.3 collective-permute-done.1.far_ref
  16.4 0.0 collective-permute-done.5.code_ref
  16.4 1.0 %sum.2 = (s16[528,128]{1,0:T(8,128)(2,1)S(1)}, s16[528,128]{1,0:T(8,128)(2,1)S(1)}) custom-call(s32[1,1,2,8]{3,2,1,0:T(2,128)S(1)} %copy-done, s32[1,1,2,8]{3,2,1,0:T(2,128)S(1)} %collective-permute-done.one_ref, s32[1,1,2,8]{3,2,1,0:T(2,128)S(1)} %collective-permute-done.1.far_ref, f32[2,8,128,128]{3,2,1,0:T(8,128)S(1)} %kept.1.kept_ref, ...), custom_call_target="tpu_custom_call" | custom-call | flops 2000000000 | bytes 20000000 | tf_op jit(solution)/shard_map/sum/pallas_call | solution.py:322
  17.4 2.7 %collective-permute-start.6 = (s16[528,128]{1,0:T(8,128)(2,1)S(1)}, s16[528,128]{1,0:T(8,128)(2,1)S(1)}, u32[]{:S(2)}, u32[]{:S(2)}) collective-permute-start(s16[528,128]{1,0:T(8,128)(2,1)S(1)} %get-tuple-element.18), channel_id=1, source_target_pairs={{0,4},{1,7},{2,6},{3,5},{4,0},{5,3},{6,2},{7,1},{8,12},{9,15},{10,... | collective-permute-start | bytes 405512 | tf_op jit(solution)/shard_map/ppermute | solution.py:249
  20.1 0.0 collective-permute-done.7.far_ref
  20.1 0.2 collective-permute-done.8.code_ref
  20.3 1.0 %sum.3 = (s16[528,128]{1,0:T(8,128)(2,1)S(1)}, s16[528,128]{1,0:T(8,128)(2,1)S(1)}, s16[528,128]{1,0:T(8,128)(2,1)S(1)}) custom-call(s32[1,1,2,8]{3,2,1,0:T(2,128)S(1)} %copy-done, s32[1,1,2,8]{3,2,1,0:T(2,128)S(1)} %collective-permute-done.one_ref, s32[1,1,2,8]{3,2,1,0:T(2,128)S(1)} %collective-permute-done.7.far_ref, f32[2,8,128,128]{3,2,1,0:T(8,128)S(1)} %kept.1.kept_ref, ...), custom_call_target="tpu_custom_call" | custom-call | tf_op jit(solution)/shard_map/sum/pallas_call | solution.py:322
  21.3 1.6 %collective-permute-start.10 = (s16[528,128]{1,0:T(8,128)(2,1)S(1)}, s16[528,128]{1,0:T(8,128)(2,1)S(1)}, u32[]{:S(2)}, u32[]{:S(2)}) collective-permute-start(s16[528,128]{1,0:T(8,128)(2,1)S(1)} %get-tuple-element.21), channel_id=1, source_target_pairs={{0,2},{1,3},{2,0},{3,1},{4,6},{5,7},{6,4},{7,5},{8,10},{9,11},{10,... | collective-permute-start | bytes 405512 | tf_op jit(solution)/shard_map/ppermute | solution.py:249
  22.9 2.5 %collective-permute-start.9 = (s16[528,128]{1,0:T(8,128)(2,1)S(1)}, s16[528,128]{1,0:T(8,128)(2,1)S(1)}, u32[]{:S(2)}, u32[]{:S(2)}) collective-permute-start(s16[528,128]{1,0:T(8,128)(2,1)S(1)} %get-tuple-element.20), channel_id=1, source_target_pairs={{0,6},{1,5},{2,4},{3,7},{4,2},{5,1},{6,0},{7,3},{8,14},{9,13},{10,... | collective-permute-start | bytes 405512 | tf_op jit(solution)/shard_map/ppermute | solution.py:249
  25.4 3.1 %collective-permute-done.6.a_ref = s16[528,128]{1,0:T(8,128)(2,1)S(1)} collective-permute-done((s16[528,128]{1,0:T(8,128)(2,1)S(1)}, s16[528,128]{1,0:T(8,128)(2,1)S(1)}, u32[]{:S(2)}, u32[]{:S(2)}) %collective-permute-start.6) | collective-permute-done | bytes 135200 | tf_op jit(solution)/shard_map/ppermute | solution.py:249
  28.5 0.4 %collective-permute-done.10.c_ref = s16[528,128]{1,0:T(8,128)(2,1)S(1)} collective-permute-done((s16[528,128]{1,0:T(8,128)(2,1)S(1)}, s16[528,128]{1,0:T(8,128)(2,1)S(1)}, u32[]{:S(2)}, u32[]{:S(2)}) %collective-permute-start.10) | collective-permute-done | bytes 135200 | tf_op jit(solution)/shard_map/ppermute | solution.py:249
  28.9 1.7 %collective-permute-done.9.b_ref = s16[528,128]{1,0:T(8,128)(2,1)S(1)} collective-permute-done((s16[528,128]{1,0:T(8,128)(2,1)S(1)}, s16[528,128]{1,0:T(8,128)(2,1)S(1)}, u32[]{:S(2)}, u32[]{:S(2)}) %collective-permute-start.9) | collective-permute-done | bytes 135200 | tf_op jit(solution)/shard_map/ppermute | solution.py:249
  30.5 1.0 %last.1 = f32[1,1,2,8,64,64]{5,4,3,2,1,0:T(8,128)} custom-call(s16[528,128]{1,0:T(8,128)(2,1)S(1)} %collective-permute-done.6.a_ref, s16[528,128]{1,0:T(8,128)(2,1)S(1)} %collective-permute-done.9.b_ref, s16[528,128]{1,0:T(8,128)(2,1)S(1)} %collective-permute-done.10.c_ref, s16[528,128]{1,0:T(8,128)(2,1)S(1)} %get-tuple-element.22.own_ref), custom_call_target="tpu_custom_call" | custom-call | tf_op jit(solution)/shard_map/last/pallas_call | solution.py:337
Async XLA Ops:
  1.1 7.1 %collective-permute-start.3 = (bf16[528,128]{1,0:T(8,128)(2,1)S(1)}, bf16[528,128]{1,0:T(8,128)(2,1)S(1)}, u32[]{:S(2)}, u32[]{:S(2)}) collective-permute-start(bf16[528,128]{1,0:T(8,128)(2,1)S(1)} %pack.1.packed_ref), channel_id=1, source_target_pairs={{0,16},{1,17},{2,18},{3,19},{4,20},{5,21},{6,22},{7,23},{8,24},{9,... | collective-permute-start | bytes 405512 | tf_op jit(solution)/shard_map/ppermute | solution.py:249
  4.1 6.2 %copy-start = (s32[1,1,2,8]{3,2,1,0:T(2,128)S(1)}, s32[1,1,2,8]{3,2,1,0:T(2,128)}, u32[]{:S(2)}) copy-start(s32[1,1,2,8]{3,2,1,0:T(2,128)} %own_ref.3) | copy-start | bytes 196
  6.6 9.8 %collective-permute-start.5 = (s16[1040,128]{1,0:T(8,128)(2,1)S(1)}, s16[1040,128]{1,0:T(8,128)(2,1)S(1)}, u32[]{:S(2)}, u32[]{:S(2)}) collective-permute-start(s16[1040,128]{1,0:T(8,128)(2,1)S(1)} %get-tuple-element.17), channel_id=1, source_target_pairs={{0,1},{1,0},{2,3},{3,2},{4,5},{5,4},{6,7},{7,6},{8,9},{9,8},{10,11... | collective-permute-start | bytes 798728 | tf_op jit(solution)/shard_map/ppermute | solution.py:249
  8.2 3.8 %collective-permute-start.2 = (bf16[528,128]{1,0:T(8,128)(2,1)S(1)}, bf16[528,128]{1,0:T(8,128)(2,1)S(1)}, u32[]{:S(2)}, u32[]{:S(2)}) collective-permute-start(bf16[528,128]{1,0:T(8,128)(2,1)S(1)} %pack.1.packed_ref), channel_id=1, source_target_pairs={{0,8},{1,9},{2,10},{3,11},{4,12},{5,13},{6,14},{7,15},{8,0},{9,1},... | collective-permute-start | bytes 405512 | tf_op jit(solution)/shard_map/ppermute | solution.py:249
  8.2 6.4 %collective-permute-start.4 = (bf16[528,128]{1,0:T(8,128)(2,1)S(1)}, bf16[528,128]{1,0:T(8,128)(2,1)S(1)}, u32[]{:S(2)}, u32[]{:S(2)}) collective-permute-start(bf16[528,128]{1,0:T(8,128)(2,1)S(1)} %collective-permute-done.3.packed_ref), channel_id=1, source_target_pairs={{0,8},{1,9},{2,10},{3,11},{4,12},{5,13},{6,14},{7,15},{8,0},{9,1},... | collective-permute-start | bytes 405512 | tf_op jit(solution)/shard_map/ppermute | solution.py:249
  9.6 10.7 %collective-permute-start.8 = (s16[1040,128]{1,0:T(8,128)(2,1)S(1)}, s16[1040,128]{1,0:T(8,128)(2,1)S(1)}, u32[]{:S(2)}, u32[]{:S(2)}) collective-permute-start(s16[1040,128]{1,0:T(8,128)(2,1)S(1)} %second.1), channel_id=1, source_target_pairs={{0,1},{1,0},{2,3},{3,2},{4,5},{5,4},{6,7},{7,6},{8,9},{9,8},{10,11... | collective-permute-start | bytes 798728 | tf_op jit(solution)/shard_map/ppermute | solution.py:249
  10.4 5.7 %collective-permute-start = (s32[1,1,2,8]{3,2,1,0:T(2,128)S(1)}, s32[1,1,2,8]{3,2,1,0:T(2,128)S(1)}, u32[]{:S(2)}, u32[]{:S(2)}) collective-permute-start(s32[1,1,2,8]{3,2,1,0:T(2,128)S(1)} %copy-done), channel_id=1, source_target_pairs={{0,2},{1,3},{2,0},{3,1},{4,6},{5,7},{6,4},{7,5},{8,10},{9,11},{10,... | collective-permute-start | bytes 200 | tf_op jit(solution)/shard_map/ppermute | solution.py:249
  12.0 4.5 %collective-permute-start.1 = (s32[1,1,2,8]{3,2,1,0:T(2,128)S(1)}, s32[1,1,2,8]{3,2,1,0:T(2,128)S(1)}, u32[]{:S(2)}, u32[]{:S(2)}) collective-permute-start(s32[1,1,2,8]{3,2,1,0:T(2,128)S(1)} %copy-done), channel_id=1, source_target_pairs={{0,4},{1,7},{2,6},{3,5},{4,0},{5,3},{6,2},{7,1},{8,12},{9,15},{10,... | collective-permute-start | bytes 200 | tf_op jit(solution)/shard_map/ppermute | solution.py:249
  14.6 5.5 %collective-permute-start.7 = (s32[1,1,2,8]{3,2,1,0:T(2,128)S(1)}, s32[1,1,2,8]{3,2,1,0:T(2,128)S(1)}, u32[]{:S(2)}, u32[]{:S(2)}) collective-permute-start(s32[1,1,2,8]{3,2,1,0:T(2,128)S(1)} %copy-done), channel_id=1, source_target_pairs={{0,6},{1,5},{2,4},{3,7},{4,2},{5,1},{6,0},{7,3},{8,14},{9,13},{10,... | collective-permute-start | bytes 200 | tf_op jit(solution)/shard_map/ppermute | solution.py:249
  17.4 11.0 %collective-permute-start.6 = (s16[528,128]{1,0:T(8,128)(2,1)S(1)}, s16[528,128]{1,0:T(8,128)(2,1)S(1)}, u32[]{:S(2)}, u32[]{:S(2)}) collective-permute-start(s16[528,128]{1,0:T(8,128)(2,1)S(1)} %get-tuple-element.18), channel_id=1, source_target_pairs={{0,4},{1,7},{2,6},{3,5},{4,0},{5,3},{6,2},{7,1},{8,12},{9,15},{10,... | collective-permute-start | bytes 405512 | tf_op jit(solution)/shard_map/ppermute | solution.py:249
  21.3 7.6 %collective-permute-start.10 = (s16[528,128]{1,0:T(8,128)(2,1)S(1)}, s16[528,128]{1,0:T(8,128)(2,1)S(1)}, u32[]{:S(2)}, u32[]{:S(2)}) collective-permute-start(s16[528,128]{1,0:T(8,128)(2,1)S(1)} %get-tuple-element.21), channel_id=1, source_target_pairs={{0,2},{1,3},{2,0},{3,1},{4,6},{5,7},{6,4},{7,5},{8,10},{9,11},{10,... | collective-permute-start | bytes 405512 | tf_op jit(solution)/shard_map/ppermute | solution.py:249
  22.9 7.6 %collective-permute-start.9 = (s16[528,128]{1,0:T(8,128)(2,1)S(1)}, s16[528,128]{1,0:T(8,128)(2,1)S(1)}, u32[]{:S(2)}, u32[]{:S(2)}) collective-permute-start(s16[528,128]{1,0:T(8,128)(2,1)S(1)} %get-tuple-element.20), channel_id=1, source_target_pairs={{0,6},{1,5},{2,4},{3,7},{4,2},{5,1},{6,0},{7,3},{8,14},{9,13},{10,... | collective-permute-start | bytes 405512 | tf_op jit(solution)/shard_map/ppermute | solution.py:249

commit v6 on v5

--- a/solution.py
+++ b/solution.py
@@ -59,7 +59,7 @@
         shrink = jnp.exp2(-power)
         grains = jnp.ceil(peak * shrink * GRAIN) + 1.0
         factor = (TOP * GRAIN / grains) * shrink
-        code_ref[m * rows : (m + 1) * rows] = jnp.round(value * factor).astype(jnp.int16)
+        code_ref[m * rows : (m + 1) * rows] = jnp.round(value * factor).astype(jnp.int32).astype(jnp.int16)
         scales = jnp.where(row == m, power, jnp.where(row == PAD // 2 + m, grains, scales))
     code_ref[len(parts) * rows :] = scales.astype(jnp.int16)
 
@@ -214,15 +214,21 @@
         keep_ref[...] = jnp.where(stays, new_ref[...], held_ref[...])
 
 
-def last_kernel(half, a_ref, b_ref, c_ref, own_ref, out_ref):
-    ib = out_ref.shape[2]
+def last_kernel(half, a_ref, b_ref, c_ref, own_ref, out_hbm, out_ref, sem):
+    ib = out_ref.shape[0]
     arrived = [decoded(ref, ib * half) for ref in (a_ref, b_ref, c_ref, own_ref)]
+    copies = []
     for m, (a, b, c, own) in enumerate(zip(*arrived)):
         total = (a + own) + (b + c)
         for i in range(ib):
             part = total[i * half : (i + 1) * half]
-            out_ref[0, 0, i, 2 * m] = part[:, :half]
-            out_ref[0, 0, i, 2 * m + 1] = part[:, half:]
+            out_ref[i, 2 * m] = part[:, :half]
+            out_ref[i, 2 * m + 1] = part[:, half:]
+            here = pl.ds(2 * m, 2)
+            copies.append(pltpu.make_async_copy(out_ref.at[i, here], out_hbm.at[0, 0, i, here], sem.at[m * ib + i]))
+            copies[-1].start()
+    for copy in copies:
+        copy.wait()
 
 
 VMEM = pl.BlockSpec(memory_space=pltpu.VMEM)
@@ -338,7 +344,11 @@
         functools.partial(last_kernel, bs),
         out_shape=jax.ShapeDtypeStruct((1, 1, ib, no, bs, bs), jnp.float32),
         in_specs=[VMEM] * len(got),
-        out_specs=VMEM,
+        out_specs=HBM,
+        scratch_shapes=[
+            pltpu.VMEM((ib, no, bs, bs), jnp.float32),
+            pltpu.SemaphoreType.DMA((ib * no // 2,)),
+        ],
         compiler_params=PARAMS,
         name="last",
     )(*got)

time: 31.7 us -> 31.6 us (level)
  no operation moved by 1% of the time
where the time goes in v6:
time: 31.6 us; the launch traced here: 31.4 us
  starting transfers between devices  17.1 us (54%)
  Pallas kernels  8.62 us (27%)
  waiting for transfers between devices  5.67 us (18%)
    ppermute x11, starting transfers between devices, send(): return lax.ppermute(value, ('row', 'col'), pairs)  17.1 us
    ppermute x11, waiting for transfers between devices, send(): return lax.ppermute(value, ('row', 'col'), pairs)  5.67 us
    pallas_call x1, Pallas kernels, grid_path(): pl.pallas_call(first_kernel, out_shape=(jax.ShapeDtypeStruct((wide_cols,...  2.48 us
    pallas_call x2, Pallas kernels, summed(): pl.pallas_call(functools.partial(sum_kernel, bs, odd), out_shape=(2 + odd...  1.92 us
    pallas_call x1, Pallas kernels, grid_path(): pl.pallas_call(functools.partial(kept_kernel, bs), out_shape=both, in_spe...  1.33 us
    pallas_call x1, Pallas kernels, grid_path(): pl.pallas_call(pack_kernel, out_shape=jax.ShapeDtypeStruct((nl * bs // LA...  1.1 us
    pallas_call x1, Pallas kernels, grid_path(): pl.pallas_call(functools.partial(last_kernel, bs), out_shape=jax.ShapeDty...  0.94 us
    pallas_call x1, Pallas kernels, grid_path(): pl.pallas_call(functools.partial(second_kernel, bs), out_shape=code, in_s...  0.85 us
  transfers between devices with their start and end apart: 11, of which 5 were waited for; matrix products, arithmetic and copies ran while one was open for 0% of the time, Pallas kernels for 21%

profile of v6, /device:TPU:0, one launch (start us, length us, event | category | flops | bytes accessed | tf_op | source)
XLA Modules:
  0.0 31.4 jit_solution(15815959951794359252)
XLA Ops:
  0.0 1.1 %pack.1.packed_ref = bf16[528,128]{1,0:T(8,128)(2,1)S(1)} custom-call(s32[1,1,2,8]{3,2,1,0:T(2,128)} %cols_hbm.1, bf16[1,1,2,8,64,64]{5,4,3,2,1,0:T(8,128)(2,1)} %left_hbm.1), custom_call_target="tpu_custom_call" | custom-call | tf_op jit(solution)/shard_map/pack/pallas_call | solution.py:268
  1.1 3.0 %collective-permute-start.3 = (bf16[528,128]{1,0:T(8,128)(2,1)S(1)}, bf16[528,128]{1,0:T(8,128)(2,1)S(1)}, u32[]{:S(2)}, u32[]{:S(2)}) collective-permute-start(bf16[528,128]{1,0:T(8,128)(2,1)S(1)} %pack.1.packed_ref), channel_id=1, source_target_pairs={{0,16},{1,17},{2,18},{3,19},{4,20},{5,21},{6,22},{7,23},{8,24},{9,... | collective-permute-start | bytes 405512 | tf_op jit(solution)/shard_map/ppermute | solution.py:255
  4.1 0.0 copy-start
  4.1 2.5 %first.1 = (bf16[8,1024,128]{2,1,0:T(8,128)(2,1)S(1)}, s16[1040,128]{1,0:T(8,128)(2,1)S(1)}) custom-call(s32[1,6,1,16]{3,2,1,0:T(1,128)} %bitcast.1, bf16[1,1,16,6,64,64]{5,4,3,2,1,0:T(8,128)(2,1)} %right_hbm.1, bf16[528,128]{1,0:T(8,128)(2,1)S(1)} %pack.1.packed_ref), custom_call_target="tpu_custom_call" | custom-call | tf_op jit(solution)/shard_map/first/pallas_call | solution.py:282
  6.6 1.6 %collective-permute-start.5 = (s16[1040,128]{1,0:T(8,128)(2,1)S(1)}, s16[1040,128]{1,0:T(8,128)(2,1)S(1)}, u32[]{:S(2)}, u32[]{:S(2)}) collective-permute-start(s16[1040,128]{1,0:T(8,128)(2,1)S(1)} %get-tuple-element.17), channel_id=1, source_target_pairs={{0,1},{1,0},{2,3},{3,2},{4,5},{5,4},{6,7},{7,6},{8,9},{9,8},{10,11... | collective-permute-start | bytes 798728 | tf_op jit(solution)/shard_map/ppermute | solution.py:255
  8.2 0.0 collective-permute-start.2
  8.2 0.0 collective-permute-done.3.packed_ref
  8.2 0.5 %collective-permute-start.4 = (bf16[528,128]{1,0:T(8,128)(2,1)S(1)}, bf16[528,128]{1,0:T(8,128)(2,1)S(1)}, u32[]{:S(2)}, u32[]{:S(2)}) collective-permute-start(bf16[528,128]{1,0:T(8,128)(2,1)S(1)} %collective-permute-done.3.packed_ref), channel_id=1, source_target_pairs={{0,8},{1,9},{2,10},{3,11},{4,12},{5,13},{6,14},{7,15},{8,0},{9,1},... | collective-permute-start | bytes 405512 | tf_op jit(solution)/shard_map/ppermute | solution.py:255
  8.7 0.8 %second.1 = s16[1040,128]{1,0:T(8,128)(2,1)S(1)} custom-call(bf16[8,1024,128]{2,1,0:T(8,128)(2,1)S(1)} %get-tuple-element.15.dense_ref, bf16[528,128]{1,0:T(8,128)(2,1)S(1)} %collective-permute-done.3.packed_ref), custom_call_target="tpu_custom_call" | custom-call | tf_op jit(solution)/shard_map/second/pallas_call | solution.py:304
  9.6 0.8 %collective-permute-start.8 = (s16[1040,128]{1,0:T(8,128)(2,1)S(1)}, s16[1040,128]{1,0:T(8,128)(2,1)S(1)}, u32[]{:S(2)}, u32[]{:S(2)}) collective-permute-start(s16[1040,128]{1,0:T(8,128)(2,1)S(1)} %second.1), channel_id=1, source_target_pairs={{0,1},{1,0},{2,3},{3,2},{4,5},{5,4},{6,7},{7,6},{8,9},{9,8},{10,11... | collective-permute-start | bytes 798728 | tf_op jit(solution)/shard_map/ppermute | solution.py:255
  10.4 0.0 copy-done
  10.4 1.6 %collective-permute-start = (s32[1,1,2,8]{3,2,1,0:T(2,128)S(1)}, s32[1,1,2,8]{3,2,1,0:T(2,128)S(1)}, u32[]{:S(2)}, u32[]{:S(2)}) collective-permute-start(s32[1,1,2,8]{3,2,1,0:T(2,128)S(1)} %copy-done), channel_id=1, source_target_pairs={{0,2},{1,3},{2,0},{3,1},{4,6},{5,7},{6,4},{7,5},{8,10},{9,11},{10,... | collective-permute-start | bytes 200 | tf_op jit(solution)/shard_map/ppermute | solution.py:255
  11.9 0.0 collective-permute-done.2.near_ref
  11.9 2.6 %collective-permute-start.1 = (s32[1,1,2,8]{3,2,1,0:T(2,128)S(1)}, s32[1,1,2,8]{3,2,1,0:T(2,128)S(1)}, u32[]{:S(2)}, u32[]{:S(2)}) collective-permute-start(s32[1,1,2,8]{3,2,1,0:T(2,128)S(1)} %copy-done), channel_id=1, source_target_pairs={{0,4},{1,7},{2,6},{3,5},{4,0},{5,3},{6,2},{7,1},{8,12},{9,15},{10,... | collective-permute-start | bytes 200 | tf_op jit(solution)/shard_map/ppermute | solution.py:255
  14.5 0.0 collective-permute-done.4.far_ref
  14.5 0.2 collective-permute-start.7
  14.8 1.3 %kept.1.kept_ref = f32[2,8,128,128]{3,2,1,0:T(8,128)S(1)} custom-call(bf16[8,1024,128]{2,1,0:T(8,128)(2,1)S(1)} %get-tuple-element.15.dense_ref, bf16[528,128]{1,0:T(8,128)(2,1)S(1)} %collective-permute-done.2.near_ref, bf16[528,128]{1,0:T(8,128)(2,1)S(1)} %collective-permute-done.4.far_ref), custom_call_target="tpu_custom_call" | custom-call | tf_op jit(solution)/shard_map/kept/pallas_call | solution.py:315
  16.1 0.0 collective-permute-done.one_ref
  16.1 0.3 collective-permute-done.1.far_ref
  16.4 0.0 collective-permute-done.5.code_ref
  16.4 0.9 %sum.2 = (s16[528,128]{1,0:T(8,128)(2,1)S(1)}, s16[528,128]{1,0:T(8,128)(2,1)S(1)}) custom-call(s32[1,1,2,8]{3,2,1,0:T(2,128)S(1)} %copy-done, s32[1,1,2,8]{3,2,1,0:T(2,128)S(1)} %collective-permute-done.one_ref, s32[1,1,2,8]{3,2,1,0:T(2,128)S(1)} %collective-permute-done.1.far_ref, f32[2,8,128,128]{3,2,1,0:T(8,128)S(1)} %kept.1.kept_ref, ...), custom_call_target="tpu_custom_call" | custom-call | flops 2000000000 | bytes 20000000 | tf_op jit(solution)/shard_map/sum/pallas_call | solution.py:328
  17.4 2.7 %collective-permute-start.6 = (s16[528,128]{1,0:T(8,128)(2,1)S(1)}, s16[528,128]{1,0:T(8,128)(2,1)S(1)}, u32[]{:S(2)}, u32[]{:S(2)}) collective-permute-start(s16[528,128]{1,0:T(8,128)(2,1)S(1)} %get-tuple-element.18), channel_id=1, source_target_pairs={{0,4},{1,7},{2,6},{3,5},{4,0},{5,3},{6,2},{7,1},{8,12},{9,15},{10,... | collective-permute-start | bytes 405512 | tf_op jit(solution)/shard_map/ppermute | solution.py:255
  20.0 0.0 collective-permute-done.7.far_ref
  20.0 0.2 collective-permute-done.8.code_ref
  20.3 1.0 %sum.3 = (s16[528,128]{1,0:T(8,128)(2,1)S(1)}, s16[528,128]{1,0:T(8,128)(2,1)S(1)}, s16[528,128]{1,0:T(8,128)(2,1)S(1)}) custom-call(s32[1,1,2,8]{3,2,1,0:T(2,128)S(1)} %copy-done, s32[1,1,2,8]{3,2,1,0:T(2,128)S(1)} %collective-permute-done.one_ref, s32[1,1,2,8]{3,2,1,0:T(2,128)S(1)} %collective-permute-done.7.far_ref, f32[2,8,128,128]{3,2,1,0:T(8,128)S(1)} %kept.1.kept_ref, ...), custom_call_target="tpu_custom_call" | custom-call | tf_op jit(solution)/shard_map/sum/pallas_call | solution.py:328
  21.2 1.6 %collective-permute-start.10 = (s16[528,128]{1,0:T(8,128)(2,1)S(1)}, s16[528,128]{1,0:T(8,128)(2,1)S(1)}, u32[]{:S(2)}, u32[]{:S(2)}) collective-permute-start(s16[528,128]{1,0:T(8,128)(2,1)S(1)} %get-tuple-element.21), channel_id=1, source_target_pairs={{0,2},{1,3},{2,0},{3,1},{4,6},{5,7},{6,4},{7,5},{8,10},{9,11},{10,... | collective-permute-start | bytes 405512 | tf_op jit(solution)/shard_map/ppermute | solution.py:255
  22.9 2.5 %collective-permute-start.9 = (s16[528,128]{1,0:T(8,128)(2,1)S(1)}, s16[528,128]{1,0:T(8,128)(2,1)S(1)}, u32[]{:S(2)}, u32[]{:S(2)}) collective-permute-start(s16[528,128]{1,0:T(8,128)(2,1)S(1)} %get-tuple-element.20), channel_id=1, source_target_pairs={{0,6},{1,5},{2,4},{3,7},{4,2},{5,1},{6,0},{7,3},{8,14},{9,13},{10,... | collective-permute-start | bytes 405512 | tf_op jit(solution)/shard_map/ppermute | solution.py:255
  25.4 3.0 %collective-permute-done.6.a_ref = s16[528,128]{1,0:T(8,128)(2,1)S(1)} collective-permute-done((s16[528,128]{1,0:T(8,128)(2,1)S(1)}, s16[528,128]{1,0:T(8,128)(2,1)S(1)}, u32[]{:S(2)}, u32[]{:S(2)}) %collective-permute-start.6) | collective-permute-done | bytes 135200 | tf_op jit(solution)/shard_map/ppermute | solution.py:255
  28.4 0.4 %collective-permute-done.10.c_ref = s16[528,128]{1,0:T(8,128)(2,1)S(1)} collective-permute-done((s16[528,128]{1,0:T(8,128)(2,1)S(1)}, s16[528,128]{1,0:T(8,128)(2,1)S(1)}, u32[]{:S(2)}, u32[]{:S(2)}) %collective-permute-start.10) | collective-permute-done | bytes 135200 | tf_op jit(solution)/shard_map/ppermute | solution.py:255
  28.8 1.7 %collective-permute-done.9.b_ref = s16[528,128]{1,0:T(8,128)(2,1)S(1)} collective-permute-done((s16[528,128]{1,0:T(8,128)(2,1)S(1)}, s16[528,128]{1,0:T(8,128)(2,1)S(1)}, u32[]{:S(2)}, u32[]{:S(2)}) %collective-permute-start.9) | collective-permute-done | bytes 135200 | tf_op jit(solution)/shard_map/ppermute | solution.py:255
  30.5 0.9 %last.1 = f32[1,1,2,8,64,64]{5,4,3,2,1,0:T(8,128)} custom-call(s16[528,128]{1,0:T(8,128)(2,1)S(1)} %collective-permute-done.6.a_ref, s16[528,128]{1,0:T(8,128)(2,1)S(1)} %collective-permute-done.9.b_ref, s16[528,128]{1,0:T(8,128)(2,1)S(1)} %collective-permute-done.10.c_ref, s16[528,128]{1,0:T(8,128)(2,1)S(1)} %get-tuple-element.22.own_ref), custom_call_target="tpu_custom_call" | custom-call | tf_op jit(solution)/shard_map/last/pallas_call | solution.py:343
Async XLA Ops:
  1.1 7.1 %collective-permute-start.3 = (bf16[528,128]{1,0:T(8,128)(2,1)S(1)}, bf16[528,128]{1,0:T(8,128)(2,1)S(1)}, u32[]{:S(2)}, u32[]{:S(2)}) collective-permute-start(bf16[528,128]{1,0:T(8,128)(2,1)S(1)} %pack.1.packed_ref), channel_id=1, source_target_pairs={{0,16},{1,17},{2,18},{3,19},{4,20},{5,21},{6,22},{7,23},{8,24},{9,... | collective-permute-start | bytes 405512 | tf_op jit(solution)/shard_map/ppermute | solution.py:255
  4.1 6.2 %copy-start = (s32[1,1,2,8]{3,2,1,0:T(2,128)S(1)}, s32[1,1,2,8]{3,2,1,0:T(2,128)}, u32[]{:S(2)}) copy-start(s32[1,1,2,8]{3,2,1,0:T(2,128)} %own_ref.3) | copy-start | bytes 196
  6.6 9.8 %collective-permute-start.5 = (s16[1040,128]{1,0:T(8,128)(2,1)S(1)}, s16[1040,128]{1,0:T(8,128)(2,1)S(1)}, u32[]{:S(2)}, u32[]{:S(2)}) collective-permute-start(s16[1040,128]{1,0:T(8,128)(2,1)S(1)} %get-tuple-element.17), channel_id=1, source_target_pairs={{0,1},{1,0},{2,3},{3,2},{4,5},{5,4},{6,7},{7,6},{8,9},{9,8},{10,11... | collective-permute-start | bytes 798728 | tf_op jit(solution)/shard_map/ppermute | solution.py:255
  8.2 3.8 %collective-permute-start.2 = (bf16[528,128]{1,0:T(8,128)(2,1)S(1)}, bf16[528,128]{1,0:T(8,128)(2,1)S(1)}, u32[]{:S(2)}, u32[]{:S(2)}) collective-permute-start(bf16[528,128]{1,0:T(8,128)(2,1)S(1)} %pack.1.packed_ref), channel_id=1, source_target_pairs={{0,8},{1,9},{2,10},{3,11},{4,12},{5,13},{6,14},{7,15},{8,0},{9,1},... | collective-permute-start | bytes 405512 | tf_op jit(solution)/shard_map/ppermute | solution.py:255
  8.2 6.4 %collective-permute-start.4 = (bf16[528,128]{1,0:T(8,128)(2,1)S(1)}, bf16[528,128]{1,0:T(8,128)(2,1)S(1)}, u32[]{:S(2)}, u32[]{:S(2)}) collective-permute-start(bf16[528,128]{1,0:T(8,128)(2,1)S(1)} %collective-permute-done.3.packed_ref), channel_id=1, source_target_pairs={{0,8},{1,9},{2,10},{3,11},{4,12},{5,13},{6,14},{7,15},{8,0},{9,1},... | collective-permute-start | bytes 405512 | tf_op jit(solution)/shard_map/ppermute | solution.py:255
  9.6 10.7 %collective-permute-start.8 = (s16[1040,128]{1,0:T(8,128)(2,1)S(1)}, s16[1040,128]{1,0:T(8,128)(2,1)S(1)}, u32[]{:S(2)}, u32[]{:S(2)}) collective-permute-start(s16[1040,128]{1,0:T(8,128)(2,1)S(1)} %second.1), channel_id=1, source_target_pairs={{0,1},{1,0},{2,3},{3,2},{4,5},{5,4},{6,7},{7,6},{8,9},{9,8},{10,11... | collective-permute-start | bytes 798728 | tf_op jit(solution)/shard_map/ppermute | solution.py:255
  10.4 5.7 %collective-permute-start = (s32[1,1,2,8]{3,2,1,0:T(2,128)S(1)}, s32[1,1,2,8]{3,2,1,0:T(2,128)S(1)}, u32[]{:S(2)}, u32[]{:S(2)}) collective-permute-start(s32[1,1,2,8]{3,2,1,0:T(2,128)S(1)} %copy-done), channel_id=1, source_target_pairs={{0,2},{1,3},{2,0},{3,1},{4,6},{5,7},{6,4},{7,5},{8,10},{9,11},{10,... | collective-permute-start | bytes 200 | tf_op jit(solution)/shard_map/ppermute | solution.py:255
  11.9 4.5 %collective-permute-start.1 = (s32[1,1,2,8]{3,2,1,0:T(2,128)S(1)}, s32[1,1,2,8]{3,2,1,0:T(2,128)S(1)}, u32[]{:S(2)}, u32[]{:S(2)}) collective-permute-start(s32[1,1,2,8]{3,2,1,0:T(2,128)S(1)} %copy-done), channel_id=1, source_target_pairs={{0,4},{1,7},{2,6},{3,5},{4,0},{5,3},{6,2},{7,1},{8,12},{9,15},{10,... | collective-permute-start | bytes 200 | tf_op jit(solution)/shard_map/ppermute | solution.py:255
  14.5 5.5 %collective-permute-start.7 = (s32[1,1,2,8]{3,2,1,0:T(2,128)S(1)}, s32[1,1,2,8]{3,2,1,0:T(2,128)S(1)}, u32[]{:S(2)}, u32[]{:S(2)}) collective-permute-start(s32[1,1,2,8]{3,2,1,0:T(2,128)S(1)} %copy-done), channel_id=1, source_target_pairs={{0,6},{1,5},{2,4},{3,7},{4,2},{5,1},{6,0},{7,3},{8,14},{9,13},{10,... | collective-permute-start | bytes 200 | tf_op jit(solution)/shard_map/ppermute | solution.py:255
  17.4 11.0 %collective-permute-start.6 = (s16[528,128]{1,0:T(8,128)(2,1)S(1)}, s16[528,128]{1,0:T(8,128)(2,1)S(1)}, u32[]{:S(2)}, u32[]{:S(2)}) collective-permute-start(s16[528,128]{1,0:T(8,128)(2,1)S(1)} %get-tuple-element.18), channel_id=1, source_target_pairs={{0,4},{1,7},{2,6},{3,5},{4,0},{5,3},{6,2},{7,1},{8,12},{9,15},{10,... | collective-permute-start | bytes 405512 | tf_op jit(solution)/shard_map/ppermute | solution.py:255
  21.2 7.6 %collective-permute-start.10 = (s16[528,128]{1,0:T(8,128)(2,1)S(1)}, s16[528,128]{1,0:T(8,128)(2,1)S(1)}, u32[]{:S(2)}, u32[]{:S(2)}) collective-permute-start(s16[528,128]{1,0:T(8,128)(2,1)S(1)} %get-tuple-element.21), channel_id=1, source_target_pairs={{0,2},{1,3},{2,0},{3,1},{4,6},{5,7},{6,4},{7,5},{8,10},{9,11},{10,... | collective-permute-start | bytes 405512 | tf_op jit(solution)/shard_map/ppermute | solution.py:255
  22.9 7.6 %collective-permute-start.9 = (s16[528,128]{1,0:T(8,128)(2,1)S(1)}, s16[528,128]{1,0:T(8,128)(2,1)S(1)}, u32[]{:S(2)}, u32[]{:S(2)}) collective-permute-start(s16[528,128]{1,0:T(8,128)(2,1)S(1)} %get-tuple-element.20), channel_id=1, source_target_pairs={{0,6},{1,5},{2,4},{3,7},{4,2},{5,1},{6,0},{7,3},{8,14},{9,13},{10,... | collective-permute-start | bytes 405512 | tf_op jit(solution)/shard_map/ppermute | solution.py:255

commit v7 on v6

--- a/solution.py
+++ b/solution.py
@@ -278,6 +278,7 @@
         compiler_params=PARAMS,
         name="pack",
     )(*in_hbm(left_cols, left_blocks))
+    far_cols = (send(out_cols, along(2, 3)), send(out_cols, along(3, 2)))
     one_cols = send(out_cols, along(1, 1))
     dense, code_one = pl.pallas_call(
         first_kernel,
@@ -310,7 +311,6 @@
         compiler_params=PARAMS,
         name="second",
     )(dense, across)
-    far_cols = (send(out_cols, along(2, 3)), send(out_cols, along(3, 2)))
     got_two = send(code_two, lambda r, c: (r, c ^ 1))
     kept = pl.pallas_call(
         functools.partial(kept_kernel, bs),
@@ -339,7 +339,8 @@
     a, held = summed(0, got_one)
     got = [send(a, along(2, 3))]
     a, b, own = summed(1, got_two, held)
-    got += [send(a, along(3, 2)), send(b, along(1, 1)), own]
+    last = send(b, along(1, 1))
+    got += [send(a, along(3, 2)), last, own]
     return pl.pallas_call(
         functools.partial(last_kernel, bs),
         out_shape=jax.ShapeDtypeStruct((1, 1, ib, no, bs, bs), jnp.float32),

time: 31.6 us -> 31.6 us (level)
  no operation moved by 1% of the time
where the time goes in v7:
time: 31.6 us; the launch traced here: 31.4 us
  starting transfers between devices  17.1 us (54%)
  Pallas kernels  8.62 us (27%)
  waiting for transfers between devices  5.67 us (18%)
    ppermute x11, starting transfers between devices, send(): return lax.ppermute(value, ('row', 'col'), pairs)  17.1 us
    ppermute x11, waiting for transfers between devices, send(): return lax.ppermute(value, ('row', 'col'), pairs)  5.67 us
    pallas_call x1, Pallas kernels, grid_path(): pl.pallas_call(first_kernel, out_shape=(jax.ShapeDtypeStruct((wide_cols,...  2.48 us
    pallas_call x2, Pallas kernels, summed(): pl.pallas_call(functools.partial(sum_kernel, bs, odd), out_shape=(2 + odd...  1.92 us
    pallas_call x1, Pallas kernels, grid_path(): pl.pallas_call(functools.partial(kept_kernel, bs), out_shape=both, in_spe...  1.33 us
    pallas_call x1, Pallas kernels, grid_path(): pl.pallas_call(pack_kernel, out_shape=jax.ShapeDtypeStruct((nl * bs // LA...  1.1 us
    pallas_call x1, Pallas kernels, grid_path(): pl.pallas_call(functools.partial(last_kernel, bs), out_shape=jax.ShapeDty...  0.94 us
    pallas_call x1, Pallas kernels, grid_path(): pl.pallas_call(functools.partial(second_kernel, bs), out_shape=code, in_s...  0.85 us
  transfers between devices with their start and end apart: 11, of which 5 were waited for; matrix products, arithmetic and copies ran while one was open for 0% of the time, Pallas kernels for 21%

profile of v7, /device:TPU:0, one launch (start us, length us, event | category | flops | bytes accessed | tf_op | source)
XLA Modules:
  0.0 31.4 jit_solution(15815959951794359252)
XLA Ops:
  0.0 1.1 %pack.1.packed_ref = bf16[528,128]{1,0:T(8,128)(2,1)S(1)} custom-call(s32[1,1,2,8]{3,2,1,0:T(2,128)} %cols_hbm.1, bf16[1,1,2,8,64,64]{5,4,3,2,1,0:T(8,128)(2,1)} %left_hbm.1), custom_call_target="tpu_custom_call" | custom-call | tf_op jit(solution)/shard_map/pack/pallas_call | solution.py:268
  1.1 3.0 %collective-permute-start.3 = (bf16[528,128]{1,0:T(8,128)(2,1)S(1)}, bf16[528,128]{1,0:T(8,128)(2,1)S(1)}, u32[]{:S(2)}, u32[]{:S(2)}) collective-permute-start(bf16[528,128]{1,0:T(8,128)(2,1)S(1)} %pack.1.packed_ref), channel_id=1, source_target_pairs={{0,16},{1,17},{2,18},{3,19},{4,20},{5,21},{6,22},{7,23},{8,24},{9,... | collective-permute-start | bytes 405512 | tf_op jit(solution)/shard_map/ppermute | solution.py:255
  4.1 0.0 copy-start
  4.1 2.5 %first.1 = (bf16[8,1024,128]{2,1,0:T(8,128)(2,1)S(1)}, s16[1040,128]{1,0:T(8,128)(2,1)S(1)}) custom-call(s32[1,6,1,16]{3,2,1,0:T(1,128)} %bitcast.1, bf16[1,1,16,6,64,64]{5,4,3,2,1,0:T(8,128)(2,1)} %right_hbm.1, bf16[528,128]{1,0:T(8,128)(2,1)S(1)} %pack.1.packed_ref), custom_call_target="tpu_custom_call" | custom-call | tf_op jit(solution)/shard_map/first/pallas_call | solution.py:283
  6.6 1.6 %collective-permute-start.5 = (s16[1040,128]{1,0:T(8,128)(2,1)S(1)}, s16[1040,128]{1,0:T(8,128)(2,1)S(1)}, u32[]{:S(2)}, u32[]{:S(2)}) collective-permute-start(s16[1040,128]{1,0:T(8,128)(2,1)S(1)} %get-tuple-element.17), channel_id=1, source_target_pairs={{0,1},{1,0},{2,3},{3,2},{4,5},{5,4},{6,7},{7,6},{8,9},{9,8},{10,11... | collective-permute-start | bytes 798728 | tf_op jit(solution)/shard_map/ppermute | solution.py:255
  8.2 0.0 collective-permute-start.2
  8.2 0.0 collective-permute-done.3.packed_ref
  8.2 0.5 %collective-permute-start.4 = (bf16[528,128]{1,0:T(8,128)(2,1)S(1)}, bf16[528,128]{1,0:T(8,128)(2,1)S(1)}, u32[]{:S(2)}, u32[]{:S(2)}) collective-permute-start(bf16[528,128]{1,0:T(8,128)(2,1)S(1)} %collective-permute-done.3.packed_ref), channel_id=1, source_target_pairs={{0,8},{1,9},{2,10},{3,11},{4,12},{5,13},{6,14},{7,15},{8,0},{9,1},... | collective-permute-start | bytes 405512 | tf_op jit(solution)/shard_map/ppermute | solution.py:255
  8.7 0.8 %second.1 = s16[1040,128]{1,0:T(8,128)(2,1)S(1)} custom-call(bf16[8,1024,128]{2,1,0:T(8,128)(2,1)S(1)} %get-tuple-element.15.dense_ref, bf16[528,128]{1,0:T(8,128)(2,1)S(1)} %collective-permute-done.3.packed_ref), custom_call_target="tpu_custom_call" | custom-call | tf_op jit(solution)/shard_map/second/pallas_call | solution.py:305
  9.6 0.8 %collective-permute-start.8 = (s16[1040,128]{1,0:T(8,128)(2,1)S(1)}, s16[1040,128]{1,0:T(8,128)(2,1)S(1)}, u32[]{:S(2)}, u32[]{:S(2)}) collective-permute-start(s16[1040,128]{1,0:T(8,128)(2,1)S(1)} %second.1), channel_id=1, source_target_pairs={{0,1},{1,0},{2,3},{3,2},{4,5},{5,4},{6,7},{7,6},{8,9},{9,8},{10,11... | collective-permute-start | bytes 798728 | tf_op jit(solution)/shard_map/ppermute | solution.py:255
  10.4 0.0 copy-done
  10.4 1.6 %collective-permute-start = (s32[1,1,2,8]{3,2,1,0:T(2,128)S(1)}, s32[1,1,2,8]{3,2,1,0:T(2,128)S(1)}, u32[]{:S(2)}, u32[]{:S(2)}) collective-permute-start(s32[1,1,2,8]{3,2,1,0:T(2,128)S(1)} %copy-done), channel_id=1, source_target_pairs={{0,2},{1,3},{2,0},{3,1},{4,6},{5,7},{6,4},{7,5},{8,10},{9,11},{10,... | collective-permute-start | bytes 200 | tf_op jit(solution)/shard_map/ppermute | solution.py:255
  11.9 0.0 collective-permute-done.2.near_ref
  11.9 2.6 %collective-permute-start.1 = (s32[1,1,2,8]{3,2,1,0:T(2,128)S(1)}, s32[1,1,2,8]{3,2,1,0:T(2,128)S(1)}, u32[]{:S(2)}, u32[]{:S(2)}) collective-permute-start(s32[1,1,2,8]{3,2,1,0:T(2,128)S(1)} %copy-done), channel_id=1, source_target_pairs={{0,4},{1,7},{2,6},{3,5},{4,0},{5,3},{6,2},{7,1},{8,12},{9,15},{10,... | collective-permute-start | bytes 200 | tf_op jit(solution)/shard_map/ppermute | solution.py:255
  14.5 0.0 collective-permute-done.4.far_ref
  14.5 0.2 collective-permute-start.7
  14.8 1.3 %kept.1.kept_ref = f32[2,8,128,128]{3,2,1,0:T(8,128)S(1)} custom-call(bf16[8,1024,128]{2,1,0:T(8,128)(2,1)S(1)} %get-tuple-element.15.dense_ref, bf16[528,128]{1,0:T(8,128)(2,1)S(1)} %collective-permute-done.2.near_ref, bf16[528,128]{1,0:T(8,128)(2,1)S(1)} %collective-permute-done.4.far_ref), custom_call_target="tpu_custom_call" | custom-call | tf_op jit(solution)/shard_map/kept/pallas_call | solution.py:315
  16.1 0.0 collective-permute-done.one_ref
  16.1 0.3 collective-permute-done.1.far_ref
  16.4 0.0 collective-permute-done.5.code_ref
  16.4 0.9 %sum.2 = (s16[528,128]{1,0:T(8,128)(2,1)S(1)}, s16[528,128]{1,0:T(8,128)(2,1)S(1)}) custom-call(s32[1,1,2,8]{3,2,1,0:T(2,128)S(1)} %copy-done, s32[1,1,2,8]{3,2,1,0:T(2,128)S(1)} %collective-permute-done.one_ref, s32[1,1,2,8]{3,2,1,0:T(2,128)S(1)} %collective-permute-done.1.far_ref, f32[2,8,128,128]{3,2,1,0:T(8,128)S(1)} %kept.1.kept_ref, ...), custom_call_target="tpu_custom_call" | custom-call | flops 2000000000 | bytes 20000000 | tf_op jit(solution)/shard_map/sum/pallas_call | solution.py:328
  17.4 2.7 %collective-permute-start.6 = (s16[528,128]{1,0:T(8,128)(2,1)S(1)}, s16[528,128]{1,0:T(8,128)(2,1)S(1)}, u32[]{:S(2)}, u32[]{:S(2)}) collective-permute-start(s16[528,128]{1,0:T(8,128)(2,1)S(1)} %get-tuple-element.18), channel_id=1, source_target_pairs={{0,4},{1,7},{2,6},{3,5},{4,0},{5,3},{6,2},{7,1},{8,12},{9,15},{10,... | collective-permute-start | bytes 405512 | tf_op jit(solution)/shard_map/ppermute | solution.py:255
  20.0 0.0 collective-permute-done.7.far_ref
  20.0 0.2 collective-permute-done.8.code_ref
  20.3 1.0 %sum.3 = (s16[528,128]{1,0:T(8,128)(2,1)S(1)}, s16[528,128]{1,0:T(8,128)(2,1)S(1)}, s16[528,128]{1,0:T(8,128)(2,1)S(1)}) custom-call(s32[1,1,2,8]{3,2,1,0:T(2,128)S(1)} %copy-done, s32[1,1,2,8]{3,2,1,0:T(2,128)S(1)} %collective-permute-done.one_ref, s32[1,1,2,8]{3,2,1,0:T(2,128)S(1)} %collective-permute-done.7.far_ref, f32[2,8,128,128]{3,2,1,0:T(8,128)S(1)} %kept.1.kept_ref, ...), custom_call_target="tpu_custom_call" | custom-call | tf_op jit(solution)/shard_map/sum/pallas_call | solution.py:328
  21.2 1.6 %collective-permute-start.10 = (s16[528,128]{1,0:T(8,128)(2,1)S(1)}, s16[528,128]{1,0:T(8,128)(2,1)S(1)}, u32[]{:S(2)}, u32[]{:S(2)}) collective-permute-start(s16[528,128]{1,0:T(8,128)(2,1)S(1)} %get-tuple-element.21), channel_id=1, source_target_pairs={{0,2},{1,3},{2,0},{3,1},{4,6},{5,7},{6,4},{7,5},{8,10},{9,11},{10,... | collective-permute-start | bytes 405512 | tf_op jit(solution)/shard_map/ppermute | solution.py:255
  22.9 2.5 %collective-permute-start.9 = (s16[528,128]{1,0:T(8,128)(2,1)S(1)}, s16[528,128]{1,0:T(8,128)(2,1)S(1)}, u32[]{:S(2)}, u32[]{:S(2)}) collective-permute-start(s16[528,128]{1,0:T(8,128)(2,1)S(1)} %get-tuple-element.20), channel_id=1, source_target_pairs={{0,6},{1,5},{2,4},{3,7},{4,2},{5,1},{6,0},{7,3},{8,14},{9,13},{10,... | collective-permute-start | bytes 405512 | tf_op jit(solution)/shard_map/ppermute | solution.py:255
  25.4 3.0 %collective-permute-done.6.a_ref = s16[528,128]{1,0:T(8,128)(2,1)S(1)} collective-permute-done((s16[528,128]{1,0:T(8,128)(2,1)S(1)}, s16[528,128]{1,0:T(8,128)(2,1)S(1)}, u32[]{:S(2)}, u32[]{:S(2)}) %collective-permute-start.6) | collective-permute-done | bytes 135200 | tf_op jit(solution)/shard_map/ppermute | solution.py:255
  28.4 0.4 %collective-permute-done.10.c_ref = s16[528,128]{1,0:T(8,128)(2,1)S(1)} collective-permute-done((s16[528,128]{1,0:T(8,128)(2,1)S(1)}, s16[528,128]{1,0:T(8,128)(2,1)S(1)}, u32[]{:S(2)}, u32[]{:S(2)}) %collective-permute-start.10) | collective-permute-done | bytes 135200 | tf_op jit(solution)/shard_map/ppermute | solution.py:255
  28.8 1.7 %collective-permute-done.9.b_ref = s16[528,128]{1,0:T(8,128)(2,1)S(1)} collective-permute-done((s16[528,128]{1,0:T(8,128)(2,1)S(1)}, s16[528,128]{1,0:T(8,128)(2,1)S(1)}, u32[]{:S(2)}, u32[]{:S(2)}) %collective-permute-start.9) | collective-permute-done | bytes 135200 | tf_op jit(solution)/shard_map/ppermute | solution.py:255
  30.5 0.9 %last.1 = f32[1,1,2,8,64,64]{5,4,3,2,1,0:T(8,128)} custom-call(s16[528,128]{1,0:T(8,128)(2,1)S(1)} %collective-permute-done.6.a_ref, s16[528,128]{1,0:T(8,128)(2,1)S(1)} %collective-permute-done.9.b_ref, s16[528,128]{1,0:T(8,128)(2,1)S(1)} %collective-permute-done.10.c_ref, s16[528,128]{1,0:T(8,128)(2,1)S(1)} %get-tuple-element.22.own_ref), custom_call_target="tpu_custom_call" | custom-call | tf_op jit(solution)/shard_map/last/pallas_call | solution.py:344
Async XLA Ops:
  1.1 7.1 %collective-permute-start.3 = (bf16[528,128]{1,0:T(8,128)(2,1)S(1)}, bf16[528,128]{1,0:T(8,128)(2,1)S(1)}, u32[]{:S(2)}, u32[]{:S(2)}) collective-permute-start(bf16[528,128]{1,0:T(8,128)(2,1)S(1)} %pack.1.packed_ref), channel_id=1, source_target_pairs={{0,16},{1,17},{2,18},{3,19},{4,20},{5,21},{6,22},{7,23},{8,24},{9,... | collective-permute-start | bytes 405512 | tf_op jit(solution)/shard_map/ppermute | solution.py:255
  4.1 6.2 %copy-start = (s32[1,1,2,8]{3,2,1,0:T(2,128)S(1)}, s32[1,1,2,8]{3,2,1,0:T(2,128)}, u32[]{:S(2)}) copy-start(s32[1,1,2,8]{3,2,1,0:T(2,128)} %own_ref.3) | copy-start | bytes 196
  6.6 9.8 %collective-permute-start.5 = (s16[1040,128]{1,0:T(8,128)(2,1)S(1)}, s16[1040,128]{1,0:T(8,128)(2,1)S(1)}, u32[]{:S(2)}, u32[]{:S(2)}) collective-permute-start(s16[1040,128]{1,0:T(8,128)(2,1)S(1)} %get-tuple-element.17), channel_id=1, source_target_pairs={{0,1},{1,0},{2,3},{3,2},{4,5},{5,4},{6,7},{7,6},{8,9},{9,8},{10,11... | collective-permute-start | bytes 798728 | tf_op jit(solution)/shard_map/ppermute | solution.py:255
  8.2 3.8 %collective-permute-start.2 = (bf16[528,128]{1,0:T(8,128)(2,1)S(1)}, bf16[528,128]{1,0:T(8,128)(2,1)S(1)}, u32[]{:S(2)}, u32[]{:S(2)}) collective-permute-start(bf16[528,128]{1,0:T(8,128)(2,1)S(1)} %pack.1.packed_ref), channel_id=1, source_target_pairs={{0,8},{1,9},{2,10},{3,11},{4,12},{5,13},{6,14},{7,15},{8,0},{9,1},... | collective-permute-start | bytes 405512 | tf_op jit(solution)/shard_map/ppermute | solution.py:255
  8.2 6.4 %collective-permute-start.4 = (bf16[528,128]{1,0:T(8,128)(2,1)S(1)}, bf16[528,128]{1,0:T(8,128)(2,1)S(1)}, u32[]{:S(2)}, u32[]{:S(2)}) collective-permute-start(bf16[528,128]{1,0:T(8,128)(2,1)S(1)} %collective-permute-done.3.packed_ref), channel_id=1, source_target_pairs={{0,8},{1,9},{2,10},{3,11},{4,12},{5,13},{6,14},{7,15},{8,0},{9,1},... | collective-permute-start | bytes 405512 | tf_op jit(solution)/shard_map/ppermute | solution.py:255
  9.6 10.7 %collective-permute-start.8 = (s16[1040,128]{1,0:T(8,128)(2,1)S(1)}, s16[1040,128]{1,0:T(8,128)(2,1)S(1)}, u32[]{:S(2)}, u32[]{:S(2)}) collective-permute-start(s16[1040,128]{1,0:T(8,128)(2,1)S(1)} %second.1), channel_id=1, source_target_pairs={{0,1},{1,0},{2,3},{3,2},{4,5},{5,4},{6,7},{7,6},{8,9},{9,8},{10,11... | collective-permute-start | bytes 798728 | tf_op jit(solution)/shard_map/ppermute | solution.py:255
  10.4 5.7 %collective-permute-start = (s32[1,1,2,8]{3,2,1,0:T(2,128)S(1)}, s32[1,1,2,8]{3,2,1,0:T(2,128)S(1)}, u32[]{:S(2)}, u32[]{:S(2)}) collective-permute-start(s32[1,1,2,8]{3,2,1,0:T(2,128)S(1)} %copy-done), channel_id=1, source_target_pairs={{0,2},{1,3},{2,0},{3,1},{4,6},{5,7},{6,4},{7,5},{8,10},{9,11},{10,... | collective-permute-start | bytes 200 | tf_op jit(solution)/shard_map/ppermute | solution.py:255
  11.9 4.5 %collective-permute-start.1 = (s32[1,1,2,8]{3,2,1,0:T(2,128)S(1)}, s32[1,1,2,8]{3,2,1,0:T(2,128)S(1)}, u32[]{:S(2)}, u32[]{:S(2)}) collective-permute-start(s32[1,1,2,8]{3,2,1,0:T(2,128)S(1)} %copy-done), channel_id=1, source_target_pairs={{0,4},{1,7},{2,6},{3,5},{4,0},{5,3},{6,2},{7,1},{8,12},{9,15},{10,... | collective-permute-start | bytes 200 | tf_op jit(solution)/shard_map/ppermute | solution.py:255
  14.5 5.5 %collective-permute-start.7 = (s32[1,1,2,8]{3,2,1,0:T(2,128)S(1)}, s32[1,1,2,8]{3,2,1,0:T(2,128)S(1)}, u32[]{:S(2)}, u32[]{:S(2)}) collective-permute-start(s32[1,1,2,8]{3,2,1,0:T(2,128)S(1)} %copy-done), channel_id=1, source_target_pairs={{0,6},{1,5},{2,4},{3,7},{4,2},{5,1},{6,0},{7,3},{8,14},{9,13},{10,... | collective-permute-start | bytes 200 | tf_op jit(solution)/shard_map/ppermute | solution.py:255
  17.4 11.0 %collective-permute-start.6 = (s16[528,128]{1,0:T(8,128)(2,1)S(1)}, s16[528,128]{1,0:T(8,128)(2,1)S(1)}, u32[]{:S(2)}, u32[]{:S(2)}) collective-permute-start(s16[528,128]{1,0:T(8,128)(2,1)S(1)} %get-tuple-element.18), channel_id=1, source_target_pairs={{0,4},{1,7},{2,6},{3,5},{4,0},{5,3},{6,2},{7,1},{8,12},{9,15},{10,... | collective-permute-start | bytes 405512 | tf_op jit(solution)/shard_map/ppermute | solution.py:255
  21.2 7.6 %collective-permute-start.10 = (s16[528,128]{1,0:T(8,128)(2,1)S(1)}, s16[528,128]{1,0:T(8,128)(2,1)S(1)}, u32[]{:S(2)}, u32[]{:S(2)}) collective-permute-start(s16[528,128]{1,0:T(8,128)(2,1)S(1)} %get-tuple-element.21), channel_id=1, source_target_pairs={{0,2},{1,3},{2,0},{3,1},{4,6},{5,7},{6,4},{7,5},{8,10},{9,11},{10,... | collective-permute-start | bytes 405512 | tf_op jit(solution)/shard_map/ppermute | solution.py:255
  22.9 7.6 %collective-permute-start.9 = (s16[528,128]{1,0:T(8,128)(2,1)S(1)}, s16[528,128]{1,0:T(8,128)(2,1)S(1)}, u32[]{:S(2)}, u32[]{:S(2)}) collective-permute-start(s16[528,128]{1,0:T(8,128)(2,1)S(1)} %get-tuple-element.20), channel_id=1, source_target_pairs={{0,6},{1,5},{2,4},{3,7},{4,2},{5,1},{6,0},{7,3},{8,14},{9,13},{10,... | collective-permute-start | bytes 405512 | tf_op jit(solution)/shard_map/ppermute | solution.py:255

commit v8 on v6

--- a/solution.py
+++ b/solution.py
@@ -234,7 +234,7 @@
 VMEM = pl.BlockSpec(memory_space=pltpu.VMEM)
 SMEM = pl.BlockSpec(memory_space=pltpu.SMEM)
 HBM = pl.BlockSpec(memory_space=pltpu.HBM)
-PARTS = 4
+PARTS = 2
 COST = pl.CostEstimate(flops=2000000000, bytes_accessed=20000000, transcendentals=0)
 PARAMS = pltpu.CompilerParams(vmem_limit_bytes=40 * 2**20)
 

time: 31.6 us -> 31.6 us (level)
  no operation moved by 1% of the time
where the time goes in v8:
time: 31.6 us; the launch traced here: 31.5 us
  starting transfers between devices  17 us (54%)
  Pallas kernels  8.67 us (27%)
  waiting for transfers between devices  5.71 us (18%)
    ppermute x11, starting transfers between devices, send(): return lax.ppermute(value, ('row', 'col'), pairs)  17 us
    ppermute x11, waiting for transfers between devices, send(): return lax.ppermute(value, ('row', 'col'), pairs)  5.71 us
    pallas_call x1, Pallas kernels, grid_path(): pl.pallas_call(first_kernel, out_shape=(jax.ShapeDtypeStruct((wide_cols,...  2.52 us
    pallas_call x2, Pallas kernels, summed(): pl.pallas_call(functools.partial(sum_kernel, bs, odd), out_shape=(2 + odd...  1.92 us
    pallas_call x1, Pallas kernels, grid_path(): pl.pallas_call(functools.partial(kept_kernel, bs), out_shape=both, in_spe...  1.33 us
    pallas_call x1, Pallas kernels, grid_path(): pl.pallas_call(pack_kernel, out_shape=jax.ShapeDtypeStruct((nl * bs // LA...  1.1 us
    pallas_call x1, Pallas kernels, grid_path(): pl.pallas_call(functools.partial(last_kernel, bs), out_shape=jax.ShapeDty...  0.94 us
    pallas_call x1, Pallas kernels, grid_path(): pl.pallas_call(functools.partial(second_kernel, bs), out_shape=code, in_s...  0.86 us
  transfers between devices with their start and end apart: 11, of which 5 were waited for; matrix products, arithmetic and copies ran while one was open for 0% of the time, Pallas kernels for 21%

profile of v8, /device:TPU:0, one launch (start us, length us, event | category | flops | bytes accessed | tf_op | source)
XLA Modules:
  0.0 31.5 jit_solution(15278819191318537963)
XLA Ops:
  0.0 1.1 %pack.1.packed_ref = bf16[528,128]{1,0:T(8,128)(2,1)S(1)} custom-call(s32[1,1,2,8]{3,2,1,0:T(2,128)} %cols_hbm.1, bf16[1,1,2,8,64,64]{5,4,3,2,1,0:T(8,128)(2,1)} %left_hbm.1), custom_call_target="tpu_custom_call" | custom-call | tf_op jit(solution)/shard_map/pack/pallas_call | solution.py:268
  1.1 3.0 %collective-permute-start.3 = (bf16[528,128]{1,0:T(8,128)(2,1)S(1)}, bf16[528,128]{1,0:T(8,128)(2,1)S(1)}, u32[]{:S(2)}, u32[]{:S(2)}) collective-permute-start(bf16[528,128]{1,0:T(8,128)(2,1)S(1)} %pack.1.packed_ref), channel_id=1, source_target_pairs={{0,16},{1,17},{2,18},{3,19},{4,20},{5,21},{6,22},{7,23},{8,24},{9,... | collective-permute-start | bytes 405512 | tf_op jit(solution)/shard_map/ppermute | solution.py:255
  4.1 0.0 copy-start
  4.1 2.5 %first.1 = (bf16[8,1024,128]{2,1,0:T(8,128)(2,1)S(1)}, s16[1040,128]{1,0:T(8,128)(2,1)S(1)}) custom-call(s32[1,6,1,16]{3,2,1,0:T(1,128)} %bitcast.1, bf16[1,1,16,6,64,64]{5,4,3,2,1,0:T(8,128)(2,1)} %right_hbm.1, bf16[528,128]{1,0:T(8,128)(2,1)S(1)} %pack.1.packed_ref), custom_call_target="tpu_custom_call" | custom-call | tf_op jit(solution)/shard_map/first/pallas_call | solution.py:282
  6.7 1.6 %collective-permute-start.5 = (s16[1040,128]{1,0:T(8,128)(2,1)S(1)}, s16[1040,128]{1,0:T(8,128)(2,1)S(1)}, u32[]{:S(2)}, u32[]{:S(2)}) collective-permute-start(s16[1040,128]{1,0:T(8,128)(2,1)S(1)} %get-tuple-element.17), channel_id=1, source_target_pairs={{0,1},{1,0},{2,3},{3,2},{4,5},{5,4},{6,7},{7,6},{8,9},{9,8},{10,11... | collective-permute-start | bytes 798728 | tf_op jit(solution)/shard_map/ppermute | solution.py:255
  8.2 0.0 collective-permute-start.2
  8.2 0.0 collective-permute-done.3.packed_ref
  8.2 0.5 %collective-permute-start.4 = (bf16[528,128]{1,0:T(8,128)(2,1)S(1)}, bf16[528,128]{1,0:T(8,128)(2,1)S(1)}, u32[]{:S(2)}, u32[]{:S(2)}) collective-permute-start(bf16[528,128]{1,0:T(8,128)(2,1)S(1)} %collective-permute-done.3.packed_ref), channel_id=1, source_target_pairs={{0,8},{1,9},{2,10},{3,11},{4,12},{5,13},{6,14},{7,15},{8,0},{9,1},... | collective-permute-start | bytes 405512 | tf_op jit(solution)/shard_map/ppermute | solution.py:255
  8.7 0.9 %second.1 = s16[1040,128]{1,0:T(8,128)(2,1)S(1)} custom-call(bf16[8,1024,128]{2,1,0:T(8,128)(2,1)S(1)} %get-tuple-element.15.dense_ref, bf16[528,128]{1,0:T(8,128)(2,1)S(1)} %collective-permute-done.3.packed_ref), custom_call_target="tpu_custom_call" | custom-call | tf_op jit(solution)/shard_map/second/pallas_call | solution.py:304
  9.6 0.8 %collective-permute-start.8 = (s16[1040,128]{1,0:T(8,128)(2,1)S(1)}, s16[1040,128]{1,0:T(8,128)(2,1)S(1)}, u32[]{:S(2)}, u32[]{:S(2)}) collective-permute-start(s16[1040,128]{1,0:T(8,128)(2,1)S(1)} %second.1), channel_id=1, source_target_pairs={{0,1},{1,0},{2,3},{3,2},{4,5},{5,4},{6,7},{7,6},{8,9},{9,8},{10,11... | collective-permute-start | bytes 798728 | tf_op jit(solution)/shard_map/ppermute | solution.py:255
  10.4 0.0 copy-done
  10.4 1.6 %collective-permute-start = (s32[1,1,2,8]{3,2,1,0:T(2,128)S(1)}, s32[1,1,2,8]{3,2,1,0:T(2,128)S(1)}, u32[]{:S(2)}, u32[]{:S(2)}) collective-permute-start(s32[1,1,2,8]{3,2,1,0:T(2,128)S(1)} %copy-done), channel_id=1, source_target_pairs={{0,2},{1,3},{2,0},{3,1},{4,6},{5,7},{6,4},{7,5},{8,10},{9,11},{10,... | collective-permute-start | bytes 200 | tf_op jit(solution)/shard_map/ppermute | solution.py:255
  11.9 0.0 collective-permute-done.2.near_ref
  11.9 2.6 %collective-permute-start.1 = (s32[1,1,2,8]{3,2,1,0:T(2,128)S(1)}, s32[1,1,2,8]{3,2,1,0:T(2,128)S(1)}, u32[]{:S(2)}, u32[]{:S(2)}) collective-permute-start(s32[1,1,2,8]{3,2,1,0:T(2,128)S(1)} %copy-done), channel_id=1, source_target_pairs={{0,4},{1,7},{2,6},{3,5},{4,0},{5,3},{6,2},{7,1},{8,12},{9,15},{10,... | collective-permute-start | bytes 200 | tf_op jit(solution)/shard_map/ppermute | solution.py:255
  14.5 0.0 collective-permute-done.4.far_ref
  14.5 0.2 collective-permute-start.7
  14.8 1.3 %kept.1.kept_ref = f32[2,8,128,128]{3,2,1,0:T(8,128)S(1)} custom-call(bf16[8,1024,128]{2,1,0:T(8,128)(2,1)S(1)} %get-tuple-element.15.dense_ref, bf16[528,128]{1,0:T(8,128)(2,1)S(1)} %collective-permute-done.2.near_ref, bf16[528,128]{1,0:T(8,128)(2,1)S(1)} %collective-permute-done.4.far_ref), custom_call_target="tpu_custom_call" | custom-call | tf_op jit(solution)/shard_map/kept/pallas_call | solution.py:315
  16.1 0.0 collective-permute-done.one_ref
  16.1 0.3 collective-permute-done.1.far_ref
  16.4 0.0 collective-permute-done.5.code_ref
  16.4 0.9 %sum.2 = (s16[528,128]{1,0:T(8,128)(2,1)S(1)}, s16[528,128]{1,0:T(8,128)(2,1)S(1)}) custom-call(s32[1,1,2,8]{3,2,1,0:T(2,128)S(1)} %copy-done, s32[1,1,2,8]{3,2,1,0:T(2,128)S(1)} %collective-permute-done.one_ref, s32[1,1,2,8]{3,2,1,0:T(2,128)S(1)} %collective-permute-done.1.far_ref, f32[2,8,128,128]{3,2,1,0:T(8,128)S(1)} %kept.1.kept_ref, ...), custom_call_target="tpu_custom_call" | custom-call | flops 2000000000 | bytes 20000000 | tf_op jit(solution)/shard_map/sum/pallas_call | solution.py:328
  17.4 2.7 %collective-permute-start.6 = (s16[528,128]{1,0:T(8,128)(2,1)S(1)}, s16[528,128]{1,0:T(8,128)(2,1)S(1)}, u32[]{:S(2)}, u32[]{:S(2)}) collective-permute-start(s16[528,128]{1,0:T(8,128)(2,1)S(1)} %get-tuple-element.18), channel_id=1, source_target_pairs={{0,4},{1,7},{2,6},{3,5},{4,0},{5,3},{6,2},{7,1},{8,12},{9,15},{10,... | collective-permute-start | bytes 405512 | tf_op jit(solution)/shard_map/ppermute | solution.py:255
  20.0 0.0 collective-permute-done.7.far_ref
  20.0 0.3 collective-permute-done.8.code_ref
  20.3 1.0 %sum.3 = (s16[528,128]{1,0:T(8,128)(2,1)S(1)}, s16[528,128]{1,0:T(8,128)(2,1)S(1)}, s16[528,128]{1,0:T(8,128)(2,1)S(1)}) custom-call(s32[1,1,2,8]{3,2,1,0:T(2,128)S(1)} %copy-done, s32[1,1,2,8]{3,2,1,0:T(2,128)S(1)} %collective-permute-done.one_ref, s32[1,1,2,8]{3,2,1,0:T(2,128)S(1)} %collective-permute-done.7.far_ref, f32[2,8,128,128]{3,2,1,0:T(8,128)S(1)} %kept.1.kept_ref, ...), custom_call_target="tpu_custom_call" | custom-call | tf_op jit(solution)/shard_map/sum/pallas_call | solution.py:328
  21.3 1.6 %collective-permute-start.10 = (s16[528,128]{1,0:T(8,128)(2,1)S(1)}, s16[528,128]{1,0:T(8,128)(2,1)S(1)}, u32[]{:S(2)}, u32[]{:S(2)}) collective-permute-start(s16[528,128]{1,0:T(8,128)(2,1)S(1)} %get-tuple-element.21), channel_id=1, source_target_pairs={{0,2},{1,3},{2,0},{3,1},{4,6},{5,7},{6,4},{7,5},{8,10},{9,11},{10,... | collective-permute-start | bytes 405512 | tf_op jit(solution)/shard_map/ppermute | solution.py:255
  22.9 2.5 %collective-permute-start.9 = (s16[528,128]{1,0:T(8,128)(2,1)S(1)}, s16[528,128]{1,0:T(8,128)(2,1)S(1)}, u32[]{:S(2)}, u32[]{:S(2)}) collective-permute-start(s16[528,128]{1,0:T(8,128)(2,1)S(1)} %get-tuple-element.20), channel_id=1, source_target_pairs={{0,6},{1,5},{2,4},{3,7},{4,2},{5,1},{6,0},{7,3},{8,14},{9,13},{10,... | collective-permute-start | bytes 405512 | tf_op jit(solution)/shard_map/ppermute | solution.py:255
  25.4 3.0 %collective-permute-done.6.a_ref = s16[528,128]{1,0:T(8,128)(2,1)S(1)} collective-permute-done((s16[528,128]{1,0:T(8,128)(2,1)S(1)}, s16[528,128]{1,0:T(8,128)(2,1)S(1)}, u32[]{:S(2)}, u32[]{:S(2)}) %collective-permute-start.6) | collective-permute-done | bytes 135200 | tf_op jit(solution)/shard_map/ppermute | solution.py:255
  28.4 0.4 %collective-permute-done.10.c_ref = s16[528,128]{1,0:T(8,128)(2,1)S(1)} collective-permute-done((s16[528,128]{1,0:T(8,128)(2,1)S(1)}, s16[528,128]{1,0:T(8,128)(2,1)S(1)}, u32[]{:S(2)}, u32[]{:S(2)}) %collective-permute-start.10) | collective-permute-done | bytes 135200 | tf_op jit(solution)/shard_map/ppermute | solution.py:255
  28.8 1.7 %collective-permute-done.9.b_ref = s16[528,128]{1,0:T(8,128)(2,1)S(1)} collective-permute-done((s16[528,128]{1,0:T(8,128)(2,1)S(1)}, s16[528,128]{1,0:T(8,128)(2,1)S(1)}, u32[]{:S(2)}, u32[]{:S(2)}) %collective-permute-start.9) | collective-permute-done | bytes 135200 | tf_op jit(solution)/shard_map/ppermute | solution.py:255
  30.5 0.9 %last.1 = f32[1,1,2,8,64,64]{5,4,3,2,1,0:T(8,128)} custom-call(s16[528,128]{1,0:T(8,128)(2,1)S(1)} %collective-permute-done.6.a_ref, s16[528,128]{1,0:T(8,128)(2,1)S(1)} %collective-permute-done.9.b_ref, s16[528,128]{1,0:T(8,128)(2,1)S(1)} %collective-permute-done.10.c_ref, s16[528,128]{1,0:T(8,128)(2,1)S(1)} %get-tuple-element.22.own_ref), custom_call_target="tpu_custom_call" | custom-call | tf_op jit(solution)/shard_map/last/pallas_call | solution.py:343
Async XLA Ops:
  1.1 7.1 %collective-permute-start.3 = (bf16[528,128]{1,0:T(8,128)(2,1)S(1)}, bf16[528,128]{1,0:T(8,128)(2,1)S(1)}, u32[]{:S(2)}, u32[]{:S(2)}) collective-permute-start(bf16[528,128]{1,0:T(8,128)(2,1)S(1)} %pack.1.packed_ref), channel_id=1, source_target_pairs={{0,16},{1,17},{2,18},{3,19},{4,20},{5,21},{6,22},{7,23},{8,24},{9,... | collective-permute-start | bytes 405512 | tf_op jit(solution)/shard_map/ppermute | solution.py:255
  4.1 6.2 %copy-start = (s32[1,1,2,8]{3,2,1,0:T(2,128)S(1)}, s32[1,1,2,8]{3,2,1,0:T(2,128)}, u32[]{:S(2)}) copy-start(s32[1,1,2,8]{3,2,1,0:T(2,128)} %own_ref.3) | copy-start | bytes 196
  6.7 9.8 %collective-permute-start.5 = (s16[1040,128]{1,0:T(8,128)(2,1)S(1)}, s16[1040,128]{1,0:T(8,128)(2,1)S(1)}, u32[]{:S(2)}, u32[]{:S(2)}) collective-permute-start(s16[1040,128]{1,0:T(8,128)(2,1)S(1)} %get-tuple-element.17), channel_id=1, source_target_pairs={{0,1},{1,0},{2,3},{3,2},{4,5},{5,4},{6,7},{7,6},{8,9},{9,8},{10,11... | collective-permute-start | bytes 798728 | tf_op jit(solution)/shard_map/ppermute | solution.py:255
  8.2 3.7 %collective-permute-start.2 = (bf16[528,128]{1,0:T(8,128)(2,1)S(1)}, bf16[528,128]{1,0:T(8,128)(2,1)S(1)}, u32[]{:S(2)}, u32[]{:S(2)}) collective-permute-start(bf16[528,128]{1,0:T(8,128)(2,1)S(1)} %pack.1.packed_ref), channel_id=1, source_target_pairs={{0,8},{1,9},{2,10},{3,11},{4,12},{5,13},{6,14},{7,15},{8,0},{9,1},... | collective-permute-start | bytes 405512 | tf_op jit(solution)/shard_map/ppermute | solution.py:255
  8.2 6.3 %collective-permute-start.4 = (bf16[528,128]{1,0:T(8,128)(2,1)S(1)}, bf16[528,128]{1,0:T(8,128)(2,1)S(1)}, u32[]{:S(2)}, u32[]{:S(2)}) collective-permute-start(bf16[528,128]{1,0:T(8,128)(2,1)S(1)} %collective-permute-done.3.packed_ref), channel_id=1, source_target_pairs={{0,8},{1,9},{2,10},{3,11},{4,12},{5,13},{6,14},{7,15},{8,0},{9,1},... | collective-permute-start | bytes 405512 | tf_op jit(solution)/shard_map/ppermute | solution.py:255
  9.6 10.7 %collective-permute-start.8 = (s16[1040,128]{1,0:T(8,128)(2,1)S(1)}, s16[1040,128]{1,0:T(8,128)(2,1)S(1)}, u32[]{:S(2)}, u32[]{:S(2)}) collective-permute-start(s16[1040,128]{1,0:T(8,128)(2,1)S(1)} %second.1), channel_id=1, source_target_pairs={{0,1},{1,0},{2,3},{3,2},{4,5},{5,4},{6,7},{7,6},{8,9},{9,8},{10,11... | collective-permute-start | bytes 798728 | tf_op jit(solution)/shard_map/ppermute | solution.py:255
  10.4 5.7 %collective-permute-start = (s32[1,1,2,8]{3,2,1,0:T(2,128)S(1)}, s32[1,1,2,8]{3,2,1,0:T(2,128)S(1)}, u32[]{:S(2)}, u32[]{:S(2)}) collective-permute-start(s32[1,1,2,8]{3,2,1,0:T(2,128)S(1)} %copy-done), channel_id=1, source_target_pairs={{0,2},{1,3},{2,0},{3,1},{4,6},{5,7},{6,4},{7,5},{8,10},{9,11},{10,... | collective-permute-start | bytes 200 | tf_op jit(solution)/shard_map/ppermute | solution.py:255
  11.9 4.5 %collective-permute-start.1 = (s32[1,1,2,8]{3,2,1,0:T(2,128)S(1)}, s32[1,1,2,8]{3,2,1,0:T(2,128)S(1)}, u32[]{:S(2)}, u32[]{:S(2)}) collective-permute-start(s32[1,1,2,8]{3,2,1,0:T(2,128)S(1)} %copy-done), channel_id=1, source_target_pairs={{0,4},{1,7},{2,6},{3,5},{4,0},{5,3},{6,2},{7,1},{8,12},{9,15},{10,... | collective-permute-start | bytes 200 | tf_op jit(solution)/shard_map/ppermute | solution.py:255
  14.5 5.5 %collective-permute-start.7 = (s32[1,1,2,8]{3,2,1,0:T(2,128)S(1)}, s32[1,1,2,8]{3,2,1,0:T(2,128)S(1)}, u32[]{:S(2)}, u32[]{:S(2)}) collective-permute-start(s32[1,1,2,8]{3,2,1,0:T(2,128)S(1)} %copy-done), channel_id=1, source_target_pairs={{0,6},{1,5},{2,4},{3,7},{4,2},{5,1},{6,0},{7,3},{8,14},{9,13},{10,... | collective-permute-start | bytes 200 | tf_op jit(solution)/shard_map/ppermute | solution.py:255
  17.4 11.0 %collective-permute-start.6 = (s16[528,128]{1,0:T(8,128)(2,1)S(1)}, s16[528,128]{1,0:T(8,128)(2,1)S(1)}, u32[]{:S(2)}, u32[]{:S(2)}) collective-permute-start(s16[528,128]{1,0:T(8,128)(2,1)S(1)} %get-tuple-element.18), channel_id=1, source_target_pairs={{0,4},{1,7},{2,6},{3,5},{4,0},{5,3},{6,2},{7,1},{8,12},{9,15},{10,... | collective-permute-start | bytes 405512 | tf_op jit(solution)/shard_map/ppermute | solution.py:255
  21.3 7.6 %collective-permute-start.10 = (s16[528,128]{1,0:T(8,128)(2,1)S(1)}, s16[528,128]{1,0:T(8,128)(2,1)S(1)}, u32[]{:S(2)}, u32[]{:S(2)}) collective-permute-start(s16[528,128]{1,0:T(8,128)(2,1)S(1)} %get-tuple-element.21), channel_id=1, source_target_pairs={{0,2},{1,3},{2,0},{3,1},{4,6},{5,7},{6,4},{7,5},{8,10},{9,11},{10,... | collective-permute-start | bytes 405512 | tf_op jit(solution)/shard_map/ppermute | solution.py:255
  22.9 7.6 %collective-permute-start.9 = (s16[528,128]{1,0:T(8,128)(2,1)S(1)}, s16[528,128]{1,0:T(8,128)(2,1)S(1)}, u32[]{:S(2)}, u32[]{:S(2)}) collective-permute-start(s16[528,128]{1,0:T(8,128)(2,1)S(1)} %get-tuple-element.20), channel_id=1, source_target_pairs={{0,6},{1,5},{2,4},{3,7},{4,2},{5,1},{6,0},{7,3},{8,14},{9,13},{10,... | collective-permute-start | bytes 405512 | tf_op jit(solution)/shard_map/ppermute | solution.py:255
